TPU v7x, 32 devices: a whole 2x2x4 slice. The times are simulated.
32 devices in a mesh: group: 4 (over y, x), head: 8 (over z, core).
Axes of the slice: x: 2, y: 2, z: 4, core: 2. Of those that a mesh axis runs over, the one named last changes fastest.
Arguments:
- hidden: bfloat16 [2048, 8192], P(('group', 'head')), may hold values from -6 to 6
- norm_gain: bfloat16 [8192], replicated, may hold values from 0.25 to 1.75
- k_weight: bfloat16 [8192, 8192], P(None, 'head'), may hold values from -0.0625 to 0.0625
- k_bias: bfloat16 [8192], P('head'), may hold values from -3 to 3
- v_weight: bfloat16 [8192, 8192], P(None, 'head'), may hold values from -0.0625 to 0.0625
- v_bias: bfloat16 [8192], P('head'), may hold values from -3 to 3
- positions: int32 [2048], replicated, may hold values from 0 to 5119, as said below
- lengths: int32 [16], replicated, may hold values from 1 to 1021, as said below
- owner: int32 [16], replicated, may hold values from 0 to 3, as said below
Outputs:
- key_cache: bfloat16 [4096, 8192], P('group', 'head')
- value_cache: bfloat16 [4096, 8192], P('group', 'head')
Inputs may be any that keep to these rules, and one draw needn't show every extreme that they name: lengths sum to 2048; the requests of one group hold at most 1024 tokens together, and one group holds exactly 1024. `owner`: every group owns exactly 4 requests. `positions`: positions rise by one from token to token inside a request.
All inputs are finite; a program needn't handle non-finite values.
Results may differ from a plain program's by a relative error of at most 0.0056.
Values may be sent and summed in bfloat16 or wider, within the bound.
No kernel may reach another device: no remote copies, remote signals or barrier semaphores. Data moves between devices by JAX's collectives and lax.ppermute only.
A program may use at most 128 MiB of HBM per device.

v0:
```python
import jax
import jax.numpy as jnp
from jax import lax
from jax.sharding import PartitionSpec as P

HD = 128


def rotate(raw, pos):
    count = raw.shape[0]
    half = HD // 2
    x = raw.astype(jnp.float32).reshape(count, -1, HD)
    freq = jnp.exp(
        jnp.arange(half, dtype=jnp.float32) * (-2.0 / HD * jnp.log(jnp.float32(1000000.0)))
    )
    angle = pos.astype(jnp.float32)[:, None] * freq[None, :]
    cosine = jnp.cos(angle)[:, None, :]
    sine = jnp.sin(angle)[:, None, :]
    first = x[:, :, :half]
    second = x[:, :, half:]
    out = jnp.concatenate([first * cosine - second * sine, second * cosine + first * sine], axis=2)
    return out.reshape(count, -1).astype(jnp.bfloat16)


def cache_map(lengths, owner, group, cap):
    inside = owner == group
    own_len = jnp.where(inside, lengths, 0)
    start = jnp.cumsum(lengths) - lengths
    local = jnp.cumsum(own_len) - own_len
    row = jnp.arange(cap, dtype=jnp.int32)[:, None]
    match = inside[None, :] & (row >= local[None, :]) & (row < (local + lengths)[None, :])
    source = jnp.sum(jnp.where(match, start[None, :] + row - local[None, :], 0), axis=1)
    return (source, jnp.any(match, axis=1))


def per_device(hidden, norm_gain, k_weight, k_bias, v_weight, v_bias, positions, lengths, owner):
    rows = hidden.astype(jnp.float32)
    scale = lax.rsqrt(jnp.mean(rows * rows, axis=1, keepdims=True) + 1e-06)
    normed = (rows * scale * norm_gain.astype(jnp.float32)).astype(jnp.bfloat16)
    group_index = lax.axis_index("group")
    head_count = lax.axis_size("head")
    rows_dev = hidden.shape[0]
    width = k_weight.shape[1]
    cap = rows_dev * lax.axis_size("group") * head_count // 2
    piece = lax.all_gather(normed, "head", axis=0, tiled=True)
    key_raw = (
        jnp.dot(piece, k_weight, preferred_element_type=jnp.float32) + k_bias.astype(jnp.float32)
    ).astype(jnp.bfloat16)
    values = (
        jnp.dot(piece, v_weight, preferred_element_type=jnp.float32) + v_bias.astype(jnp.float32)
    ).astype(jnp.bfloat16)
    projected = jnp.concatenate([key_raw, values], axis=1)
    source, valid = cache_map(lengths, owner, group_index, cap)
    zero = jnp.zeros((), jnp.bfloat16)
    everything = lax.all_gather(projected, "group", axis=0, tiled=True)
    cache = jnp.where(valid[:, None], jnp.take(everything, source, axis=0), zero)
    key_cache = cache[:, :width]
    value_cache = cache[:, width:]
    row_pos = jnp.take(positions, source, axis=0)
    key_cache = jnp.where(valid[:, None], rotate(key_cache, row_pos), zero)
    return (key_cache, value_cache)


def solution(mesh):
    in_specs = (
        P(("group", "head"), None),
        P(),
        P(None, "head"),
        P("head"),
        P(None, "head"),
        P("head"),
        P(),
        P(),
        P(),
    )
    out_specs = (P("group", "head"), P("group", "head"))
    return jax.shard_map(
        per_device, mesh=mesh, in_specs=in_specs, out_specs=out_specs, check_vma=False
    )
```

profile of v0, /device:TPU:0, one launch (start us, length us, event | category | flops | bytes accessed | tf_op | source)
XLA Modules:
  0.0 245.4 jit_solution(154960862298972979)
XLA Ops:
  7.2 0.0 copy-start
  7.2 0.0 copy-start.2
  7.2 0.0 copy-start.3
  7.2 0.0 all-gather.3.cloned.1.call-start
  7.2 0.7 convert_element_type.34
  8.0 1.5 fusion
  9.5 2.5 %fusion.2 = bf16[64,8192]{1,0:T(8,128)(2,1)} fusion(bf16[64,8192]{1,0:T(8,128)(2,1)} %param.9, f32[8192]{0:T(1024)S(1)} %convert_element_type.34, f32[64]{0:T(128)S(1)} %add_rsqrt_fusion), kind=kLoop, calls=%fused_computation.10 | loop fusion | flops 2097152 | bytes 2130176 | tf_op jit(solution)/shard_map/convert_element_type | solution.py:39
  12.0 0.0 all-gather.3.cloned.1.call-update
  12.0 0.0 all-gather.5.cloned.1.call-start
  12.1 0.0 copy-done.2
  12.1 0.0 copy-done.3
  12.1 84.8 %all-gather.3.cloned.1.call-done = bf16[512,8192]{1,0:T(8,128)(2,1)} async-done(((bf16[64,8192]{1,0:T(8,128)(2,1)}), bf16[512,8192]{1,0:T(8,128)(2,1)}) %all-gather.3.cloned.1.call-update) | async-done | bytes 8388624 | tf_op jit(solution)/shard_map/all_gather | solution.py:45
  97.0 0.0 copy-start.5
  97.0 17.2 %add_convert_fusion.1 = bf16[512,1024]{1,0:T(8,128)(2,1)S(1)} fusion(bf16[512,8192]{1,0:T(8,128)(2,1)} %all-gather.3.cloned.1.call-done, bf16[8192,1024]{1,0:T(8,128)(2,1)} %param.13, f32[1024]{0:T(1024)S(1)} %convert_element_type.38), kind=kOutput, calls=%fused_computation.14 | convolution fusion | flops 8590983168 | bytes 26218496 | tf_op jit(solution)/shard_map/dot_general | solution.py:50
  114.2 0.0 copy-done.5
  114.2 12.6 %add_convert_fusion.2 = bf16[512,1024]{1,0:T(8,128)(2,1)S(1)} fusion(bf16[512,8192]{1,0:T(8,128)(2,1)S(1)} %copy-done.5, bf16[8192,1024]{1,0:T(8,128)(2,1)} %param.11, f32[1024]{0:T(1024)S(1)} %convert_element_type.36), kind=kOutput, calls=%fused_computation.15 | convolution fusion | flops 8590983168 | bytes 26218496 | tf_op jit(solution)/shard_map/dot_general | solution.py:47
  126.7 0.0 copy-start.1
  126.7 0.0 copy-start.4
  126.7 1.5 pad_maximum_fusion
  128.3 0.0 all-gather.5.cloned.1.call-update
  128.3 0.0 copy-done.1
  128.3 0.0 copy-done.4
  128.3 0.1 copy.15
  128.4 0.1 reduce
  128.6 0.1 copy.16
  128.7 0.1 reduce.1
  128.8 0.1 select_reduce_fusion
  128.9 0.0 copy-done
  129.0 6.2 %gather_fusion.1 = s32[1024]{0:T(1024)S(1)} fusion(s32[2048]{0:T(1024)S(1)} %copy-done, s32[1024]{0:T(1024)S(1)} %broadcast_clamp_fusion), kind=kCustom, calls=%fused_computation.1 | custom fusion | bytes 12288 | tf_op jit(solution)/shard_map/jit(_take)/gather | solution.py:59
  135.1 0.1 fusion.5
  135.2 1.9 multiply_cosine_fusion
  137.1 77.4 %all-gather.5.cloned.1.call-done = bf16[2048,2048]{1,0:T(8,128)(2,1)} async-done(((bf16[512,2048]{1,0:T(8,128)(2,1)}), bf16[2048,2048]{1,0:T(8,128)(2,1)}) %all-gather.5.cloned.1.call-update) | async-done | bytes 8388624 | tf_op jit(solution)/shard_map/all_gather | solution.py:55
  214.6 13.3 %gather_fusion = bf16[1024,2048]{1,0:T(8,128)(2,1)} fusion(bf16[2048,2048]{1,0:T(8,128)(2,1)} %all-gather.5.cloned.1.call-done, s32[1024]{0:T(1024)S(1)} %broadcast_clamp_fusion), kind=kCustom, calls=%fused_computation | custom fusion | bytes 8392704 | tf_op jit(solution)/shard_map/jit(_take)/gather | solution.py:56
  227.9 2.9 %select_select_fusion = bf16[1024,2048]{1,0:T(8,128)(2,1)S(1)} fusion(bf16[1024,2048]{1,0:T(8,128)(2,1)} %gather_fusion, pred[1024]{0:T(1024)(128)(4,1)S(1)} %get-tuple-element.3, pred[1024]{0:T(1024)(128)(4,1)S(1)} %fusion.5), kind=kLoop, calls=%fused_computation.5 | loop fusion | flops 4194304 | bytes 8390656 | tf_op jit(solution)/shard_map/jit(_where)/select_n | solution.py:56
  230.8 2.0 fusion.10
  232.8 1.0 copy.17
  233.9 1.8 subtract_convert_fusion
  235.7 1.2 pad_maximum_fusion.1
  236.9 1.7 bitcast_select_fusion
  (11 shorter events, 0.1 us)
Async XLA Ops:
  7.2 121.8 %copy-start = (s32[2048]{0:T(1024)S(1)}, s32[2048]{0:T(1024)}, u32[]{:S(2)}) copy-start(s32[2048]{0:T(1024)} %param.15) | copy-start | bytes 24580
  7.2 4.9 %copy-start.2 = (bf16[1024]{0:T(1024)(128)(2,1)S(1)}, bf16[1024]{0:T(1024)(128)(2,1)}, u32[]{:S(2)}) copy-start(bf16[1024]{0:T(1024)(128)(2,1)} %param.14) | copy-start | bytes 6148
  7.2 4.9 %copy-start.3 = (bf16[1024]{0:T(1024)(128)(2,1)S(1)}, bf16[1024]{0:T(1024)(128)(2,1)}, u32[]{:S(2)}) copy-start(bf16[1024]{0:T(1024)(128)(2,1)} %param.12) | copy-start | bytes 6148
  7.2 89.8 %all-gather.3.cloned.1.call-start = ((), (), s32[]{:S(2)}) async-start(), calls=%async_computation | async-start | bytes 9437184 | tf_op jit(solution)/shard_map/all_gather | solution.py:45
  12.0 202.5 %all-gather.5.cloned.1.call-start = ((), (), s32[]{:S(2)}) async-start(), calls=%async_computation.1 | async-start | bytes 10485760 | tf_op jit(solution)/shard_map/all_gather | solution.py:55
  97.0 17.2 %copy-start.5 = (bf16[512,8192]{1,0:T(8,128)(2,1)S(1)}, bf16[512,8192]{1,0:T(8,128)(2,1)}, u32[]{:S(2)}) copy-start(bf16[512,8192]{1,0:T(8,128)(2,1)} %all-gather.3.cloned.1.call-done) | copy-start | bytes 25165828
  126.7 1.6 copy-start.1
  126.7 1.6 copy-start.4
Sparse Core Ops, SparseCore 0:
  12.2 84.7 all-gather.2
  128.4 86.1 all-gather.4
where the time goes:
time: 246 us; the launch traced here: 245 us
  waiting for transfers between devices  162 us (66%)
  matrix products  29.7 us (12%)
  local copies, waits for them, and re-layouts  20.7 us (8%)
  other arithmetic  18.3 us (7%)
  between operations  14.3 us (6%)
    all_gather x1, waiting for transfers between devices, per_device(): piece = lax.all_gather(normed, 'head', axis=0, tiled=True)  84.8 us
    all_gather x1, waiting for transfers between devices, per_device(): everything = lax.all_gather(projected, 'group', axis=0, tiled=True)  77.4 us
    dot_general x1, matrix products, per_device(): jnp.dot(piece, v_weight, preferred_element_type=jnp.float32)  17.2 us
    gather x1, local copies, waits for them, and re-layouts, per_device(): jnp.take(everything, source, axis=0)  13.3 us
    dot_general x1, matrix products, per_device(): jnp.dot(piece, k_weight, preferred_element_type=jnp.float32)  12.6 us
    gather x1, local copies, waits for them, and re-layouts, per_device(): row_pos = jnp.take(positions, source, axis=0)  6.15 us
  transfers between devices with their start and end apart: 2, of which 2 were waited for; matrix products, arithmetic and copies ran while one was open for 4% of the time, Pallas kernels for 0%

commit v1 on v0

--- a/solution.py
+++ b/solution.py
@@ -1,9 +1,18 @@
+import functools
+
 import jax
 import jax.numpy as jnp
 from jax import lax
+from jax.experimental import pallas as pl
+from jax.experimental.pallas import tpu as pltpu
 from jax.sharding import PartitionSpec as P
 
 HD = 128
+BF = jnp.bfloat16
+F32 = jnp.float32
+MIB = 1 << 20
+VMEM = pltpu.VMEM
+ANY = pl.ANY
 
 
 def rotate(raw, pos):
@@ -33,7 +42,7 @@
     return (source, jnp.any(match, axis=1))
 
 
-def per_device(hidden, norm_gain, k_weight, k_bias, v_weight, v_bias, positions, lengths, owner):
+def gathered(hidden, norm_gain, k_weight, k_bias, v_weight, v_bias, positions, lengths, owner):
     rows = hidden.astype(jnp.float32)
     scale = lax.rsqrt(jnp.mean(rows * rows, axis=1, keepdims=True) + 1e-06)
     normed = (rows * scale * norm_gain.astype(jnp.float32)).astype(jnp.bfloat16)
@@ -61,6 +70,296 @@
     return (key_cache, value_cache)
 
 
+def norm_kernel(x_ref, gain_ref, lo_ref, hi_ref):
+    half = lo_ref.shape[0]
+    step = 16
+    for at in range(0, x_ref.shape[0], step):
+        x = x_ref[at : at + step, :].astype(F32)
+        scale = lax.rsqrt(jnp.mean(x * x, axis=1, keepdims=True) + 1e-06)
+        y = (x * scale * gain_ref[...].astype(F32)).astype(BF)
+        if at < half:
+            lo_ref[at : at + step, :] = y
+        else:
+            hi_ref[at - half : at - half + step, :] = y
+
+
+def normalise(hidden, gain):
+    rows, wide = hidden.shape
+    half = jax.ShapeDtypeStruct((rows // 2, wide), BF)
+    return pl.pallas_call(
+        norm_kernel,
+        out_shape=(half, half),
+        name="norm",
+        cost_estimate=pl.CostEstimate(flops=5 * rows * wide, bytes_accessed=4 * rows * wide, transcendentals=rows),
+        compiler_params=pltpu.CompilerParams(vmem_limit_bytes=16 * MIB),
+    )(hidden, gain.reshape(1, wide))
+
+
+def project(parts, m, x_ref, wk, wv, kb, vb, cos, sin, outs, before):
+    width = wk.shape[1]
+    tile = 256
+    split = outs[0].shape[0]
+
+    def put(at, y):
+        outs[0][:, pl.ds(at, tile)] = y[:split]
+        outs[1][:, pl.ds(at, tile)] = y[split:]
+
+    def keys(i, carry):
+        at = pl.multiple_of(i * tile, tile)
+        raw = jnp.dot(x_ref[...], wk[:, pl.ds(at, tile)], preferred_element_type=F32)
+        raw = (raw + kb[:, pl.ds(at, tile)].astype(F32)).astype(BF).astype(F32)
+        c = jnp.concatenate([cos[pl.ds(pl.multiple_of(o, 8), n), :] for o, n in parts], axis=0)
+        s = jnp.concatenate([sin[pl.ds(pl.multiple_of(o, 8), n), :] for o, n in parts], axis=0)
+        heads = []
+        for h in range(tile // HD):
+            one = raw[:, h * HD : (h + 1) * HD]
+            heads.append(one * c + pltpu.roll(one, HD // 2, axis=1) * s)
+        put(at, jnp.concatenate(heads, axis=1).astype(BF))
+        return carry
+
+    def values(i, carry):
+        at = pl.multiple_of(i * tile, tile)
+        raw = jnp.dot(x_ref[...], wv[:, pl.ds(at, tile)], preferred_element_type=F32)
+        put(pl.multiple_of(width + i * tile, tile), (raw + vb[:, pl.ds(at, tile)].astype(F32)).astype(BF))
+        return carry
+
+    if before is None:
+        lax.fori_loop(0, width // tile, keys, 0)
+        lax.fori_loop(0, width // tile, values, 0)
+    else:
+        for i in range(width // tile):
+            before(0, i)
+            keys(i, 0)
+        for i in range(width // tile):
+            before(1, i)
+            values(i, 0)
+
+
+def part_offsets(layout):
+    head = lax.axis_index("head")
+    chip, core = head // 2, head % 2
+    out = []
+    for w, j, u, n in layout:
+        out.append(((chip ^ w) * 128 + (core ^ j) * 64 + u * 32, n))
+    return out
+
+
+def first_kernel(layout, lo, hi, slo, shi, wk, wv, kb, vb, cos, sin, p0, p1, wko, wvo, x, xsem, wsem):
+    width = wk.shape[1]
+    tile = 256
+    half = lo.shape[0]
+    loads = []
+    for i, src in enumerate((lo, hi, slo, shi)):
+        loads.append(pltpu.make_async_copy(src, x.at[pl.ds(i * half, half)], xsem.at[i]))
+        loads[-1].start()
+    copies = []
+    for a, (src, dst) in enumerate(((wk, wko), (wv, wvo))):
+        for i in range(width // tile):
+            cols = pl.ds(i * tile, tile)
+            copies.append(pltpu.make_async_copy(src.at[:, cols], dst.at[:, cols], wsem.at[a * (width // tile) + i]))
+            copies[-1].start()
+    for one in loads:
+        one.wait()
+
+    def before(a, i):
+        copies[a * (width // tile) + i].wait()
+
+    project(part_offsets(layout), x.shape[0], x, wko, wvo, kb, vb, cos, sin, (p0, p1), before)
+
+
+def wave_kernel(layout, ends, *refs):
+    count = len(layout)
+    sources = refs[: count * (2 if ends else 1)]
+    wk, wv, kb, vb, cos, sin, p0, p1, x, sem = refs[len(sources) :]
+    row = 0
+    copies = []
+    chip = lax.axis_index("head") // 2
+    at_end = (chip == 0) | (chip == 3)
+    for i, (w, j, u, n) in enumerate(layout):
+        dst = x.at[pl.ds(row, n)]
+        if ends:
+            pl.when(jnp.logical_not(at_end))(pltpu.make_async_copy(sources[i], dst, sem.at[i]).start)
+            pl.when(at_end)(pltpu.make_async_copy(sources[count + i], dst, sem.at[i]).start)
+        else:
+            pltpu.make_async_copy(sources[i], dst, sem.at[i]).start()
+        copies.append(pltpu.make_async_copy(sources[i], dst, sem.at[i]))
+        row += n
+    for one in copies:
+        one.wait()
+    project(part_offsets(layout), x.shape[0], x, wk, wv, kb, vb, cos, sin, (p0, p1), None)
+
+
+def cost(m, deep, width, weights):
+    return pl.CostEstimate(
+        flops=2 * m * deep * width * 2,
+        bytes_accessed=2 * (m * deep + m * width * 2 + (deep * width * 2 if weights else 0)),
+        transcendentals=0,
+    )
+
+
+def first_wave(layout, own, sibling, wk, wv, rest):
+    deep, width = wk.shape
+    m = sum(n for _, _, _, n in layout)
+    half = jax.ShapeDtypeStruct((m // 2, 2 * width), BF)
+    kept = VMEM((deep, width), BF)
+    full = pl.BlockSpec(memory_space=VMEM)
+    hbm = pl.BlockSpec(memory_space=ANY)
+    return pl.pallas_call(
+        functools.partial(first_kernel, layout),
+        out_shape=(half, half, kept, kept),
+        in_specs=[hbm] * 6 + [full] * 4,
+        out_specs=(full,) * 4,
+        scratch_shapes=[VMEM((m, deep), BF), pltpu.SemaphoreType.DMA((4,)), pltpu.SemaphoreType.DMA((2 * width // 256,))],
+        name="wave0",
+        cost_estimate=cost(m, deep, width, True),
+        compiler_params=pltpu.CompilerParams(vmem_limit_bytes=16 * MIB),
+    )(*own, *sibling, wk, wv, *rest)
+
+
+def wave(name, layout, sources, ends, wk, wv, rest):
+    deep, width = wk.shape
+    m = sum(n for _, _, _, n in layout)
+    half = jax.ShapeDtypeStruct((m // 2, 2 * width), BF)
+    full = pl.BlockSpec(memory_space=VMEM)
+    hbm = pl.BlockSpec(memory_space=ANY)
+    return pl.pallas_call(
+        functools.partial(wave_kernel, layout, ends),
+        out_shape=(half, half),
+        in_specs=[hbm] * len(sources) + [full] * 6,
+        out_specs=(full, full),
+        scratch_shapes=[VMEM((m, deep), BF), pltpu.SemaphoreType.DMA((len(layout),))],
+        name=name,
+        cost_estimate=cost(m, deep, width, False),
+        compiler_params=pltpu.CompilerParams(vmem_limit_bytes=16 * MIB),
+    )(*sources, wk, wv, *rest)
+
+
+def place_kernel(units, lengths, owner, *refs):
+    arrays = max(unit[4] for unit in units) + 1
+    sources = refs[:arrays]
+    key_out, value_out, rows, sem = refs[arrays:]
+    width = key_out.shape[1]
+    group = lax.axis_index("group")
+    head = lax.axis_index("head")
+    copies = []
+    for i, (d, w, j, u, a, row, n) in enumerate(units):
+        at = (group ^ d) * 512 + ((head // 2) ^ w) * 128 + ((head % 2) ^ j) * 64 + u * 32
+        copy = pltpu.make_async_copy(
+            sources[a].at[pl.ds(row, n)], rows.at[pl.ds(pl.multiple_of(at, 32), n)], sem.at[i]
+        )
+        copy.start()
+        copies.append(copy)
+    key_out[...] = jnp.zeros_like(key_out)
+    value_out[...] = jnp.zeros_like(value_out)
+    for copy in copies:
+        copy.wait()
+    tile, window = 128, 256
+    total = rows.shape[0]
+
+    def request(q, carry):
+        start, local = carry
+        length = lengths[q]
+        mine = owner[q] == group
+
+        @pl.when(mine)
+        def _():
+            def step(t, c):
+                top = pl.multiple_of(t * tile, tile)
+                base = start + top - local
+                at = pl.multiple_of(jnp.clip((base >> 4) << 4, 0, total - window), 16)
+                src = at + lax.broadcasted_iota(jnp.int32, (tile, window), 1)
+                dst = base + lax.broadcasted_iota(jnp.int32, (tile, window), 0)
+                hit = (src == dst) & (src >= start) & (src < start + length)
+                pick = jnp.where(hit, 1.0, 0.0).astype(BF)
+                for part, out in ((0, key_out), (1, value_out)):
+                    moved = jnp.dot(pick, rows[pl.ds(at, window), part * width : (part + 1) * width], preferred_element_type=F32)
+                    out[pl.ds(top, tile), :] += moved.astype(BF)
+                return c
+
+            lax.fori_loop(local // tile, (local + length - 1) // tile + 1, step, 0)
+
+        return (start + length, local + jnp.where(mine, length, 0))
+
+    lax.fori_loop(0, lengths.shape[0], request, (jnp.int32(0), jnp.int32(0)))
+
+
+def place(units, arrays, lengths, owner, cap, width, total):
+    out = jax.ShapeDtypeStruct((cap, width), BF)
+    smem = pl.BlockSpec(memory_space=pltpu.SMEM)
+    hbm = pl.BlockSpec(memory_space=ANY)
+    full = pl.BlockSpec(memory_space=VMEM)
+    return pl.pallas_call(
+        functools.partial(place_kernel, units),
+        out_shape=(out, out),
+        in_specs=[smem, smem] + [hbm] * len(arrays),
+        out_specs=(full, full),
+        scratch_shapes=[VMEM((total, 2 * width), BF), pltpu.SemaphoreType.DMA((len(units),))],
+        name="place",
+        cost_estimate=pl.CostEstimate(flops=0, bytes_accessed=20 * MIB, transcendentals=0),
+        compiler_params=pltpu.CompilerParams(vmem_limit_bytes=28 * MIB),
+    )(lengths, owner, *arrays)
+
+
+def pipelined(hidden, norm_gain, k_weight, k_bias, v_weight, v_bias, positions, lengths, owner):
+    width = k_weight.shape[1]
+    group = lax.axis_index("group")
+
+    def line(x, pairs):
+        return lax.ppermute(x, "head", [(2 * a + c, 2 * b + c) for a, b in pairs for c in range(2)])
+
+    def sibling(x):
+        return lax.ppermute(x, "head", [(i, i ^ 1) for i in range(8)])
+
+    def across(x, bit):
+        return lax.ppermute(x, "group", [(i, i ^ bit) for i in range(4)])
+
+    own = normalise(hidden, norm_gain)
+    far = [line(x, [(0, 2), (1, 3), (2, 0), (3, 1)]) for x in own]
+    near = [line(x, [(0, 1), (1, 0), (2, 3), (3, 2)]) for x in own]
+    middle = [line(x, [(1, 2), (2, 1), (0, 0), (3, 3)]) for x in own]
+    relay = [line(x, [(1, 0), (2, 3), (0, 1), (3, 2)]) for x in far]
+    own_s, far_s, near_s, middle_s, relay_s = (
+        [sibling(x) for x in xs] for xs in (own, far, near, middle, relay)
+    )
+
+    half = HD // 2
+    freq = jnp.exp(jnp.arange(half, dtype=F32) * (-2.0 / HD * jnp.log(F32(1000000.0))))
+    pos = lax.dynamic_slice(positions, (group * 512,), (512,)).astype(F32)
+    angle = pos[:, None] * freq[None, :]
+    cosine, sine = jnp.cos(angle), jnp.sin(angle)
+    cos = jnp.concatenate([cosine, cosine], axis=1)
+    sin = jnp.concatenate([-sine, sine], axis=1)
+    rest = (k_bias.reshape(1, width), v_bias.reshape(1, width), cos, sin)
+
+    units, arrays = [], []
+
+    def spread(layouts, parts):
+        got = [parts, [across(p, 1) for p in parts], [across(p, 2) for p in parts]]
+        got.append([across(got[1][0], 2), across(got[2][1], 1)])
+        for d, pair in enumerate(got):
+            for layout, array in zip(layouts, pair):
+                row = 0
+                for w, j, u, n in layout:
+                    units.append((d, w, j, u, len(arrays), row, n))
+                    row += n
+                arrays.append(array)
+
+    layout = [(0, 0, 0, 32), (0, 0, 1, 32), (0, 1, 0, 32), (0, 1, 1, 32)]
+    p0, p1, wk, wv = first_wave(layout, own, own_s, k_weight, v_weight, rest)
+    spread([layout[:2], layout[2:]], [p0, p1])
+    for u in range(2):
+        layout = [(2, 0, u, 32), (2, 1, u, 32), (1, 0, u, 32), (1, 1, u, 32)]
+        sources = [far[u], far_s[u], near[u], near_s[u]]
+        parts = wave("wave%d" % (1 + u), layout, sources, False, wk, wv, rest)
+        spread([layout[:2], layout[2:]], parts)
+    for u in range(2):
+        layout = [(3, 0, u, 32), (3, 1, u, 32)]
+        sources = [middle[u], middle_s[u], relay[u], relay_s[u]]
+        parts = wave("wave%d" % (3 + u), layout, sources, True, wk, wv, rest)
+        spread([layout[:1], layout[1:]], parts)
+    return place(units, arrays, lengths, owner, 1024, width, 2048)
+
+
 def solution(mesh):
     in_specs = (
         P(("group", "head"), None),
@@ -74,6 +373,7 @@
         P(),
     )
     out_specs = (P("group", "head"), P("group", "head"))
+    square = mesh.shape["group"] == 4 and mesh.shape["head"] == 8
     return jax.shard_map(
-        per_device, mesh=mesh, in_specs=in_specs, out_specs=out_specs, check_vma=False
-    )
+        pipelined if square else gathered, mesh=mesh, in_specs=in_specs, out_specs=out_specs, check_vma=False
+    )

time: 246 us -> 205 us (0.83)
  waiting for transfers between devices: 162 us -> 60.1 us
  Pallas kernels: 0 us -> 70.3 us
  starting transfers between devices: 0.08 us -> 44.6 us
  matrix products: 29.7 us -> 0 us
  other arithmetic: 18.3 us -> 1.97 us
  between operations: 14.3 us -> 1.01 us
  local copies, waits for them, and re-layouts: 20.7 us -> 26.4 us
    all_gather x2 -> x0, waiting for transfers between devices: 162 us -> none  [the longest x1 84.8 us: per_device(): piece = lax.all_gather(normed, 'head', axis=0, tiled=True)]
    pallas_call x0 -> x7, Pallas kernels: none -> 70.3 us  [the longest x4 29.8 us: wave(): pl.pallas_call(functools.partial(wave_kernel, layout, ends), out_shape=(h...]
    ppermute x0 -> x48, waiting for transfers between devices: none -> 60.1 us  [the longest x30 35.7 us: across(): return lax.ppermute(x, 'group', [(i, i ^ bit) for i in range(4)])]
    ppermute x0 -> x48, starting transfers between devices: none -> 44.6 us  [the longest x30 27.5 us: across(): return lax.ppermute(x, 'group', [(i, i ^ bit) for i in range(4)])]
    dot_general x2 -> x0, matrix products: 29.7 us -> none  [the longest x1 17.2 us: per_device(): jnp.dot(piece, v_weight, preferred_element_type=jnp.float32)]
    unnamed x13 -> x14, local copies, waits for them, and re-layouts: 1.04 us -> 24.3 us
    gather x2 -> x0, local copies, waits for them, and re-layouts: 19.4 us -> none  [the longest x1 13.3 us: per_device(): jnp.take(everything, source, axis=0)]
    select_n x3 -> x0, other arithmetic: 4.59 us -> none  [the longest x1 2.92 us: per_device(): jnp.where(valid[:, None], jnp.take(everything, source, axis=0), zero)]
  transfers between devices with their start and end apart: 2 -> 48, of which waited for: 2 -> 19; matrix products, arithmetic and copies ran while one was open for 4% -> 2% of each run, Pallas kernels for 0% -> 24%
where the time goes in v1:
time: 205 us; the launch traced here: 204 us
  Pallas kernels  70.3 us (34%)
  waiting for transfers between devices  60.1 us (29%)
  starting transfers between devices  44.6 us (22%)
  local copies, waits for them, and re-layouts  26.4 us (13%)
    ppermute x30, waiting for transfers between devices, across(): return lax.ppermute(x, 'group', [(i, i ^ bit) for i in range(4)])  35.7 us
    pallas_call x4, Pallas kernels, wave(): pl.pallas_call(functools.partial(wave_kernel, layout, ends), out_shape=(h...  29.8 us
    ppermute x30, starting transfers between devices, across(): return lax.ppermute(x, 'group', [(i, i ^ bit) for i in range(4)])  27.5 us
    unnamed x14, local copies, waits for them, and re-layouts  24.3 us
    ppermute x8, waiting for transfers between devices, line(): lax.ppermute(x, 'head', [(2 * a + c, 2 * b + c) for a, b in pairs for c i...  24.3 us
    pallas_call x1, Pallas kernels, first_wave(): pl.pallas_call(functools.partial(first_kernel, layout), out_shape=(half,...  20 us
    pallas_call x1, Pallas kernels, place(): pl.pallas_call(functools.partial(place_kernel, units), out_shape=(out, ou...  19.9 us
    ppermute x8, starting transfers between devices, line(): lax.ppermute(x, 'head', [(2 * a + c, 2 * b + c) for a, b in pairs for c i...  14.9 us
  transfers between devices with their start and end apart: 48, of which 19 were waited for; matrix products, arithmetic and copies ran while one was open for 2% of the time, Pallas kernels for 24%

profile of v1, /device:TPU:0, one launch (start us, length us, event | category | flops | bytes accessed | tf_op | source)
XLA Modules:
  0.0 204.3 jit_solution(4392600617753891858)
XLA Ops:
  0.6 0.7 reshape.19.gain_ref
  1.4 1.2 copy-done.4
  2.6 0.7 norm.1
  3.3 0.5 collective-permute-start
  3.9 4.0 %collective-permute-start.18 = (bf16[32,8192]{1,0:T(8,128)(2,1)S(1)}, bf16[32,8192]{1,0:T(8,128)(2,1)S(1)}, u32[]{:S(2)}, u32[]{:S(2)}) collective-permute-start(bf16[32,8192]{1,0:T(8,128)(2,1)S(1)} %get-tuple-element.17.hi), channel_id=1, source_target_pairs={{0,4},{1,5},{2,6},{3,7},{4,0},{5,1},{6,2},{7,3},{8,12},{9,13},{10,... | collective-permute-start | bytes 1572872 | tf_op jit(solution)/shard_map/ppermute | solution.py:308
  7.9 0.7 collective-permute-start.38
  8.6 4.3 %collective-permute-start.8 = (bf16[32,8192]{1,0:T(8,128)(2,1)S(1)}, bf16[32,8192]{1,0:T(8,128)(2,1)S(1)}, u32[]{:S(2)}, u32[]{:S(2)}) collective-permute-start(bf16[32,8192]{1,0:T(8,128)(2,1)S(1)} %get-tuple-element.16.lo), channel_id=1, source_target_pairs={{0,4},{1,5},{2,6},{3,7},{4,0},{5,1},{6,2},{7,3},{8,12},{9,13},{10,... | collective-permute-start | bytes 1572872 | tf_op jit(solution)/shard_map/ppermute | solution.py:308
  12.9 0.7 reshape.20.kb.refs_6_
  13.6 0.7 reshape.21.vb.refs_7_
  14.3 0.8 dynamic-slice_convert_fusion
  15.0 1.0 fusion
  16.1 0.9 collective-permute-start.28
  16.9 1.9 collective-permute-start.20
  18.8 24.3 %collective-permute-done.18.refs_0_ = bf16[32,8192]{1,0:T(8,128)(2,1)S(1)} collective-permute-done((bf16[32,8192]{1,0:T(8,128)(2,1)S(1)}, bf16[32,8192]{1,0:T(8,128)(2,1)S(1)}, u32[]{:S(2)}, u32[]{:S(2)}) %collective-permute-start.18) | collective-permute-done | bytes 524320 | tf_op jit(solution)/shard_map/ppermute | solution.py:308
  43.5 20.0 %wave0.1 = (bf16[64,2048]{1,0:T(8,128)(2,1)S(1)}, bf16[64,2048]{1,0:T(8,128)(2,1)S(1)}, bf16[8192,1024]{1,0:T(8,128)(2,1)S(1)}, bf16[8192,1024]{1,0:T(8,128)(2,1)S(1)}) custom-call(bf16[32,8192]{1,0:T(8,128)(2,1)S(1)} %get-tuple-element.16.lo, bf16[32,8192]{1,0:T(8,128)(2,1)S(1)} %get-tuple-element.17.hi, bf16[32,8192]{1,0:T(8,128)(2,1)S(1)} %collective-permute-done.slo, ...), custom_call_target="tpu_custom_call" | custom-call | flops 4294967296 | bytes 36175872 | tf_op jit(solution)/shard_map/wave0/pallas_call | solution.py:207
  63.5 5.8 %copy-done = bf16[8192,1024]{1,0:T(8,128)(2,1)} copy-done((bf16[8192,1024]{1,0:T(8,128)(2,1)}, bf16[8192,1024]{1,0:T(8,128)(2,1)S(1)}, u32[]{:S(2)}) %copy-start) | copy-done | bytes 16777240
  69.3 5.8 %copy-done.2 = bf16[8192,1024]{1,0:T(8,128)(2,1)} copy-done((bf16[8192,1024]{1,0:T(8,128)(2,1)}, bf16[8192,1024]{1,0:T(8,128)(2,1)S(1)}, u32[]{:S(2)}) %copy-start.2) | copy-done | bytes 16777240
  75.1 1.6 collective-permute-start.2
  76.7 1.5 collective-permute-start.5
  78.3 2.0 collective-permute-start.40
  80.8 2.2 %collective-permute-done.2.refs_2_ = bf16[64,2048]{1,0:T(8,128)(2,1)S(1)} collective-permute-done((bf16[64,2048]{1,0:T(8,128)(2,1)S(1)}, bf16[64,2048]{1,0:T(8,128)(2,1)S(1)}, u32[]{:S(2)}, u32[]{:S(2)}) %collective-permute-start.2) | collective-permute-done | bytes 262176 | tf_op jit(solution)/shard_map/ppermute | solution.py:314
  83.0 1.5 collective-permute-start.3
  84.5 1.5 collective-permute-start.4
  86.0 4.0 %collective-permute-done.3.refs_3_ = bf16[64,2048]{1,0:T(8,128)(2,1)S(1)} collective-permute-done((bf16[64,2048]{1,0:T(8,128)(2,1)S(1)}, bf16[64,2048]{1,0:T(8,128)(2,1)S(1)}, u32[]{:S(2)}, u32[]{:S(2)}) %collective-permute-start.3) | collective-permute-done | bytes 262176 | tf_op jit(solution)/shard_map/ppermute | solution.py:314
  90.0 1.1 collective-permute-done.4.refs_4_
  91.1 0.8 collective-permute-start.30
  92.5 5.8 %copy-done.1 = bf16[8192,1024]{1,0:T(8,128)(2,1)S(1)} copy-done((bf16[8192,1024]{1,0:T(8,128)(2,1)S(1)}, bf16[8192,1024]{1,0:T(8,128)(2,1)}, u32[]{:S(2)}) %copy-start.1) | copy-done | bytes 16777240
  98.3 5.8 %copy-done.3 = bf16[8192,1024]{1,0:T(8,128)(2,1)S(1)} copy-done((bf16[8192,1024]{1,0:T(8,128)(2,1)S(1)}, bf16[8192,1024]{1,0:T(8,128)(2,1)}, u32[]{:S(2)}) %copy-start.3) | copy-done | bytes 16777240
  104.0 7.4 %wave2.1 = (bf16[64,2048]{1,0:T(8,128)(2,1)S(1)}, bf16[64,2048]{1,0:T(8,128)(2,1)S(1)}) custom-call(bf16[32,8192]{1,0:T(8,128)(2,1)S(1)} %collective-permute-done.18.refs_0_, bf16[32,8192]{1,0:T(8,128)(2,1)S(1)} %collective-permute-done.19.refs_1_, bf16[32,8192]{1,0:T(8,128)(2,1)S(1)} %collective-permute-done.20.refs_2_, ...), custom_call_target="tpu_custom_call" | custom-call | flops 4294967296 | bytes 2621440 | tf_op jit(solution)/shard_map/wave2/pallas_call | solution.py:225
  111.4 1.6 collective-permute-start.6
  113.0 0.5 collective-permute-start.7
  113.9 1.7 collective-permute-start.23
  115.9 7.2 %wave1.1 = (bf16[64,2048]{1,0:T(8,128)(2,1)S(1)}, bf16[64,2048]{1,0:T(8,128)(2,1)S(1)}) custom-call(bf16[32,8192]{1,0:T(8,128)(2,1)S(1)} %collective-permute-done.8.refs_0_, bf16[32,8192]{1,0:T(8,128)(2,1)S(1)} %collective-permute-done.9.refs_1_, bf16[32,8192]{1,0:T(8,128)(2,1)S(1)} %collective-permute-done.10.refs_2_, ...), custom_call_target="tpu_custom_call" | custom-call | flops 4294967296 | bytes 2621440 | tf_op jit(solution)/shard_map/wave1/pallas_call | solution.py:225
  123.1 1.8 collective-permute-start.24
  124.9 1.5 collective-permute-start.12
  126.4 7.0 %collective-permute-done.22.refs_18_ = bf16[64,2048]{1,0:T(8,128)(2,1)S(1)} collective-permute-done((bf16[64,2048]{1,0:T(8,128)(2,1)S(1)}, bf16[64,2048]{1,0:T(8,128)(2,1)S(1)}, u32[]{:S(2)}, u32[]{:S(2)}) %collective-permute-start.22) | collective-permute-done | bytes 262176 | tf_op jit(solution)/shard_map/ppermute | solution.py:314
  133.4 0.5 collective-permute-start.31
  133.9 0.5 collective-permute-start.15
  134.7 4.3 %collective-permute-done.12.refs_10_ = bf16[64,2048]{1,0:T(8,128)(2,1)S(1)} collective-permute-done((bf16[64,2048]{1,0:T(8,128)(2,1)S(1)}, bf16[64,2048]{1,0:T(8,128)(2,1)S(1)}, u32[]{:S(2)}, u32[]{:S(2)}) %collective-permute-start.12) | collective-permute-done | bytes 262176 | tf_op jit(solution)/shard_map/ppermute | solution.py:314
  139.1 4.0 %collective-permute-done.15.refs_13_ = bf16[64,2048]{1,0:T(8,128)(2,1)S(1)} collective-permute-done((bf16[64,2048]{1,0:T(8,128)(2,1)S(1)}, bf16[64,2048]{1,0:T(8,128)(2,1)S(1)}, u32[]{:S(2)}, u32[]{:S(2)}) %collective-permute-start.15) | collective-permute-done | bytes 262176 | tf_op jit(solution)/shard_map/ppermute | solution.py:314
  143.1 0.5 collective-permute-start.26
  143.9 0.5 collective-permute-start.27
  144.4 4.3 %collective-permute-done.14.refs_12_ = bf16[64,2048]{1,0:T(8,128)(2,1)S(1)} collective-permute-done((bf16[64,2048]{1,0:T(8,128)(2,1)S(1)}, bf16[64,2048]{1,0:T(8,128)(2,1)S(1)}, u32[]{:S(2)}, u32[]{:S(2)}) %collective-permute-start.14) | collective-permute-done | bytes 262176 | tf_op jit(solution)/shard_map/ppermute | solution.py:314
  148.7 0.5 collective-permute-start.16
  149.5 7.6 %wave4.1 = (bf16[32,2048]{1,0:T(8,128)(2,1)S(1)}, bf16[32,2048]{1,0:T(8,128)(2,1)S(1)}) custom-call(bf16[32,8192]{1,0:T(8,128)(2,1)S(1)} %collective-permute-done.38.refs_0_, bf16[32,8192]{1,0:T(8,128)(2,1)S(1)} %collective-permute-done.39.refs_1_, bf16[32,8192]{1,0:T(8,128)(2,1)S(1)} %collective-permute-done.40.refs_2_, ...), custom_call_target="tpu_custom_call" | custom-call | flops 2147483648 | bytes 1310720 | tf_op jit(solution)/shard_map/wave4/pallas_call | solution.py:225
  157.1 1.8 collective-permute-start.42
  158.9 1.5 collective-permute-start.45
  160.4 7.6 %wave3.1 = (bf16[32,2048]{1,0:T(8,128)(2,1)S(1)}, bf16[32,2048]{1,0:T(8,128)(2,1)S(1)}) custom-call(bf16[32,8192]{1,0:T(8,128)(2,1)S(1)} %collective-permute-done.28.refs_0_, bf16[32,8192]{1,0:T(8,128)(2,1)S(1)} %collective-permute-done.29.refs_1_, bf16[32,8192]{1,0:T(8,128)(2,1)S(1)} %collective-permute-done.30.refs_2_, ...), custom_call_target="tpu_custom_call" | custom-call | flops 2147483648 | bytes 1310720 | tf_op jit(solution)/shard_map/wave3/pallas_call | solution.py:225
  168.0 0.6 collective-permute-start.43
  168.9 1.7 collective-permute-start.32
  170.6 1.5 collective-permute-start.35
  172.2 0.5 collective-permute-start.33
  172.7 1.4 collective-permute-done.43.refs_35_
  174.2 0.7 collective-permute-done.44.refs_36_
  174.9 1.2 collective-permute-start.46
  176.1 0.8 collective-permute-done.32.refs_26_
  177.1 0.6 collective-permute-done.35.refs_29_
  177.7 0.9 collective-permute-start.36
  178.6 0.7 collective-permute-done.33.refs_27_
  179.3 0.6 collective-permute-start.37
  180.2 1.4 collective-permute-done.46.refs_38_
  181.8 1.1 collective-permute-done.36.refs_30_
  183.0 1.3 collective-permute-done.37.refs_31_
  184.3 19.9 %place.1 = (bf16[1024,1024]{1,0:T(8,128)(2,1)}, bf16[1024,1024]{1,0:T(8,128)(2,1)}) custom-call(s32[16]{0:T(128)S(1)} %copy-done.5, s32[16]{0:T(128)S(1)} %copy-done.6, bf16[64,2048]{1,0:T(8,128)(2,1)S(1)} %get-tuple-element.18.refs_0_, bf16[64,2048]{1,0:T(8,128)(2,1)S(1)} %get-tuple-element.19.refs_1_, bf16[64,2048]{1,0:T(8,128)(2,1)S(1)} %collective-permute-done.2.refs_2_, ...), custom_call_target="tpu_custom_call" | custom-call | bytes 20971520 | tf_op jit(solution)/shard_map/place/pallas_call | solution.py:291
  (60 shorter events, 4.5 us)
Async XLA Ops:
  1.4 1.2 copy-start.4
  3.3 12.8 %collective-permute-start = (bf16[32,8192]{1,0:T(8,128)(2,1)S(1)}, bf16[32,8192]{1,0:T(8,128)(2,1)S(1)}, u32[]{:S(2)}, u32[]{:S(2)}) collective-permute-start(bf16[32,8192]{1,0:T(8,128)(2,1)S(1)} %get-tuple-element.16.lo), channel_id=1, source_target_pairs={{0,1},{1,0},{2,3},{3,2},{4,5},{5,4},{6,7},{7,6},{8,9},{9,8},{10,11... | collective-permute-start | bytes 1572872 | tf_op jit(solution)/shard_map/ppermute | solution.py:311
  3.8 13.1 %collective-permute-start.1 = (bf16[32,8192]{1,0:T(8,128)(2,1)S(1)}, bf16[32,8192]{1,0:T(8,128)(2,1)}, u32[]{:S(2)}, u32[]{:S(2)}) collective-permute-start(bf16[32,8192]{1,0:T(8,128)(2,1)S(1)} %get-tuple-element.17.hi), channel_id=1, source_target_pairs={{0,1},{1,0},{2,3},{3,2},{4,5},{5,4},{6,7},{7,6},{8,9},{9,8},{10,11... | collective-permute-start | bytes 1572872 | tf_op jit(solution)/shard_map/ppermute | solution.py:311
  3.9 39.2 %collective-permute-start.18 = (bf16[32,8192]{1,0:T(8,128)(2,1)S(1)}, bf16[32,8192]{1,0:T(8,128)(2,1)S(1)}, u32[]{:S(2)}, u32[]{:S(2)}) collective-permute-start(bf16[32,8192]{1,0:T(8,128)(2,1)S(1)} %get-tuple-element.17.hi), channel_id=1, source_target_pairs={{0,4},{1,5},{2,6},{3,7},{4,0},{5,1},{6,2},{7,3},{8,12},{9,13},{10,... | collective-permute-start | bytes 1572872 | tf_op jit(solution)/shard_map/ppermute | solution.py:308
  7.9 67.2 %collective-permute-start.38 = (bf16[32,8192]{1,0:T(8,128)(2,1)S(1)}, bf16[32,8192]{1,0:T(8,128)(2,1)S(1)}, u32[]{:S(2)}, u32[]{:S(2)}) collective-permute-start(bf16[32,8192]{1,0:T(8,128)(2,1)S(1)} %get-tuple-element.17.hi), channel_id=1, source_target_pairs={{2,4},{3,5},{4,2},{5,3},{0,0},{1,1},{6,6},{7,7},{10,12},{11,13},{1... | collective-permute-start | bytes 1572872 | tf_op jit(solution)/shard_map/ppermute | solution.py:308
  8.6 68.2 %collective-permute-start.8 = (bf16[32,8192]{1,0:T(8,128)(2,1)S(1)}, bf16[32,8192]{1,0:T(8,128)(2,1)S(1)}, u32[]{:S(2)}, u32[]{:S(2)}) collective-permute-start(bf16[32,8192]{1,0:T(8,128)(2,1)S(1)} %get-tuple-element.16.lo), channel_id=1, source_target_pairs={{0,4},{1,5},{2,6},{3,7},{4,0},{5,1},{6,2},{7,3},{8,12},{9,13},{10,... | collective-permute-start | bytes 1572872 | tf_op jit(solution)/shard_map/ppermute | solution.py:308
  16.1 62.2 %collective-permute-start.28 = (bf16[32,8192]{1,0:T(8,128)(2,1)S(1)}, bf16[32,8192]{1,0:T(8,128)(2,1)S(1)}, u32[]{:S(2)}, u32[]{:S(2)}) collective-permute-start(bf16[32,8192]{1,0:T(8,128)(2,1)S(1)} %get-tuple-element.16.lo), channel_id=1, source_target_pairs={{2,4},{3,5},{4,2},{5,3},{0,0},{1,1},{6,6},{7,7},{10,12},{11,13},{1... | collective-permute-start | bytes 1572872 | tf_op jit(solution)/shard_map/ppermute | solution.py:308
  16.9 63.3 %collective-permute-start.20 = (bf16[32,8192]{1,0:T(8,128)(2,1)S(1)}, bf16[32,8192]{1,0:T(8,128)(2,1)S(1)}, u32[]{:S(2)}, u32[]{:S(2)}) collective-permute-start(bf16[32,8192]{1,0:T(8,128)(2,1)S(1)} %get-tuple-element.17.hi), channel_id=1, source_target_pairs={{0,2},{1,3},{2,0},{3,1},{4,6},{5,7},{6,4},{7,5},{8,10},{9,11},{10,... | collective-permute-start | bytes 1572872 | tf_op jit(solution)/shard_map/ppermute | solution.py:308
  43.1 37.2 %collective-permute-start.10 = (bf16[32,8192]{1,0:T(8,128)(2,1)S(1)}, bf16[32,8192]{1,0:T(8,128)(2,1)S(1)}, u32[]{:S(2)}, u32[]{:S(2)}) collective-permute-start(bf16[32,8192]{1,0:T(8,128)(2,1)S(1)} %get-tuple-element.16.lo), channel_id=1, source_target_pairs={{0,2},{1,3},{2,0},{3,1},{4,6},{5,7},{6,4},{7,5},{8,10},{9,11},{10,... | collective-permute-start | bytes 1572872 | tf_op jit(solution)/shard_map/ppermute | solution.py:308
  63.5 5.8 %copy-start = (bf16[8192,1024]{1,0:T(8,128)(2,1)}, bf16[8192,1024]{1,0:T(8,128)(2,1)S(1)}, u32[]{:S(2)}) copy-start(bf16[8192,1024]{1,0:T(8,128)(2,1)S(1)} %get-tuple-element.20.refs_4_) | copy-start | bytes 50331652
  69.3 5.8 %copy-start.2 = (bf16[8192,1024]{1,0:T(8,128)(2,1)}, bf16[8192,1024]{1,0:T(8,128)(2,1)S(1)}, u32[]{:S(2)}) copy-start(bf16[8192,1024]{1,0:T(8,128)(2,1)S(1)} %get-tuple-element.21.refs_5_) | copy-start | bytes 50331652
  75.1 7.9 %collective-permute-start.2 = (bf16[64,2048]{1,0:T(8,128)(2,1)S(1)}, bf16[64,2048]{1,0:T(8,128)(2,1)S(1)}, u32[]{:S(2)}, u32[]{:S(2)}) collective-permute-start(bf16[64,2048]{1,0:T(8,128)(2,1)S(1)} %get-tuple-element.18.refs_0_), channel_id=1, source_target_pairs={{0,8},{8,0},{16,24},{24,16},{1,9},{9,1},{17,25},{25,17},{2,10},{10... | collective-permute-start | bytes 786440 | tf_op jit(solution)/shard_map/ppermute | solution.py:314
  76.7 7.8 %collective-permute-start.5 = (bf16[64,2048]{1,0:T(8,128)(2,1)S(1)}, bf16[64,2048]{1,0:T(8,128)(2,1)S(1)}, u32[]{:S(2)}, u32[]{:S(2)}) collective-permute-start(bf16[64,2048]{1,0:T(8,128)(2,1)S(1)} %get-tuple-element.19.refs_1_), channel_id=1, source_target_pairs={{0,16},{8,24},{16,0},{24,8},{1,17},{9,25},{17,1},{25,9},{2,18},{10... | collective-permute-start | bytes 786440 | tf_op jit(solution)/shard_map/ppermute | solution.py:314
  78.3 13.6 %collective-permute-start.40 = (bf16[32,8192]{1,0:T(8,128)(2,1)S(1)}, bf16[32,8192]{1,0:T(8,128)(2,1)S(1)}, u32[]{:S(2)}, u32[]{:S(2)}) collective-permute-start(bf16[32,8192]{1,0:T(8,128)(2,1)S(1)} %collective-permute-done.18.refs_0_), channel_id=1, source_target_pairs={{2,0},{3,1},{4,6},{5,7},{0,2},{1,3},{6,4},{7,5},{10,8},{11,9},{12,... | collective-permute-start | bytes 1572872 | tf_op jit(solution)/shard_map/ppermute | solution.py:308
  80.3 11.6 %collective-permute-start.19 = (bf16[32,8192]{1,0:T(8,128)(2,1)S(1)}, bf16[32,8192]{1,0:T(8,128)(2,1)S(1)}, u32[]{:S(2)}, u32[]{:S(2)}) collective-permute-start(bf16[32,8192]{1,0:T(8,128)(2,1)S(1)} %collective-permute-done.18.refs_0_), channel_id=1, source_target_pairs={{0,1},{1,0},{2,3},{3,2},{4,5},{5,4},{6,7},{7,6},{8,9},{9,8},{10,11... | collective-permute-start | bytes 1572872 | tf_op jit(solution)/shard_map/ppermute | solution.py:311
  80.3 12.1 %collective-permute-start.21 = (bf16[32,8192]{1,0:T(8,128)(2,1)S(1)}, bf16[32,8192]{1,0:T(8,128)(2,1)S(1)}, u32[]{:S(2)}, u32[]{:S(2)}) collective-permute-start(bf16[32,8192]{1,0:T(8,128)(2,1)S(1)} %collective-permute-done.20.refs_2_), channel_id=1, source_target_pairs={{0,1},{1,0},{2,3},{3,2},{4,5},{5,4},{6,7},{7,6},{8,9},{9,8},{10,11... | collective-permute-start | bytes 1572872 | tf_op jit(solution)/shard_map/ppermute | solution.py:311
  83.0 7.0 %collective-permute-start.3 = (bf16[64,2048]{1,0:T(8,128)(2,1)S(1)}, bf16[64,2048]{1,0:T(8,128)(2,1)S(1)}, u32[]{:S(2)}, u32[]{:S(2)}) collective-permute-start(bf16[64,2048]{1,0:T(8,128)(2,1)S(1)} %get-tuple-element.19.refs_1_), channel_id=1, source_target_pairs={{0,8},{8,0},{16,24},{24,16},{1,9},{9,1},{17,25},{25,17},{2,10},{10... | collective-permute-start | bytes 786440 | tf_op jit(solution)/shard_map/ppermute | solution.py:314
  84.5 6.6 %collective-permute-start.4 = (bf16[64,2048]{1,0:T(8,128)(2,1)S(1)}, bf16[64,2048]{1,0:T(8,128)(2,1)S(1)}, u32[]{:S(2)}, u32[]{:S(2)}) collective-permute-start(bf16[64,2048]{1,0:T(8,128)(2,1)S(1)} %get-tuple-element.18.refs_0_), channel_id=1, source_target_pairs={{0,16},{8,24},{16,0},{24,8},{1,17},{9,25},{17,1},{25,9},{2,18},{10... | collective-permute-start | bytes 786440 | tf_op jit(solution)/shard_map/ppermute | solution.py:314
  90.0 21.4 %collective-permute-start.39 = (bf16[32,8192]{1,0:T(8,128)(2,1)S(1)}, bf16[32,8192]{1,0:T(8,128)(2,1)S(1)}, u32[]{:S(2)}, u32[]{:S(2)}) collective-permute-start(bf16[32,8192]{1,0:T(8,128)(2,1)S(1)} %collective-permute-done.38.refs_0_), channel_id=1, source_target_pairs={{0,1},{1,0},{2,3},{3,2},{4,5},{5,4},{6,7},{7,6},{8,9},{9,8},{10,11... | collective-permute-start | bytes 1572872 | tf_op jit(solution)/shard_map/ppermute | solution.py:311
  91.1 22.0 %collective-permute-start.30 = (bf16[32,8192]{1,0:T(8,128)(2,1)S(1)}, bf16[32,8192]{1,0:T(8,128)(2,1)S(1)}, u32[]{:S(2)}, u32[]{:S(2)}) collective-permute-start(bf16[32,8192]{1,0:T(8,128)(2,1)S(1)} %collective-permute-done.8.refs_0_), channel_id=1, source_target_pairs={{2,0},{3,1},{4,6},{5,7},{0,2},{1,3},{6,4},{7,5},{10,8},{11,9},{12,... | collective-permute-start | bytes 1572872 | tf_op jit(solution)/shard_map/ppermute | solution.py:308
  91.9 21.6 %collective-permute-start.29 = (bf16[32,8192]{1,0:T(8,128)(2,1)S(1)}, bf16[32,8192]{1,0:T(8,128)(2,1)S(1)}, u32[]{:S(2)}, u32[]{:S(2)}) collective-permute-start(bf16[32,8192]{1,0:T(8,128)(2,1)S(1)} %collective-permute-done.28.refs_0_), channel_id=1, source_target_pairs={{0,1},{1,0},{2,3},{3,2},{4,5},{5,4},{6,7},{7,6},{8,9},{9,8},{10,11... | collective-permute-start | bytes 1572872 | tf_op jit(solution)/shard_map/ppermute | solution.py:311
  91.9 21.9 %collective-permute-start.9 = (bf16[32,8192]{1,0:T(8,128)(2,1)S(1)}, bf16[32,8192]{1,0:T(8,128)(2,1)S(1)}, u32[]{:S(2)}, u32[]{:S(2)}) collective-permute-start(bf16[32,8192]{1,0:T(8,128)(2,1)S(1)} %collective-permute-done.8.refs_0_), channel_id=1, source_target_pairs={{0,1},{1,0},{2,3},{3,2},{4,5},{5,4},{6,7},{7,6},{8,9},{9,8},{10,11... | collective-permute-start | bytes 1572872 | tf_op jit(solution)/shard_map/ppermute | solution.py:311
  92.4 23.1 %collective-permute-start.11 = (bf16[32,8192]{1,0:T(8,128)(2,1)S(1)}, bf16[32,8192]{1,0:T(8,128)(2,1)S(1)}, u32[]{:S(2)}, u32[]{:S(2)}) collective-permute-start(bf16[32,8192]{1,0:T(8,128)(2,1)S(1)} %collective-permute-done.10.refs_2_), channel_id=1, source_target_pairs={{0,1},{1,0},{2,3},{3,2},{4,5},{5,4},{6,7},{7,6},{8,9},{9,8},{10,11... | collective-permute-start | bytes 1572872 | tf_op jit(solution)/shard_map/ppermute | solution.py:311
  92.5 5.8 %copy-start.1 = (bf16[8192,1024]{1,0:T(8,128)(2,1)S(1)}, bf16[8192,1024]{1,0:T(8,128)(2,1)}, u32[]{:S(2)}) copy-start(bf16[8192,1024]{1,0:T(8,128)(2,1)} %copy-done) | copy-start | bytes 50331652
  98.3 5.8 %copy-start.3 = (bf16[8192,1024]{1,0:T(8,128)(2,1)S(1)}, bf16[8192,1024]{1,0:T(8,128)(2,1)}, u32[]{:S(2)}) copy-start(bf16[8192,1024]{1,0:T(8,128)(2,1)} %copy-done.2) | copy-start | bytes 50331652
  111.4 11.7 %collective-permute-start.6 = (bf16[64,2048]{1,0:T(8,128)(2,1)S(1)}, bf16[64,2048]{1,0:T(8,128)(2,1)S(1)}, u32[]{:S(2)}, u32[]{:S(2)}) collective-permute-start(bf16[64,2048]{1,0:T(8,128)(2,1)S(1)} %collective-permute-done.2.refs_2_), channel_id=1, source_target_pairs={{0,16},{8,24},{16,0},{24,8},{1,17},{9,25},{17,1},{25,9},{2,18},{10... | collective-permute-start | bytes 786440 | tf_op jit(solution)/shard_map/ppermute | solution.py:314
  113.0 11.9 %collective-permute-start.7 = (bf16[64,2048]{1,0:T(8,128)(2,1)S(1)}, bf16[64,2048]{1,0:T(8,128)(2,1)S(1)}, u32[]{:S(2)}, u32[]{:S(2)}) collective-permute-start(bf16[64,2048]{1,0:T(8,128)(2,1)S(1)} %collective-permute-done.5.refs_5_), channel_id=1, source_target_pairs={{0,8},{8,0},{16,24},{24,16},{1,9},{9,1},{17,25},{25,17},{2,10},{10... | collective-permute-start | bytes 786440 | tf_op jit(solution)/shard_map/ppermute | solution.py:314
  113.6 19.9 %collective-permute-start.25 = (bf16[64,2048]{1,0:T(8,128)(2,1)S(1)}, bf16[64,2048]{1,0:T(8,128)(2,1)S(1)}, u32[]{:S(2)}, u32[]{:S(2)}) collective-permute-start(bf16[64,2048]{1,0:T(8,128)(2,1)S(1)} %get-tuple-element.25.refs_17_), channel_id=1, source_target_pairs={{0,16},{8,24},{16,0},{24,8},{1,17},{9,25},{17,1},{25,9},{2,18},{10... | collective-permute-start | bytes 786440 | tf_op jit(solution)/shard_map/ppermute | solution.py:314
  113.9 20.1 %collective-permute-start.23 = (bf16[64,2048]{1,0:T(8,128)(2,1)S(1)}, bf16[64,2048]{1,0:T(8,128)(2,1)S(1)}, u32[]{:S(2)}, u32[]{:S(2)}) collective-permute-start(bf16[64,2048]{1,0:T(8,128)(2,1)S(1)} %get-tuple-element.25.refs_17_), channel_id=1, source_target_pairs={{0,8},{8,0},{16,24},{24,16},{1,9},{9,1},{17,25},{25,17},{2,10},{10... | collective-permute-start | bytes 786440 | tf_op jit(solution)/shard_map/ppermute | solution.py:314
  115.6 17.8 %collective-permute-start.22 = (bf16[64,2048]{1,0:T(8,128)(2,1)S(1)}, bf16[64,2048]{1,0:T(8,128)(2,1)S(1)}, u32[]{:S(2)}, u32[]{:S(2)}) collective-permute-start(bf16[64,2048]{1,0:T(8,128)(2,1)S(1)} %get-tuple-element.24.refs_16_), channel_id=1, source_target_pairs={{0,8},{8,0},{16,24},{24,16},{1,9},{9,1},{17,25},{25,17},{2,10},{10... | collective-permute-start | bytes 786440 | tf_op jit(solution)/shard_map/ppermute | solution.py:314
  123.1 11.3 %collective-permute-start.24 = (bf16[64,2048]{1,0:T(8,128)(2,1)S(1)}, bf16[64,2048]{1,0:T(8,128)(2,1)S(1)}, u32[]{:S(2)}, u32[]{:S(2)}) collective-permute-start(bf16[64,2048]{1,0:T(8,128)(2,1)S(1)} %get-tuple-element.24.refs_16_), channel_id=1, source_target_pairs={{0,16},{8,24},{16,0},{24,8},{1,17},{9,25},{17,1},{25,9},{2,18},{10... | collective-permute-start | bytes 786440 | tf_op jit(solution)/shard_map/ppermute | solution.py:314
  124.9 14.1 %collective-permute-start.12 = (bf16[64,2048]{1,0:T(8,128)(2,1)S(1)}, bf16[64,2048]{1,0:T(8,128)(2,1)S(1)}, u32[]{:S(2)}, u32[]{:S(2)}) collective-permute-start(bf16[64,2048]{1,0:T(8,128)(2,1)S(1)} %get-tuple-element.22.refs_8_), channel_id=1, source_target_pairs={{0,8},{8,0},{16,24},{24,16},{1,9},{9,1},{17,25},{25,17},{2,10},{10... | collective-permute-start | bytes 786440 | tf_op jit(solution)/shard_map/ppermute | solution.py:314
  133.4 15.8 %collective-permute-start.41 = (bf16[32,8192]{1,0:T(8,128)(2,1)S(1)}, bf16[32,8192]{1,0:T(8,128)(2,1)S(1)}, u32[]{:S(2)}, u32[]{:S(2)}) collective-permute-start(bf16[32,8192]{1,0:T(8,128)(2,1)S(1)} %collective-permute-done.40.refs_2_), channel_id=1, source_target_pairs={{0,1},{1,0},{2,3},{3,2},{4,5},{5,4},{6,7},{7,6},{8,9},{9,8},{10,11... | collective-permute-start | bytes 1572872 | tf_op jit(solution)/shard_map/ppermute | solution.py:311
  133.4 23.7 %collective-permute-start.31 = (bf16[32,8192]{1,0:T(8,128)(2,1)S(1)}, bf16[32,8192]{1,0:T(8,128)(2,1)S(1)}, u32[]{:S(2)}, u32[]{:S(2)}) collective-permute-start(bf16[32,8192]{1,0:T(8,128)(2,1)S(1)} %collective-permute-done.30.refs_2_), channel_id=1, source_target_pairs={{0,1},{1,0},{2,3},{3,2},{4,5},{5,4},{6,7},{7,6},{8,9},{9,8},{10,11... | collective-permute-start | bytes 1572872 | tf_op jit(solution)/shard_map/ppermute | solution.py:311
  133.9 9.2 %collective-permute-start.15 = (bf16[64,2048]{1,0:T(8,128)(2,1)S(1)}, bf16[64,2048]{1,0:T(8,128)(2,1)S(1)}, u32[]{:S(2)}, u32[]{:S(2)}) collective-permute-start(bf16[64,2048]{1,0:T(8,128)(2,1)S(1)} %get-tuple-element.23.refs_9_), channel_id=1, source_target_pairs={{0,16},{8,24},{16,0},{24,8},{1,17},{9,25},{17,1},{25,9},{2,18},{10... | collective-permute-start | bytes 786440 | tf_op jit(solution)/shard_map/ppermute | solution.py:314
  134.4 9.4 %collective-permute-start.13 = (bf16[64,2048]{1,0:T(8,128)(2,1)S(1)}, bf16[64,2048]{1,0:T(8,128)(2,1)S(1)}, u32[]{:S(2)}, u32[]{:S(2)}) collective-permute-start(bf16[64,2048]{1,0:T(8,128)(2,1)S(1)} %get-tuple-element.23.refs_9_), channel_id=1, source_target_pairs={{0,8},{8,0},{16,24},{24,16},{1,9},{9,1},{17,25},{25,17},{2,10},{10... | collective-permute-start | bytes 786440 | tf_op jit(solution)/shard_map/ppermute | solution.py:314
  139.0 9.7 %collective-permute-start.14 = (bf16[64,2048]{1,0:T(8,128)(2,1)S(1)}, bf16[64,2048]{1,0:T(8,128)(2,1)S(1)}, u32[]{:S(2)}, u32[]{:S(2)}) collective-permute-start(bf16[64,2048]{1,0:T(8,128)(2,1)S(1)} %get-tuple-element.22.refs_8_), channel_id=1, source_target_pairs={{0,16},{8,24},{16,0},{24,8},{1,17},{9,25},{17,1},{25,9},{2,18},{10... | collective-permute-start | bytes 786440 | tf_op jit(solution)/shard_map/ppermute | solution.py:314
  143.1 15.8 %collective-permute-start.26 = (bf16[64,2048]{1,0:T(8,128)(2,1)S(1)}, bf16[64,2048]{1,0:T(8,128)(2,1)S(1)}, u32[]{:S(2)}, u32[]{:S(2)}) collective-permute-start(bf16[64,2048]{1,0:T(8,128)(2,1)S(1)} %collective-permute-done.22.refs_18_), channel_id=1, source_target_pairs={{0,16},{8,24},{16,0},{24,8},{1,17},{9,25},{17,1},{25,9},{2,18},{10... | collective-permute-start | bytes 786440 | tf_op jit(solution)/shard_map/ppermute | solution.py:314
  143.9 24.2 %collective-permute-start.27 = (bf16[64,2048]{1,0:T(8,128)(2,1)S(1)}, bf16[64,2048]{1,0:T(8,128)(2,1)S(1)}, u32[]{:S(2)}, u32[]{:S(2)}) collective-permute-start(bf16[64,2048]{1,0:T(8,128)(2,1)S(1)} %collective-permute-done.25.refs_21_), channel_id=1, source_target_pairs={{0,8},{8,0},{16,24},{24,16},{1,9},{9,1},{17,25},{25,17},{2,10},{10... | collective-permute-start | bytes 786440 | tf_op jit(solution)/shard_map/ppermute | solution.py:314
  148.7 19.9 %collective-permute-start.16 = (bf16[64,2048]{1,0:T(8,128)(2,1)S(1)}, bf16[64,2048]{1,0:T(8,128)(2,1)S(1)}, u32[]{:S(2)}, u32[]{:S(2)}) collective-permute-start(bf16[64,2048]{1,0:T(8,128)(2,1)S(1)} %collective-permute-done.12.refs_10_), channel_id=1, source_target_pairs={{0,16},{8,24},{16,0},{24,8},{1,17},{9,25},{17,1},{25,9},{2,18},{10... | collective-permute-start | bytes 786440 | tf_op jit(solution)/shard_map/ppermute | solution.py:314
  149.2 19.7 %collective-permute-start.17 = (bf16[64,2048]{1,0:T(8,128)(2,1)S(1)}, bf16[64,2048]{1,0:T(8,128)(2,1)S(1)}, u32[]{:S(2)}, u32[]{:S(2)}) collective-permute-start(bf16[64,2048]{1,0:T(8,128)(2,1)S(1)} %collective-permute-done.15.refs_13_), channel_id=1, source_target_pairs={{0,8},{8,0},{16,24},{24,16},{1,9},{9,1},{17,25},{25,17},{2,10},{10... | collective-permute-start | bytes 786440 | tf_op jit(solution)/shard_map/ppermute | solution.py:314
  157.1 13.5 %collective-permute-start.42 = (bf16[32,2048]{1,0:T(8,128)(2,1)S(1)}, bf16[32,2048]{1,0:T(8,128)(2,1)S(1)}, u32[]{:S(2)}, u32[]{:S(2)}) collective-permute-start(bf16[32,2048]{1,0:T(8,128)(2,1)S(1)} %get-tuple-element.28.refs_32_), channel_id=1, source_target_pairs={{0,8},{8,0},{16,24},{24,16},{1,9},{9,1},{17,25},{25,17},{2,10},{10... | collective-permute-start | bytes 393224 | tf_op jit(solution)/shard_map/ppermute | solution.py:314
  158.9 25.4 %copy-start.5 = (s32[16]{0:T(128)S(1)}, s32[16]{0:T(128)}, u32[]{:S(2)}) copy-start(s32[16]{0:T(128)} %lengths.1) | copy-start | bytes 196
  158.9 25.4 %copy-start.6 = (s32[16]{0:T(128)S(1)}, s32[16]{0:T(128)}, u32[]{:S(2)}) copy-start(s32[16]{0:T(128)} %owner.1) | copy-start | bytes 196
  158.9 13.3 %collective-permute-start.45 = (bf16[32,2048]{1,0:T(8,128)(2,1)S(1)}, bf16[32,2048]{1,0:T(8,128)(2,1)S(1)}, u32[]{:S(2)}, u32[]{:S(2)}) collective-permute-start(bf16[32,2048]{1,0:T(8,128)(2,1)S(1)} %get-tuple-element.29.refs_33_), channel_id=1, source_target_pairs={{0,16},{8,24},{16,0},{24,8},{1,17},{9,25},{17,1},{25,9},{2,18},{10... | collective-permute-start | bytes 393224 | tf_op jit(solution)/shard_map/ppermute | solution.py:314
  168.0 6.0 %collective-permute-start.43 = (bf16[32,2048]{1,0:T(8,128)(2,1)S(1)}, bf16[32,2048]{1,0:T(8,128)(2,1)S(1)}, u32[]{:S(2)}, u32[]{:S(2)}) collective-permute-start(bf16[32,2048]{1,0:T(8,128)(2,1)S(1)} %get-tuple-element.29.refs_33_), channel_id=1, source_target_pairs={{0,8},{8,0},{16,24},{24,16},{1,9},{9,1},{17,25},{25,17},{2,10},{10... | collective-permute-start | bytes 393224 | tf_op jit(solution)/shard_map/ppermute | solution.py:314
  168.6 6.3 %collective-permute-start.44 = (bf16[32,2048]{1,0:T(8,128)(2,1)S(1)}, bf16[32,2048]{1,0:T(8,128)(2,1)S(1)}, u32[]{:S(2)}, u32[]{:S(2)}) collective-permute-start(bf16[32,2048]{1,0:T(8,128)(2,1)S(1)} %get-tuple-element.28.refs_32_), channel_id=1, source_target_pairs={{0,16},{8,24},{16,0},{24,8},{1,17},{9,25},{17,1},{25,9},{2,18},{10... | collective-permute-start | bytes 393224 | tf_op jit(solution)/shard_map/ppermute | solution.py:314
  168.9 8.0 %collective-permute-start.32 = (bf16[32,2048]{1,0:T(8,128)(2,1)S(1)}, bf16[32,2048]{1,0:T(8,128)(2,1)S(1)}, u32[]{:S(2)}, u32[]{:S(2)}) collective-permute-start(bf16[32,2048]{1,0:T(8,128)(2,1)S(1)} %get-tuple-element.26.refs_24_), channel_id=1, source_target_pairs={{0,8},{8,0},{16,24},{24,16},{1,9},{9,1},{17,25},{25,17},{2,10},{10... | collective-permute-start | bytes 393224 | tf_op jit(solution)/shard_map/ppermute | solution.py:314
  170.6 7.1 %collective-permute-start.35 = (bf16[32,2048]{1,0:T(8,128)(2,1)S(1)}, bf16[32,2048]{1,0:T(8,128)(2,1)S(1)}, u32[]{:S(2)}, u32[]{:S(2)}) collective-permute-start(bf16[32,2048]{1,0:T(8,128)(2,1)S(1)} %get-tuple-element.27.refs_25_), channel_id=1, source_target_pairs={{0,16},{8,24},{16,0},{24,8},{1,17},{9,25},{17,1},{25,9},{2,18},{10... | collective-permute-start | bytes 393224 | tf_op jit(solution)/shard_map/ppermute | solution.py:314
  172.2 7.1 %collective-permute-start.33 = (bf16[32,2048]{1,0:T(8,128)(2,1)S(1)}, bf16[32,2048]{1,0:T(8,128)(2,1)S(1)}, u32[]{:S(2)}, u32[]{:S(2)}) collective-permute-start(bf16[32,2048]{1,0:T(8,128)(2,1)S(1)} %get-tuple-element.27.refs_25_), channel_id=1, source_target_pairs={{0,8},{8,0},{16,24},{24,16},{1,9},{9,1},{17,25},{25,17},{2,10},{10... | collective-permute-start | bytes 393224 | tf_op jit(solution)/shard_map/ppermute | solution.py:314
  174.1 6.1 %collective-permute-start.34 = (bf16[32,2048]{1,0:T(8,128)(2,1)S(1)}, bf16[32,2048]{1,0:T(8,128)(2,1)S(1)}, u32[]{:S(2)}, u32[]{:S(2)}) collective-permute-start(bf16[32,2048]{1,0:T(8,128)(2,1)S(1)} %get-tuple-element.26.refs_24_), channel_id=1, source_target_pairs={{0,16},{8,24},{16,0},{24,8},{1,17},{9,25},{17,1},{25,9},{2,18},{10... | collective-permute-start | bytes 393224 | tf_op jit(solution)/shard_map/ppermute | solution.py:314
  174.9 6.6 %collective-permute-start.46 = (bf16[32,2048]{1,0:T(8,128)(2,1)S(1)}, bf16[32,2048]{1,0:T(8,128)(2,1)S(1)}, u32[]{:S(2)}, u32[]{:S(2)}) collective-permute-start(bf16[32,2048]{1,0:T(8,128)(2,1)S(1)} %collective-permute-done.42.refs_34_), channel_id=1, source_target_pairs={{0,16},{8,24},{16,0},{24,8},{1,17},{9,25},{17,1},{25,9},{2,18},{10... | collective-permute-start | bytes 393224 | tf_op jit(solution)/shard_map/ppermute | solution.py:314
  176.9 5.0 %collective-permute-start.47 = (bf16[32,2048]{1,0:T(8,128)(2,1)S(1)}, bf16[32,2048]{1,0:T(8,128)(2,1)S(1)}, u32[]{:S(2)}, u32[]{:S(2)}) collective-permute-start(bf16[32,2048]{1,0:T(8,128)(2,1)S(1)} %collective-permute-done.45.refs_37_), channel_id=1, source_target_pairs={{0,8},{8,0},{16,24},{24,16},{1,9},{9,1},{17,25},{25,17},{2,10},{10... | collective-permute-start | bytes 393224 | tf_op jit(solution)/shard_map/ppermute | solution.py:314
  177.7 5.2 %collective-permute-start.36 = (bf16[32,2048]{1,0:T(8,128)(2,1)S(1)}, bf16[32,2048]{1,0:T(8,128)(2,1)S(1)}, u32[]{:S(2)}, u32[]{:S(2)}) collective-permute-start(bf16[32,2048]{1,0:T(8,128)(2,1)S(1)} %collective-permute-done.32.refs_26_), channel_id=1, source_target_pairs={{0,16},{8,24},{16,0},{24,8},{1,17},{9,25},{17,1},{25,9},{2,18},{10... | collective-permute-start | bytes 393224 | tf_op jit(solution)/shard_map/ppermute | solution.py:314
  179.3 5.0 %collective-permute-start.37 = (bf16[32,2048]{1,0:T(8,128)(2,1)S(1)}, bf16[32,2048]{1,0:T(8,128)(2,1)S(1)}, u32[]{:S(2)}, u32[]{:S(2)}) collective-permute-start(bf16[32,2048]{1,0:T(8,128)(2,1)S(1)} %collective-permute-done.35.refs_29_), channel_id=1, source_target_pairs={{0,8},{8,0},{16,24},{24,16},{1,9},{9,1},{17,25},{25,17},{2,10},{10... | collective-permute-start | bytes 393224 | tf_op jit(solution)/shard_map/ppermute | solution.py:314

commit v2 on v0

--- a/solution.py
+++ b/solution.py
@@ -1,9 +1,18 @@
+import functools
+
 import jax
 import jax.numpy as jnp
 from jax import lax
+from jax.experimental import pallas as pl
+from jax.experimental.pallas import tpu as pltpu
 from jax.sharding import PartitionSpec as P
 
 HD = 128
+BF = jnp.bfloat16
+F32 = jnp.float32
+MIB = 1 << 20
+VMEM = pltpu.VMEM
+ANY = pltpu.HBM
 
 
 def rotate(raw, pos):
@@ -33,7 +42,7 @@
     return (source, jnp.any(match, axis=1))
 
 
-def per_device(hidden, norm_gain, k_weight, k_bias, v_weight, v_bias, positions, lengths, owner):
+def gathered(hidden, norm_gain, k_weight, k_bias, v_weight, v_bias, positions, lengths, owner):
     rows = hidden.astype(jnp.float32)
     scale = lax.rsqrt(jnp.mean(rows * rows, axis=1, keepdims=True) + 1e-06)
     normed = (rows * scale * norm_gain.astype(jnp.float32)).astype(jnp.bfloat16)
@@ -61,6 +70,320 @@
     return (key_cache, value_cache)
 
 
+def norm_kernel(x_ref, gain_ref, out_ref, lo_ref, hi_ref):
+    step = 16
+    first = lo_ref.shape[0]
+    gain = gain_ref[...].astype(F32)
+    for at in range(0, x_ref.shape[0], step):
+        x = x_ref[at : at + step, :].astype(F32)
+        scale = lax.rsqrt(jnp.mean(x * x, axis=1, keepdims=True) + 1e-06)
+        y = (x * scale * gain).astype(BF)
+        out_ref[at : at + step, :] = y
+        if at < first:
+            lo_ref[at : at + step, :] = y
+        else:
+            hi_ref[at - first : at - first + step, :] = y
+
+
+def normalise(hidden, gain):
+    rows, wide = hidden.shape
+    return pl.pallas_call(
+        norm_kernel,
+        out_shape=tuple(VMEM((n, wide), BF) for n in (rows, *PART)),
+        name="norm",
+        cost_estimate=pl.CostEstimate(flops=rows * wide, bytes_accessed=rows, transcendentals=rows),
+        compiler_params=pltpu.CompilerParams(vmem_limit_bytes=16 * MIB),
+    )(hidden, gain.reshape(1, wide))
+
+
+PART = (32, 32)
+PART_AT = (0, 64)
+
+
+def piece_at(step, part):
+    return pl.multiple_of(((lax.axis_index("head") // 2) ^ step) * 128 + PART_AT[part], 32)
+
+
+def rotation(pieces, cos, sin):
+    return [
+        jnp.concatenate([table[pl.ds(piece_at(*piece), 2 * PART[piece[1]]), :] for piece in pieces], axis=0)
+        for table in (cos, sin)
+    ]
+
+
+def load_rows(x, pieces, sources, sem, start=True, wait=True):
+    core = lax.axis_index("head") % 2
+    base = 0
+    for i, ((step, part), (own, sib, row)) in enumerate(zip(pieces, sources)):
+        n = PART[part]
+        for j, src in enumerate((own, sib)):
+            at = pl.multiple_of(base + (core ^ j) * n, 16)
+            copy = pltpu.make_async_copy(src.at[pl.ds(row, n)], x.at[pl.ds(at, n)], sem.at[2 * i + j])
+            if start:
+                copy.start()
+            if wait:
+                copy.wait()
+        base += 2 * n
+
+
+def turn(raw, c, s):
+    raw = raw.astype(BF).astype(F32)
+    heads = []
+    for h in range(raw.shape[1] // HD):
+        one = raw[:, h * HD : (h + 1) * HD]
+        heads.append(one * c + pltpu.roll(one, HD // 2, axis=1) * s)
+    return jnp.concatenate(heads, axis=1).astype(BF)
+
+
+WHOLE = [(0, 0), (0, 1)]
+
+
+def both(own, sib):
+    return [(own, sib, 0), (own, sib, PART[0])]
+
+
+def wave_kernel(pieces, kind, count, *refs):
+    sources = refs[:count]
+    wk, wv, kb, vb, cos, sin = refs[count : count + 6]
+    outs, x, blocks, sem, wsem = refs[count + 6 : -4], *refs[-4:]
+    deep, width = wk.shape
+    depth, _, tile = blocks.shape
+    each = width // tile
+    half = deep // 2
+    copies = []
+    for i in range(2 * each):
+        cols = pl.ds(i % each * tile, tile)
+        copies.append(
+            [
+                pltpu.make_async_copy(
+                    (wk, wv)[i // each].at[pl.ds(j * half, half), cols],
+                    blocks.at[i % depth, pl.ds(j * half, half)],
+                    wsem.at[2 * i + j],
+                )
+                for j in range(2)
+            ]
+        )
+
+    def fetch(i):
+        for copy in copies[i]:
+            copy.start()
+
+    load = functools.partial(load_rows, x, pieces)
+    if kind == "relayed":
+        chip = lax.axis_index("head") // 2
+        at_end = (chip == 0) | (chip == 3)
+        rows = both(*sources[:2])
+        ends = both(*sources[2:])
+        pl.when(jnp.logical_not(at_end))(lambda: load(rows, sem, wait=False))
+        pl.when(at_end)(lambda: load(ends, sem, wait=False))
+    else:
+        rows = both(*sources) if kind == "whole" else [(sources[i], sources[i + 1], 0) for i in range(0, count, 2)]
+        load(rows, sem, wait=False)
+    for i in range(depth):
+        fetch(i)
+    c, s = rotation(pieces, cos, sin)
+    load(rows, sem, start=False)
+    part = x.shape[0] // len(outs)
+    for i in range(2 * each):
+        for copy in copies[i]:
+            copy.wait()
+        raw = jnp.dot(x[...], blocks[i % depth], preferred_element_type=F32)
+        if i < each:
+            y = turn(raw + kb[:, i * tile : (i + 1) * tile].astype(F32), c, s)
+        else:
+            at = (i - each) * tile
+            y = (raw + vb[:, at : at + tile].astype(F32)).astype(BF)
+        for k, out in enumerate(outs):
+            for j in range(out.shape[0] // part):
+                out[j * part : (j + 1) * part, i * tile : (i + 1) * tile] = y[k * part : (k + 1) * part]
+        if i + depth < 2 * each:
+            fetch(i + depth)
+
+
+def cost(m, deep, width, weights):
+    return pl.CostEstimate(flops=m * width, bytes_accessed=2 * m * width, transcendentals=0)
+
+
+def in_hbm(x):
+    return pltpu.with_memory_space_constraint(x, pltpu.HBM)
+
+
+def wave(name, pieces, kind, sources, wk, wv, rest, split=1, copies=1):
+    deep, width = wk.shape
+    m = sum(2 * PART[part] for _, part in pieces)
+    tile, depth = 256, 3
+    full = pl.BlockSpec(memory_space=VMEM)
+    hbm = pl.BlockSpec(memory_space=ANY)
+    return pl.pallas_call(
+        functools.partial(wave_kernel, pieces, kind, len(sources)),
+        out_shape=[VMEM((copies * m // split, 2 * width), BF)] * split,
+        in_specs=[hbm] * (len(sources) + 2) + [full] * 4,
+        out_specs=[full] * split,
+        scratch_shapes=[
+            VMEM((m, deep), BF),
+            VMEM((depth, deep, tile), BF),
+            pltpu.SemaphoreType.DMA((2 * len(pieces),)),
+            pltpu.SemaphoreType.DMA((4 * width // tile,)),
+        ],
+        name=name,
+        cost_estimate=cost(m, deep, width, True),
+        compiler_params=pltpu.CompilerParams(vmem_limit_bytes=24 * MIB),
+    )(*sources, wk, wv, *rest)
+
+
+def place_kernel(units, lengths, owner, *refs):
+    count = max(unit[3] for unit in units) + 1
+    sources = refs[:count]
+    key_out, value_out, rows = refs[count:]
+    width = key_out.shape[1]
+    group = lax.axis_index("group")
+    chip = lax.axis_index("head") // 2
+    for d, step, at, a, row, n in units:
+        whose = d[0] if isinstance(d, tuple) else group ^ d
+        to = pl.multiple_of(whose * 512 + (chip ^ step) * 128 + at, 16)
+        rows[pl.ds(to, n), :] = sources[a][row : row + n, :]
+    key_out[...] = jnp.zeros_like(key_out)
+    value_out[...] = jnp.zeros_like(value_out)
+    tile, window = 128, 256
+    total = rows.shape[0]
+
+    def request(q, carry):
+        start, local = carry
+        length = lengths[q]
+        mine = owner[q] == group
+
+        @pl.when(mine)
+        def _():
+            def step(t, c):
+                top = pl.multiple_of(t * tile, tile)
+                base = start + top - local
+                at = pl.multiple_of(jnp.clip((base >> 7) << 7, 0, total - window), 128)
+                lane = lax.broadcasted_iota(jnp.int32, (tile, window), 1)
+                p = lane & 127
+                first, second = PART
+                stay = (p < first) | (p >= 128 - second)
+                src = at + lane + jnp.where(stay, 0, jnp.where(p < 2 * first, second, -first))
+                dst = base + lax.broadcasted_iota(jnp.int32, (tile, window), 0)
+                hit = (src == dst) & (src >= start) & (src < start + length)
+                pick = jnp.where(hit, 1.0, 0.0).astype(BF)
+                for part, out in ((0, key_out), (1, value_out)):
+                    moved = jnp.dot(pick, rows[pl.ds(at, window), part * width : (part + 1) * width], preferred_element_type=F32)
+                    out[pl.ds(top, tile), :] += moved.astype(BF)
+                return c
+
+            lax.fori_loop(local // tile, (local + length - 1) // tile + 1, step, 0)
+
+        return (start + length, local + jnp.where(mine, length, 0))
+
+    lax.fori_loop(0, lengths.shape[0], request, (jnp.int32(0), jnp.int32(0)))
+
+
+def place(units, arrays, lengths, owner, cap, width, total):
+    out = jax.ShapeDtypeStruct((cap, width), BF)
+    smem = pl.BlockSpec(memory_space=pltpu.SMEM)
+    full = pl.BlockSpec(memory_space=VMEM)
+    return pl.pallas_call(
+        functools.partial(place_kernel, units),
+        out_shape=(out, out),
+        in_specs=[smem, smem] + [full] * len(arrays),
+        out_specs=(full, full),
+        scratch_shapes=[VMEM((total, 2 * width), BF)],
+        name="place",
+        cost_estimate=pl.CostEstimate(flops=0, bytes_accessed=20 * MIB, transcendentals=0),
+        compiler_params=pltpu.CompilerParams(vmem_limit_bytes=28 * MIB),
+    )(lengths, owner, *arrays)
+
+
+def pipelined(hidden, norm_gain, k_weight, k_bias, v_weight, v_bias, positions, lengths, owner):
+    width = k_weight.shape[1]
+    group = lax.axis_index("group")
+
+    def line(x, pairs):
+        return lax.ppermute(x, "head", [(2 * a + c, 2 * b + c) for a, b in pairs for c in range(2)])
+
+    def sibling(x):
+        return lax.ppermute(x, "head", [(i, i ^ 1) for i in range(8)])
+
+    def across(x, bit):
+        return lax.ppermute(x, "group", [(i, i ^ bit) for i in range(4)])
+
+    far_pairs = [(0, 2), (1, 3), (2, 0), (3, 1)]
+    near_pairs = [(0, 1), (1, 0), (2, 3), (3, 2)]
+    middle_pairs = [(1, 2), (2, 1)]
+
+    def after(x, *done):
+        return lax.optimization_barrier((x,) + done)[0]
+
+    own, lo, hi = normalise(hidden, norm_gain)
+    own_s = sibling(own)
+    far1, near1 = line(lo, far_pairs), line(lo, near_pairs)
+
+    half = HD // 2
+    freq = jnp.exp(jnp.arange(half, dtype=F32) * (-2.0 / HD * jnp.log(F32(1000000.0))))
+    pos = lax.dynamic_slice(positions, (group * 512,), (512,)).astype(F32)
+    pos = pos.reshape(4, 2, 64)
+    pos = jnp.concatenate([pos[:, :, : PART[0]].reshape(4, -1), pos[:, :, PART[0] :].reshape(4, -1)], axis=1).reshape(512)
+    angle = pos[:, None] * freq[None, :]
+    cosine, sine = jnp.cos(angle), jnp.sin(angle)
+    cos = jnp.concatenate([cosine, cosine], axis=1)
+    sin = jnp.concatenate([-sine, sine], axis=1)
+    rest = (k_bias.reshape(1, width), v_bias.reshape(1, width), cos, sin)
+
+    wk, wv = in_hbm(k_weight), in_hbm(v_weight)
+    together = lax.optimization_barrier
+
+    def to_all(p):
+        return [across(p, d) for d in (1, 2, 3)]
+
+    (p0,) = wave("wave0", WHOLE, "whole", [own, own_s], wk, wv, rest)
+    far1, near1, p0, lo, hi = together((far1, near1, p0, lo, hi))
+
+    a0 = to_all(p0)
+    far2, near2 = line(hi, far_pairs), line(hi, near_pairs)
+    pieces1 = [(2, 0), (1, 0)]
+    (p1,) = wave("wave1", pieces1, "pieces", [far1, sibling(far1), near1, sibling(near1)], wk, wv, rest)
+    a0, far1, far2, near2, p1, own = together((a0, far1, far2, near2, p1, own))
+
+    a1 = to_all(p1)
+    middle, relay = line(own, middle_pairs), line(jnp.concatenate([far1, far2]), near_pairs)
+    pieces2 = [(2, 1), (1, 1)]
+    p2 = wave("wave2", pieces2, "pieces", [far2, sibling(far2), near2, sibling(near2)], wk, wv, rest, 2)
+    a1, middle, relay, p2 = together((a1, middle, relay, p2))
+
+    x2, y2 = [across(p, 1) for p in p2], [across(p, 2) for p in p2]
+    sources = [middle, sibling(middle), relay, sibling(relay)]
+    pieces3 = [(3, 0), (3, 1)]
+    p3 = wave("wave3", pieces3, "relayed", sources, wk, wv, rest, 2)
+    p3, x2, y2 = together((p3, x2, y2))
+    x3, y3 = [across(p, 1) for p in p3], [across(p, 2) for p in p3]
+    d2 = [across(x2[0], 2), across(y2[1], 1)]
+    x3, y3, d2 = together((x3, y3, d2))
+    d3 = [across(x3[0], 2), across(y3[1], 1)]
+
+    units, arrays = [], []
+
+    def arrived(pieces, split, got):
+        total = sum(2 * PART[part] for _, part in pieces)
+        each = total // split
+        for d, parts in enumerate(got):
+            row = 0
+            for step, part in pieces:
+                done = 0
+                while done < 2 * PART[part]:
+                    i = (row + done) // each
+                    n = min(2 * PART[part] - done, (i + 1) * each - row - done)
+                    units.append((d, step, PART_AT[part] + done, len(arrays) + i, row + done - i * each, n))
+                    done += n
+                row += done
+            arrays.extend(parts)
+
+    arrived(pieces2, 2, (p2, x2, y2, d2))
+    arrived(pieces3, 2, (p3, x3, y3, d3))
+    arrived(WHOLE, 1, [[one] for one in (p0, *a0)])
+    arrived(pieces1, 1, [[one] for one in (p1, *a1)])
+    return place(units, arrays, lengths, owner, 1024, width, 2048)
+
+
 def solution(mesh):
     in_specs = (
         P(("group", "head"), None),
@@ -74,6 +397,7 @@
         P(),
     )
     out_specs = (P("group", "head"), P("group", "head"))
+    square = mesh.shape["group"] == 4 and mesh.shape["head"] == 8
     return jax.shard_map(
-        per_device, mesh=mesh, in_specs=in_specs, out_specs=out_specs, check_vma=False
+        pipelined if square else gathered, mesh=mesh, in_specs=in_specs, out_specs=out_specs, check_vma=False
     )

time: 246 us -> 144 us (0.59)
  waiting for transfers between devices: 162 us -> 45.1 us
  Pallas kernels: 0 us -> 60 us
  starting transfers between devices: 0.08 us -> 31.7 us
  matrix products: 29.7 us -> 0 us
  local copies, waits for them, and re-layouts: 20.7 us -> 4.47 us
  other arithmetic: 18.3 us -> 2.11 us
  between operations: 14.3 us -> 0.8 us
    all_gather x2 -> x0, waiting for transfers between devices: 162 us -> none  [the longest x1 84.8 us: per_device(): piece = lax.all_gather(normed, 'head', axis=0, tiled=True)]
    pallas_call x0 -> x6, Pallas kernels: none -> 60 us  [the longest x4 51.5 us: wave(): pl.pallas_call(functools.partial(wave_kernel, pieces, kind, len(sources))...]
    ppermute x0 -> x31, waiting for transfers between devices: none -> 45.1 us  [the longest x18 31.1 us: across(): return lax.ppermute(x, 'group', [(i, i ^ bit) for i in range(4)])]
    ppermute x0 -> x31, starting transfers between devices: none -> 31.7 us  [the longest x18 20.3 us: across(): return lax.ppermute(x, 'group', [(i, i ^ bit) for i in range(4)])]
    dot_general x2 -> x0, matrix products: 29.7 us -> none  [the longest x1 17.2 us: per_device(): jnp.dot(piece, v_weight, preferred_element_type=jnp.float32)]
    gather x2 -> x0, local copies, waits for them, and re-layouts: 19.4 us -> none  [the longest x1 13.3 us: per_device(): jnp.take(everything, source, axis=0)]
    select_n x3 -> x0, other arithmetic: 4.59 us -> none  [the longest x1 2.92 us: per_device(): jnp.where(valid[:, None], jnp.take(everything, source, axis=0), zero)]
    convert_element_type x5 -> x1, other arithmetic: 3.25 us -> 0.76 us  [pipelined(): pos = lax.dynamic_slice(positions, (group * 512,), (512,)).astype(F32)]
  transfers between devices with their start and end apart: 2 -> 31, of which waited for: 2 -> 13; matrix products, arithmetic and copies ran while one was open for 4% -> 3% of each run, Pallas kernels for 0% -> 36%
where the time goes in v2:
time: 144 us
  Pallas kernels  60 us (42%)
  waiting for transfers between devices  45.1 us (31%)
  starting transfers between devices  31.7 us (22%)
  local copies, waits for them, and re-layouts  4.47 us (3%)
  other arithmetic  2.11 us (1%)
    pallas_call x4, Pallas kernels, wave(): pl.pallas_call(functools.partial(wave_kernel, pieces, kind, len(sources))...  51.5 us
    ppermute x18, waiting for transfers between devices, across(): return lax.ppermute(x, 'group', [(i, i ^ bit) for i in range(4)])  31.1 us
    ppermute x18, starting transfers between devices, across(): return lax.ppermute(x, 'group', [(i, i ^ bit) for i in range(4)])  20.3 us
    ppermute x6, waiting for transfers between devices, line(): lax.ppermute(x, 'head', [(2 * a + c, 2 * b + c) for a, b in pairs for c i...  14 us
    ppermute x6, starting transfers between devices, line(): lax.ppermute(x, 'head', [(2 * a + c, 2 * b + c) for a, b in pairs for c i...  9.31 us
    pallas_call x1, Pallas kernels, place(): pl.pallas_call(functools.partial(place_kernel, units), out_shape=(out, ou...  7.21 us
  transfers between devices with their start and end apart: 31, of which 13 were waited for; matrix products, arithmetic and copies ran while one was open for 3% of the time, Pallas kernels for 36%

profile of v2, /device:TPU:0, one launch (start us, length us, event | category | flops | bytes accessed | tf_op | source)
XLA Modules:
  0.0 144.1 jit_solution(6412392799196442581)
XLA Ops:
  0.6 0.7 reshape.28.gain_ref
  1.4 1.2 copy-done
  2.6 1.3 norm.1
  3.9 0.8 copy-done.3
  4.7 0.5 collective-permute-start.2
  5.1 2.6 %collective-permute-start.1 = (bf16[32,8192]{1,0:T(8,128)(2,1)}, bf16[32,8192]{1,0:T(8,128)(2,1)S(1)}, u32[]{:S(2)}, u32[]{:S(2)}) collective-permute-start(bf16[32,8192]{1,0:T(8,128)(2,1)} %get-tuple-element.40), channel_id=1, source_target_pairs={{0,2},{1,3},{2,0},{3,1},{4,6},{5,7},{6,4},{7,5},{8,10},{9,11},{10,... | collective-permute-start | bytes 1572872 | tf_op jit(solution)/shard_map/ppermute | solution.py:302
  7.7 2.6 %collective-permute-start = (bf16[32,8192]{1,0:T(8,128)(2,1)}, bf16[32,8192]{1,0:T(8,128)(2,1)S(1)}, u32[]{:S(2)}, u32[]{:S(2)}) collective-permute-start(bf16[32,8192]{1,0:T(8,128)(2,1)} %get-tuple-element.40), channel_id=1, source_target_pairs={{0,4},{1,5},{2,6},{3,7},{4,0},{5,1},{6,2},{7,3},{8,12},{9,13},{10,... | collective-permute-start | bytes 1572872 | tf_op jit(solution)/shard_map/ppermute | solution.py:302
  10.3 0.8 dynamic-slice_convert_fusion
  11.0 0.1 reshape.31
  11.1 0.1 fusion.1
  11.2 0.7 reshape.29.refs_4_.refs_6_
  11.9 0.7 reshape.30.refs_5_.refs_7_
  12.6 0.1 reshape.32
  12.7 0.1 reshape.33
  12.7 0.1 maximum_bitcast_fusion
  12.8 1.0 fusion
  13.8 0.2 pad_maximum_fusion.1
  14.0 0.0 copy-start.4
  14.1 12.8 %wave0.1.refs_16_ = bf16[128,2048]{1,0:T(8,128)(2,1)S(1)} custom-call(bf16[64,8192]{1,0:T(8,128)(2,1)S(1)} %get-tuple-element.48.refs_0_, bf16[64,8192]{1,0:T(8,128)(2,1)S(1)} %collective-permute-done.2.refs_1_, bf16[8192,1024]{1,0:T(8,128)(2,1)} %refs_4_.5, bf16[8192,1024]{1,0:T(8,128)(2,1)} %refs_5_.5, bf16[1,1024]{1,0:T(2,128)(2,1)S(1)} %reshape.29.refs_4_.refs_6_, ...), custom_call_target="tpu_custom_call" | custom-call | flops 131072 | bytes 262144 | tf_op jit(solution)/shard_map/wave0/pallas_call | solution.py:217
  26.8 4.8 %collective-permute-done.1.refs_2_ = bf16[32,8192]{1,0:T(8,128)(2,1)S(1)} collective-permute-done((bf16[32,8192]{1,0:T(8,128)(2,1)}, bf16[32,8192]{1,0:T(8,128)(2,1)S(1)}, u32[]{:S(2)}, u32[]{:S(2)}) %collective-permute-start.1) | collective-permute-done | bytes 524320 | tf_op jit(solution)/shard_map/ppermute | solution.py:302
  31.6 2.6 %collective-permute-done.refs_0_ = bf16[32,8192]{1,0:T(8,128)(2,1)S(1)} collective-permute-done((bf16[32,8192]{1,0:T(8,128)(2,1)}, bf16[32,8192]{1,0:T(8,128)(2,1)S(1)}, u32[]{:S(2)}, u32[]{:S(2)}) %collective-permute-start) | collective-permute-done | bytes 524320 | tf_op jit(solution)/shard_map/ppermute | solution.py:302
  34.2 0.5 collective-permute-start.8
  34.7 0.4 collective-permute-start.7
  35.1 2.6 %collective-permute-start.6 = (bf16[32,8192]{1,0:T(8,128)(2,1)S(1)}, bf16[32,8192]{1,0:T(8,128)(2,1)S(1)}, u32[]{:S(2)}, u32[]{:S(2)}) collective-permute-start(bf16[32,8192]{1,0:T(8,128)(2,1)S(1)} %copy-done.4), channel_id=1, source_target_pairs={{0,4},{1,5},{2,6},{3,7},{4,0},{5,1},{6,2},{7,3},{8,12},{9,13},{10,... | collective-permute-start | bytes 1572872 | tf_op jit(solution)/shard_map/ppermute | solution.py:302
  37.7 2.4 %collective-permute-start.5 = (bf16[128,2048]{1,0:T(8,128)(2,1)S(1)}, bf16[128,2048]{1,0:T(8,128)(2,1)S(1)}, u32[]{:S(2)}, u32[]{:S(2)}) collective-permute-start(bf16[128,2048]{1,0:T(8,128)(2,1)S(1)} %wave0.1.refs_16_), channel_id=1, source_target_pairs={{0,24},{8,16},{16,8},{24,0},{1,25},{9,17},{17,9},{25,1},{2,26},{10... | collective-permute-start | bytes 1572872 | tf_op jit(solution)/shard_map/ppermute | solution.py:308
  40.1 0.5 collective-permute-start.4
  40.6 0.5 collective-permute-start.3
  41.2 12.9 %wave1.1.refs_20_ = bf16[128,2048]{1,0:T(8,128)(2,1)S(1)} custom-call(bf16[32,8192]{1,0:T(8,128)(2,1)S(1)} %collective-permute-done.refs_0_, bf16[32,8192]{1,0:T(8,128)(2,1)S(1)} %collective-permute-done.8.refs_1_, bf16[32,8192]{1,0:T(8,128)(2,1)S(1)} %collective-permute-done.1.refs_2_, bf16[32,8192]{1,0:T(8,128)(2,1)S(1)} %collective-permute-done.9.refs_3_, ...), custom_call_target="tpu_custom_call" | custom-call | flops 131072 | bytes 262144 | tf_op jit(solution)/shard_map/wave1/pallas_call | solution.py:217
  54.1 5.3 %collective-permute-done.7.refs_2_ = bf16[32,8192]{1,0:T(8,128)(2,1)S(1)} collective-permute-done((bf16[32,8192]{1,0:T(8,128)(2,1)S(1)}, bf16[32,8192]{1,0:T(8,128)(2,1)S(1)}, u32[]{:S(2)}, u32[]{:S(2)}) %collective-permute-start.7) | collective-permute-done | bytes 524320 | tf_op jit(solution)/shard_map/ppermute | solution.py:302
  59.5 1.4 collective-permute-done.6.refs_0_
  60.8 2.3 %collective-permute-done.4.refs_18_ = bf16[128,2048]{1,0:T(8,128)(2,1)S(1)} collective-permute-done((bf16[128,2048]{1,0:T(8,128)(2,1)S(1)}, bf16[128,2048]{1,0:T(8,128)(2,1)S(1)}, u32[]{:S(2)}, u32[]{:S(2)}) %collective-permute-start.4) | collective-permute-done | bytes 524320 | tf_op jit(solution)/shard_map/ppermute | solution.py:308
  63.1 0.1 collective-permute-done.3.refs_17_
  63.2 0.5 collective-permute-start.15
  63.7 0.1 pad_maximum_fusion
  63.8 0.4 collective-permute-start.14
  64.2 0.7 collective-permute-start.13
  64.9 1.7 %collective-permute-start.12 = (bf16[128,2048]{1,0:T(8,128)(2,1)S(1)}, bf16[128,2048]{1,0:T(8,128)(2,1)S(1)}, u32[]{:S(2)}, u32[]{:S(2)}) collective-permute-start(bf16[128,2048]{1,0:T(8,128)(2,1)S(1)} %wave1.1.refs_20_), channel_id=1, source_target_pairs={{0,24},{8,16},{16,8},{24,0},{1,25},{9,17},{17,9},{25,1},{2,26},{10... | collective-permute-start | bytes 1572872 | tf_op jit(solution)/shard_map/ppermute | solution.py:308
  66.6 1.3 collective-permute-start.11
  67.9 0.5 collective-permute-start.10
  68.5 12.8 %wave2.1 = (bf16[64,2048]{1,0:T(8,128)(2,1)S(1)}, bf16[64,2048]{1,0:T(8,128)(2,1)S(1)}) custom-call(bf16[32,8192]{1,0:T(8,128)(2,1)S(1)} %collective-permute-done.6.refs_0_, bf16[32,8192]{1,0:T(8,128)(2,1)S(1)} %collective-permute-done.15.refs_1_, bf16[32,8192]{1,0:T(8,128)(2,1)S(1)} %collective-permute-done.7.refs_2_, ...), custom_call_target="tpu_custom_call" | custom-call | flops 131072 | bytes 262144 | tf_op jit(solution)/shard_map/wave2/pallas_call | solution.py:217
  81.3 9.4 %collective-permute-done.11.refs_22_ = bf16[128,2048]{1,0:T(8,128)(2,1)S(1)} collective-permute-done((bf16[128,2048]{1,0:T(8,128)(2,1)S(1)}, bf16[128,2048]{1,0:T(8,128)(2,1)S(1)}, u32[]{:S(2)}, u32[]{:S(2)}) %collective-permute-start.11) | collective-permute-done | bytes 524320 | tf_op jit(solution)/shard_map/ppermute | solution.py:308
  90.7 0.0 collective-permute-done.10.refs_21_
  90.7 0.1 collective-permute-start.17
  90.8 0.5 collective-permute-start.18
  91.3 1.4 collective-permute-start.21
  92.7 0.8 collective-permute-start.19
  93.5 1.3 collective-permute-start.22
  94.8 0.5 collective-permute-start.20
  95.3 13.0 %wave3.1 = (bf16[64,2048]{1,0:T(8,128)(2,1)S(1)}, bf16[64,2048]{1,0:T(8,128)(2,1)S(1)}) custom-call(bf16[64,8192]{1,0:T(8,128)(2,1)S(1)} %collective-permute-done.13.refs_0_, bf16[64,8192]{1,0:T(8,128)(2,1)S(1)} %collective-permute-done.17.refs_1_, bf16[64,8192]{1,0:T(8,128)(2,1)S(1)} %collective-permute-done.14.refs_2_, ...), custom_call_target="tpu_custom_call" | custom-call | flops 131072 | bytes 262144 | tf_op jit(solution)/shard_map/wave3/pallas_call | solution.py:217
  108.4 1.5 %collective-permute-start.27 = (bf16[64,2048]{1,0:T(8,128)(2,1)S(1)}, bf16[64,2048]{1,0:T(8,128)(2,1)S(1)}, u32[]{:S(2)}, u32[]{:S(2)}) collective-permute-start(bf16[64,2048]{1,0:T(8,128)(2,1)S(1)} %collective-permute-done.19.refs_2_), channel_id=1, source_target_pairs={{0,16},{8,24},{16,0},{24,8},{1,17},{9,25},{17,1},{25,9},{2,18},{10... | collective-permute-start | bytes 786440 | tf_op jit(solution)/shard_map/ppermute | solution.py:308
  109.9 0.6 collective-permute-start.25
  110.5 1.5 %collective-permute-start.23 = (bf16[64,2048]{1,0:T(8,128)(2,1)S(1)}, bf16[64,2048]{1,0:T(8,128)(2,1)S(1)}, u32[]{:S(2)}, u32[]{:S(2)}) collective-permute-start(bf16[64,2048]{1,0:T(8,128)(2,1)S(1)} %get-tuple-element.64.refs_8_), channel_id=1, source_target_pairs={{0,8},{8,0},{16,24},{24,16},{1,9},{9,1},{17,25},{25,17},{2,10},{10... | collective-permute-start | bytes 786440 | tf_op jit(solution)/shard_map/ppermute | solution.py:308
  112.0 0.5 collective-permute-start.28
  112.5 1.4 collective-permute-start.26
  114.0 3.7 %collective-permute-done.27.refs_6_ = bf16[64,2048]{1,0:T(8,128)(2,1)S(1)} collective-permute-done((bf16[64,2048]{1,0:T(8,128)(2,1)S(1)}, bf16[64,2048]{1,0:T(8,128)(2,1)S(1)}, u32[]{:S(2)}, u32[]{:S(2)}) %collective-permute-start.27) | collective-permute-done | bytes 262176 | tf_op jit(solution)/shard_map/ppermute | solution.py:308
  117.7 1.5 %collective-permute-start.24 = (bf16[64,2048]{1,0:T(8,128)(2,1)S(1)}, bf16[64,2048]{1,0:T(8,128)(2,1)S(1)}, u32[]{:S(2)}, u32[]{:S(2)}) collective-permute-start(bf16[64,2048]{1,0:T(8,128)(2,1)S(1)} %get-tuple-element.65.refs_9_), channel_id=1, source_target_pairs={{0,8},{8,0},{16,24},{24,16},{1,9},{9,1},{17,25},{25,17},{2,10},{10... | collective-permute-start | bytes 786440 | tf_op jit(solution)/shard_map/ppermute | solution.py:308
  119.2 6.2 %collective-permute-done.28.refs_7_ = bf16[64,2048]{1,0:T(8,128)(2,1)S(1)} collective-permute-done((bf16[64,2048]{1,0:T(8,128)(2,1)S(1)}, bf16[64,2048]{1,0:T(8,128)(2,1)S(1)}, u32[]{:S(2)}, u32[]{:S(2)}) %collective-permute-start.28) | collective-permute-done | bytes 262176 | tf_op jit(solution)/shard_map/ppermute | solution.py:308
  125.4 2.3 %collective-permute-done.26.refs_13_ = bf16[64,2048]{1,0:T(8,128)(2,1)S(1)} collective-permute-done((bf16[64,2048]{1,0:T(8,128)(2,1)S(1)}, bf16[64,2048]{1,0:T(8,128)(2,1)S(1)}, u32[]{:S(2)}, u32[]{:S(2)}) %collective-permute-start.26) | collective-permute-done | bytes 262176 | tf_op jit(solution)/shard_map/ppermute | solution.py:308
  127.7 1.5 %collective-permute-done.24.refs_11_ = bf16[64,2048]{1,0:T(8,128)(2,1)S(1)} collective-permute-done((bf16[64,2048]{1,0:T(8,128)(2,1)S(1)}, bf16[64,2048]{1,0:T(8,128)(2,1)S(1)}, u32[]{:S(2)}, u32[]{:S(2)}) %collective-permute-start.24) | collective-permute-done | bytes 262176 | tf_op jit(solution)/shard_map/ppermute | solution.py:308
  129.1 1.4 collective-permute-start.29
  130.6 0.8 collective-permute-start.30
  131.3 4.2 %collective-permute-done.29.refs_14_ = bf16[64,2048]{1,0:T(8,128)(2,1)S(1)} collective-permute-done((bf16[64,2048]{1,0:T(8,128)(2,1)S(1)}, bf16[64,2048]{1,0:T(8,128)(2,1)S(1)}, u32[]{:S(2)}, u32[]{:S(2)}) %collective-permute-start.29) | collective-permute-done | bytes 262176 | tf_op jit(solution)/shard_map/ppermute | solution.py:308
  135.6 1.4 collective-permute-done.30.refs_15_
  136.9 7.2 %place.1 = (bf16[1024,1024]{1,0:T(8,128)(2,1)}, bf16[1024,1024]{1,0:T(8,128)(2,1)}) custom-call(s32[16]{0:T(128)S(1)} %copy-done.1, s32[16]{0:T(128)S(1)} %copy-done.2, bf16[64,2048]{1,0:T(8,128)(2,1)S(1)} %get-tuple-element.54.refs_0_, bf16[64,2048]{1,0:T(8,128)(2,1)S(1)} %get-tuple-element.55.refs_1_, ...), custom_call_target="tpu_custom_call" | custom-call | bytes 20971520 | tf_op jit(solution)/shard_map/place/pallas_call | solution.py:285
  (27 shorter events, 0.1 us)
Async XLA Ops:
  1.4 1.2 copy-start
  3.9 0.8 copy-start.3
  4.7 9.4 %collective-permute-start.2 = (bf16[64,8192]{1,0:T(8,128)(2,1)S(1)}, bf16[64,8192]{1,0:T(8,128)(2,1)S(1)}, u32[]{:S(2)}, u32[]{:S(2)}) collective-permute-start(bf16[64,8192]{1,0:T(8,128)(2,1)S(1)} %get-tuple-element.48.refs_0_), channel_id=1, source_target_pairs={{0,1},{1,0},{2,3},{3,2},{4,5},{5,4},{6,7},{7,6},{8,9},{9,8},{10,11... | collective-permute-start | bytes 3145736 | tf_op jit(solution)/shard_map/ppermute | solution.py:305
  5.1 26.5 %collective-permute-start.1 = (bf16[32,8192]{1,0:T(8,128)(2,1)}, bf16[32,8192]{1,0:T(8,128)(2,1)S(1)}, u32[]{:S(2)}, u32[]{:S(2)}) collective-permute-start(bf16[32,8192]{1,0:T(8,128)(2,1)} %get-tuple-element.40), channel_id=1, source_target_pairs={{0,2},{1,3},{2,0},{3,1},{4,6},{5,7},{6,4},{7,5},{8,10},{9,11},{10,... | collective-permute-start | bytes 1572872 | tf_op jit(solution)/shard_map/ppermute | solution.py:302
  7.7 26.5 %collective-permute-start = (bf16[32,8192]{1,0:T(8,128)(2,1)}, bf16[32,8192]{1,0:T(8,128)(2,1)S(1)}, u32[]{:S(2)}, u32[]{:S(2)}) collective-permute-start(bf16[32,8192]{1,0:T(8,128)(2,1)} %get-tuple-element.40), channel_id=1, source_target_pairs={{0,4},{1,5},{2,6},{3,7},{4,0},{5,1},{6,2},{7,3},{8,12},{9,13},{10,... | collective-permute-start | bytes 1572872 | tf_op jit(solution)/shard_map/ppermute | solution.py:302
  14.0 20.6 %copy-start.4 = (bf16[32,8192]{1,0:T(8,128)(2,1)S(1)}, bf16[32,8192]{1,0:T(8,128)(2,1)}, u32[]{:S(2)}) copy-start(bf16[32,8192]{1,0:T(8,128)(2,1)} %copy-done.3) | copy-start | bytes 1572868
  34.1 6.0 %collective-permute-start.9 = (bf16[32,8192]{1,0:T(8,128)(2,1)S(1)}, bf16[32,8192]{1,0:T(8,128)(2,1)S(1)}, u32[]{:S(2)}, u32[]{:S(2)}) collective-permute-start(bf16[32,8192]{1,0:T(8,128)(2,1)S(1)} %collective-permute-done.1.refs_2_), channel_id=1, source_target_pairs={{0,1},{1,0},{2,3},{3,2},{4,5},{5,4},{6,7},{7,6},{8,9},{9,8},{10,11... | collective-permute-start | bytes 1572872 | tf_op jit(solution)/shard_map/ppermute | solution.py:305
  34.2 6.5 %collective-permute-start.8 = (bf16[32,8192]{1,0:T(8,128)(2,1)S(1)}, bf16[32,8192]{1,0:T(8,128)(2,1)S(1)}, u32[]{:S(2)}, u32[]{:S(2)}) collective-permute-start(bf16[32,8192]{1,0:T(8,128)(2,1)S(1)} %collective-permute-done.refs_0_), channel_id=1, source_target_pairs={{0,1},{1,0},{2,3},{3,2},{4,5},{5,4},{6,7},{7,6},{8,9},{9,8},{10,11... | collective-permute-start | bytes 1572872 | tf_op jit(solution)/shard_map/ppermute | solution.py:305
  34.7 24.8 %collective-permute-start.7 = (bf16[32,8192]{1,0:T(8,128)(2,1)S(1)}, bf16[32,8192]{1,0:T(8,128)(2,1)S(1)}, u32[]{:S(2)}, u32[]{:S(2)}) collective-permute-start(bf16[32,8192]{1,0:T(8,128)(2,1)S(1)} %copy-done.4), channel_id=1, source_target_pairs={{0,2},{1,3},{2,0},{3,1},{4,6},{5,7},{6,4},{7,5},{8,10},{9,11},{10,... | collective-permute-start | bytes 1572872 | tf_op jit(solution)/shard_map/ppermute | solution.py:302
  35.1 25.7 %collective-permute-start.6 = (bf16[32,8192]{1,0:T(8,128)(2,1)S(1)}, bf16[32,8192]{1,0:T(8,128)(2,1)S(1)}, u32[]{:S(2)}, u32[]{:S(2)}) collective-permute-start(bf16[32,8192]{1,0:T(8,128)(2,1)S(1)} %copy-done.4), channel_id=1, source_target_pairs={{0,4},{1,5},{2,6},{3,7},{4,0},{5,1},{6,2},{7,3},{8,12},{9,13},{10,... | collective-permute-start | bytes 1572872 | tf_op jit(solution)/shard_map/ppermute | solution.py:302
  37.7 23.1 %collective-permute-start.5 = (bf16[128,2048]{1,0:T(8,128)(2,1)S(1)}, bf16[128,2048]{1,0:T(8,128)(2,1)S(1)}, u32[]{:S(2)}, u32[]{:S(2)}) collective-permute-start(bf16[128,2048]{1,0:T(8,128)(2,1)S(1)} %wave0.1.refs_16_), channel_id=1, source_target_pairs={{0,24},{8,16},{16,8},{24,0},{1,25},{9,17},{17,9},{25,1},{2,26},{10... | collective-permute-start | bytes 1572872 | tf_op jit(solution)/shard_map/ppermute | solution.py:308
  40.1 23.0 %collective-permute-start.4 = (bf16[128,2048]{1,0:T(8,128)(2,1)S(1)}, bf16[128,2048]{1,0:T(8,128)(2,1)S(1)}, u32[]{:S(2)}, u32[]{:S(2)}) collective-permute-start(bf16[128,2048]{1,0:T(8,128)(2,1)S(1)} %wave0.1.refs_16_), channel_id=1, source_target_pairs={{0,16},{8,24},{16,0},{24,8},{1,17},{9,25},{17,1},{25,9},{2,18},{10... | collective-permute-start | bytes 1572872 | tf_op jit(solution)/shard_map/ppermute | solution.py:308
  40.6 22.5 %collective-permute-start.3 = (bf16[128,2048]{1,0:T(8,128)(2,1)S(1)}, bf16[128,2048]{1,0:T(8,128)(2,1)S(1)}, u32[]{:S(2)}, u32[]{:S(2)}) collective-permute-start(bf16[128,2048]{1,0:T(8,128)(2,1)S(1)} %wave0.1.refs_16_), channel_id=1, source_target_pairs={{0,8},{8,0},{16,24},{24,16},{1,9},{9,1},{17,25},{25,17},{2,10},{10... | collective-permute-start | bytes 1572872 | tf_op jit(solution)/shard_map/ppermute | solution.py:308
  63.2 3.4 %collective-permute-start.16 = (bf16[32,8192]{1,0:T(8,128)(2,1)S(1)}, bf16[32,8192]{1,0:T(8,128)(2,1)S(1)}, u32[]{:S(2)}, u32[]{:S(2)}) collective-permute-start(bf16[32,8192]{1,0:T(8,128)(2,1)S(1)} %collective-permute-done.7.refs_2_), channel_id=1, source_target_pairs={{0,1},{1,0},{2,3},{3,2},{4,5},{5,4},{6,7},{7,6},{8,9},{9,8},{10,11... | collective-permute-start | bytes 1572872 | tf_op jit(solution)/shard_map/ppermute | solution.py:305
  63.2 4.7 %collective-permute-start.15 = (bf16[32,8192]{1,0:T(8,128)(2,1)S(1)}, bf16[32,8192]{1,0:T(8,128)(2,1)S(1)}, u32[]{:S(2)}, u32[]{:S(2)}) collective-permute-start(bf16[32,8192]{1,0:T(8,128)(2,1)S(1)} %collective-permute-done.6.refs_0_), channel_id=1, source_target_pairs={{0,1},{1,0},{2,3},{3,2},{4,5},{5,4},{6,7},{7,6},{8,9},{9,8},{10,11... | collective-permute-start | bytes 1572872 | tf_op jit(solution)/shard_map/ppermute | solution.py:305
  63.8 26.9 %collective-permute-start.14 = (bf16[64,8192]{1,0:T(8,128)(2,1)S(1)}, bf16[64,8192]{1,0:T(8,128)(2,1)S(1)}, u32[]{:S(2)}, u32[]{:S(2)}) collective-permute-start(bf16[64,8192]{1,0:T(8,128)(2,1)S(1)} %pad_maximum_fusion), channel_id=1, source_target_pairs={{0,2},{1,3},{2,0},{3,1},{4,6},{5,7},{6,4},{7,5},{8,10},{9,11},{10,... | collective-permute-start | bytes 3145736 | tf_op jit(solution)/shard_map/ppermute | solution.py:302
  64.2 26.5 %collective-permute-start.13 = (bf16[64,8192]{1,0:T(8,128)(2,1)S(1)}, bf16[64,8192]{1,0:T(8,128)(2,1)S(1)}, u32[]{:S(2)}, u32[]{:S(2)}) collective-permute-start(bf16[64,8192]{1,0:T(8,128)(2,1)S(1)} %get-tuple-element.48.refs_0_), channel_id=1, source_target_pairs={{2,4},{3,5},{4,2},{5,3},{10,12},{11,13},{12,10},{13,11},{18,20},{1... | collective-permute-start | bytes 3145736 | tf_op jit(solution)/shard_map/ppermute | solution.py:302
  64.9 16.3 %collective-permute-start.12 = (bf16[128,2048]{1,0:T(8,128)(2,1)S(1)}, bf16[128,2048]{1,0:T(8,128)(2,1)S(1)}, u32[]{:S(2)}, u32[]{:S(2)}) collective-permute-start(bf16[128,2048]{1,0:T(8,128)(2,1)S(1)} %wave1.1.refs_20_), channel_id=1, source_target_pairs={{0,24},{8,16},{16,8},{24,0},{1,25},{9,17},{17,9},{25,1},{2,26},{10... | collective-permute-start | bytes 1572872 | tf_op jit(solution)/shard_map/ppermute | solution.py:308
  66.6 24.0 %collective-permute-start.11 = (bf16[128,2048]{1,0:T(8,128)(2,1)S(1)}, bf16[128,2048]{1,0:T(8,128)(2,1)S(1)}, u32[]{:S(2)}, u32[]{:S(2)}) collective-permute-start(bf16[128,2048]{1,0:T(8,128)(2,1)S(1)} %wave1.1.refs_20_), channel_id=1, source_target_pairs={{0,16},{8,24},{16,0},{24,8},{1,17},{9,25},{17,1},{25,9},{2,18},{10... | collective-permute-start | bytes 1572872 | tf_op jit(solution)/shard_map/ppermute | solution.py:308
  67.9 22.7 %collective-permute-start.10 = (bf16[128,2048]{1,0:T(8,128)(2,1)S(1)}, bf16[128,2048]{1,0:T(8,128)(2,1)S(1)}, u32[]{:S(2)}, u32[]{:S(2)}) collective-permute-start(bf16[128,2048]{1,0:T(8,128)(2,1)S(1)} %wave1.1.refs_20_), channel_id=1, source_target_pairs={{0,8},{8,0},{16,24},{24,16},{1,9},{9,1},{17,25},{25,17},{2,10},{10... | collective-permute-start | bytes 1572872 | tf_op jit(solution)/shard_map/ppermute | solution.py:308
  90.7 46.2 %copy-start.1 = (s32[16]{0:T(128)S(1)}, s32[16]{0:T(128)}, u32[]{:S(2)}) copy-start(s32[16]{0:T(128)} %lengths.1) | copy-start | bytes 196
  90.7 46.2 %copy-start.2 = (s32[16]{0:T(128)S(1)}, s32[16]{0:T(128)}, u32[]{:S(2)}) copy-start(s32[16]{0:T(128)} %owner.1) | copy-start | bytes 196
  90.7 4.1 %collective-permute-start.17 = (bf16[64,8192]{1,0:T(8,128)(2,1)S(1)}, bf16[64,8192]{1,0:T(8,128)(2,1)S(1)}, u32[]{:S(2)}, u32[]{:S(2)}) collective-permute-start(bf16[64,8192]{1,0:T(8,128)(2,1)S(1)} %collective-permute-done.13.refs_0_), channel_id=1, source_target_pairs={{0,1},{1,0},{2,3},{3,2},{4,5},{5,4},{6,7},{7,6},{8,9},{9,8},{10,11... | collective-permute-start | bytes 3145736 | tf_op jit(solution)/shard_map/ppermute | solution.py:305
  90.8 4.6 %collective-permute-start.18 = (bf16[64,8192]{1,0:T(8,128)(2,1)S(1)}, bf16[64,8192]{1,0:T(8,128)(2,1)S(1)}, u32[]{:S(2)}, u32[]{:S(2)}) collective-permute-start(bf16[64,8192]{1,0:T(8,128)(2,1)S(1)} %collective-permute-done.14.refs_2_), channel_id=1, source_target_pairs={{0,1},{1,0},{2,3},{3,2},{4,5},{5,4},{6,7},{7,6},{8,9},{9,8},{10,11... | collective-permute-start | bytes 3145736 | tf_op jit(solution)/shard_map/ppermute | solution.py:305
  91.3 17.1 %collective-permute-start.21 = (bf16[64,2048]{1,0:T(8,128)(2,1)S(1)}, bf16[64,2048]{1,0:T(8,128)(2,1)S(1)}, u32[]{:S(2)}, u32[]{:S(2)}) collective-permute-start(bf16[64,2048]{1,0:T(8,128)(2,1)S(1)} %get-tuple-element.54.refs_0_), channel_id=1, source_target_pairs={{0,16},{8,24},{16,0},{24,8},{1,17},{9,25},{17,1},{25,9},{2,18},{10... | collective-permute-start | bytes 786440 | tf_op jit(solution)/shard_map/ppermute | solution.py:308
  92.7 15.7 %collective-permute-start.19 = (bf16[64,2048]{1,0:T(8,128)(2,1)S(1)}, bf16[64,2048]{1,0:T(8,128)(2,1)S(1)}, u32[]{:S(2)}, u32[]{:S(2)}) collective-permute-start(bf16[64,2048]{1,0:T(8,128)(2,1)S(1)} %get-tuple-element.54.refs_0_), channel_id=1, source_target_pairs={{0,8},{8,0},{16,24},{24,16},{1,9},{9,1},{17,25},{25,17},{2,10},{10... | collective-permute-start | bytes 786440 | tf_op jit(solution)/shard_map/ppermute | solution.py:308
  93.5 14.9 %collective-permute-start.22 = (bf16[64,2048]{1,0:T(8,128)(2,1)S(1)}, bf16[64,2048]{1,0:T(8,128)(2,1)S(1)}, u32[]{:S(2)}, u32[]{:S(2)}) collective-permute-start(bf16[64,2048]{1,0:T(8,128)(2,1)S(1)} %get-tuple-element.55.refs_1_), channel_id=1, source_target_pairs={{0,16},{8,24},{16,0},{24,8},{1,17},{9,25},{17,1},{25,9},{2,18},{10... | collective-permute-start | bytes 786440 | tf_op jit(solution)/shard_map/ppermute | solution.py:308
  94.8 13.6 %collective-permute-start.20 = (bf16[64,2048]{1,0:T(8,128)(2,1)S(1)}, bf16[64,2048]{1,0:T(8,128)(2,1)S(1)}, u32[]{:S(2)}, u32[]{:S(2)}) collective-permute-start(bf16[64,2048]{1,0:T(8,128)(2,1)S(1)} %get-tuple-element.55.refs_1_), channel_id=1, source_target_pairs={{0,8},{8,0},{16,24},{24,16},{1,9},{9,1},{17,25},{25,17},{2,10},{10... | collective-permute-start | bytes 786440 | tf_op jit(solution)/shard_map/ppermute | solution.py:308
  108.4 9.3 %collective-permute-start.27 = (bf16[64,2048]{1,0:T(8,128)(2,1)S(1)}, bf16[64,2048]{1,0:T(8,128)(2,1)S(1)}, u32[]{:S(2)}, u32[]{:S(2)}) collective-permute-start(bf16[64,2048]{1,0:T(8,128)(2,1)S(1)} %collective-permute-done.19.refs_2_), channel_id=1, source_target_pairs={{0,16},{8,24},{16,0},{24,8},{1,17},{9,25},{17,1},{25,9},{2,18},{10... | collective-permute-start | bytes 786440 | tf_op jit(solution)/shard_map/ppermute | solution.py:308
  109.9 15.5 %collective-permute-start.25 = (bf16[64,2048]{1,0:T(8,128)(2,1)S(1)}, bf16[64,2048]{1,0:T(8,128)(2,1)S(1)}, u32[]{:S(2)}, u32[]{:S(2)}) collective-permute-start(bf16[64,2048]{1,0:T(8,128)(2,1)S(1)} %get-tuple-element.64.refs_8_), channel_id=1, source_target_pairs={{0,16},{8,24},{16,0},{24,8},{1,17},{9,25},{17,1},{25,9},{2,18},{10... | collective-permute-start | bytes 786440 | tf_op jit(solution)/shard_map/ppermute | solution.py:308
  110.5 14.9 %collective-permute-start.23 = (bf16[64,2048]{1,0:T(8,128)(2,1)S(1)}, bf16[64,2048]{1,0:T(8,128)(2,1)S(1)}, u32[]{:S(2)}, u32[]{:S(2)}) collective-permute-start(bf16[64,2048]{1,0:T(8,128)(2,1)S(1)} %get-tuple-element.64.refs_8_), channel_id=1, source_target_pairs={{0,8},{8,0},{16,24},{24,16},{1,9},{9,1},{17,25},{25,17},{2,10},{10... | collective-permute-start | bytes 786440 | tf_op jit(solution)/shard_map/ppermute | solution.py:308
  112.0 13.4 %collective-permute-start.28 = (bf16[64,2048]{1,0:T(8,128)(2,1)S(1)}, bf16[64,2048]{1,0:T(8,128)(2,1)S(1)}, u32[]{:S(2)}, u32[]{:S(2)}) collective-permute-start(bf16[64,2048]{1,0:T(8,128)(2,1)S(1)} %collective-permute-done.22.refs_5_), channel_id=1, source_target_pairs={{0,8},{8,0},{16,24},{24,16},{1,9},{9,1},{17,25},{25,17},{2,10},{10... | collective-permute-start | bytes 786440 | tf_op jit(solution)/shard_map/ppermute | solution.py:308
  112.5 15.1 %collective-permute-start.26 = (bf16[64,2048]{1,0:T(8,128)(2,1)S(1)}, bf16[64,2048]{1,0:T(8,128)(2,1)S(1)}, u32[]{:S(2)}, u32[]{:S(2)}) collective-permute-start(bf16[64,2048]{1,0:T(8,128)(2,1)S(1)} %get-tuple-element.65.refs_9_), channel_id=1, source_target_pairs={{0,16},{8,24},{16,0},{24,8},{1,17},{9,25},{17,1},{25,9},{2,18},{10... | collective-permute-start | bytes 786440 | tf_op jit(solution)/shard_map/ppermute | solution.py:308
  117.7 11.4 %collective-permute-start.24 = (bf16[64,2048]{1,0:T(8,128)(2,1)S(1)}, bf16[64,2048]{1,0:T(8,128)(2,1)S(1)}, u32[]{:S(2)}, u32[]{:S(2)}) collective-permute-start(bf16[64,2048]{1,0:T(8,128)(2,1)S(1)} %get-tuple-element.65.refs_9_), channel_id=1, source_target_pairs={{0,8},{8,0},{16,24},{24,16},{1,9},{9,1},{17,25},{25,17},{2,10},{10... | collective-permute-start | bytes 786440 | tf_op jit(solution)/shard_map/ppermute | solution.py:308
  129.1 6.4 %collective-permute-start.29 = (bf16[64,2048]{1,0:T(8,128)(2,1)S(1)}, bf16[64,2048]{1,0:T(8,128)(2,1)S(1)}, u32[]{:S(2)}, u32[]{:S(2)}) collective-permute-start(bf16[64,2048]{1,0:T(8,128)(2,1)S(1)} %collective-permute-done.23.refs_10_), channel_id=1, source_target_pairs={{0,16},{8,24},{16,0},{24,8},{1,17},{9,25},{17,1},{25,9},{2,18},{10... | collective-permute-start | bytes 786440 | tf_op jit(solution)/shard_map/ppermute | solution.py:308
  130.6 6.4 %collective-permute-start.30 = (bf16[64,2048]{1,0:T(8,128)(2,1)S(1)}, bf16[64,2048]{1,0:T(8,128)(2,1)S(1)}, u32[]{:S(2)}, u32[]{:S(2)}) collective-permute-start(bf16[64,2048]{1,0:T(8,128)(2,1)S(1)} %collective-permute-done.26.refs_13_), channel_id=1, source_target_pairs={{0,8},{8,0},{16,24},{24,16},{1,9},{9,1},{17,25},{25,17},{2,10},{10... | collective-permute-start | bytes 786440 | tf_op jit(solution)/shard_map/ppermute | solution.py:308

commit v3 on v2

--- a/solution.py
+++ b/solution.py
@@ -76,8 +76,9 @@
     gain = gain_ref[...].astype(F32)
     for at in range(0, x_ref.shape[0], step):
         x = x_ref[at : at + step, :].astype(F32)
-        scale = lax.rsqrt(jnp.mean(x * x, axis=1, keepdims=True) + 1e-06)
-        y = (x * scale * gain).astype(BF)
+        x = x * lax.rsqrt(jnp.mean(x * x, axis=1, keepdims=True) + 1e-06)
+        y = [x[:, i * HD : (i + 1) * HD] * gain[i : i + 1, :] for i in range(gain.shape[0])]
+        y = jnp.concatenate(y, axis=1).astype(BF)
         out_ref[at : at + step, :] = y
         if at < first:
             lo_ref[at : at + step, :] = y
@@ -93,7 +94,7 @@
         name="norm",
         cost_estimate=pl.CostEstimate(flops=rows * wide, bytes_accessed=rows, transcendentals=rows),
         compiler_params=pltpu.CompilerParams(vmem_limit_bytes=16 * MIB),
-    )(hidden, gain.reshape(1, wide))
+    )(hidden, gain.reshape(wide // HD, HD))
 
 
 PART = (32, 32)
@@ -142,27 +143,46 @@
     return [(own, sib, 0), (own, sib, PART[0])]
 
 
-def wave_kernel(pieces, kind, count, *refs):
+def wave_kernel(pieces, kind, mode, count, *refs):
     sources = refs[:count]
     wk, wv, kb, vb, cos, sin = refs[count : count + 6]
-    outs, x, blocks, sem, wsem = refs[count + 6 : -4], *refs[-4:]
+    outs, x, sem, scratch = list(refs[count + 6 :]), None, None, []
+    if mode == "use":
+        x, sem = outs[-2:]
+        outs = outs[:-2]
+        kept = (wk, wv)
+    elif mode == "keep":
+        x, sem, wsem = outs[-3:]
+        kept = outs[-5:-3]
+        outs = outs[:-5]
+    else:
+        x, sem, wsem, blocks = outs[-4:]
+        outs = outs[:-4]
     deep, width = wk.shape
-    depth, _, tile = blocks.shape
+    tile = 256
     each = width // tile
+    total = 2 * each
     half = deep // 2
+
+    def block(i):
+        if mode == "stream":
+            return blocks.at[i % blocks.shape[0]]
+        return kept[i // each].at[:, pl.ds(i % each * tile, tile)]
+
     copies = []
-    for i in range(2 * each):
-        cols = pl.ds(i % each * tile, tile)
-        copies.append(
-            [
-                pltpu.make_async_copy(
-                    (wk, wv)[i // each].at[pl.ds(j * half, half), cols],
-                    blocks.at[i % depth, pl.ds(j * half, half)],
-                    wsem.at[2 * i + j],
-                )
-                for j in range(2)
-            ]
-        )
+    if mode != "use":
+        for i in range(total):
+            cols = pl.ds(i % each * tile, tile)
+            copies.append(
+                [
+                    pltpu.make_async_copy(
+                        (wk, wv)[i // each].at[pl.ds(j * half, half), cols],
+                        block(i).at[pl.ds(j * half, half)],
+                        wsem.at[2 * i + j],
+                    )
+                    for j in range(2)
+                ]
+            )
 
     def fetch(i):
         for copy in copies[i]:
@@ -179,25 +199,29 @@
     else:
         rows = both(*sources) if kind == "whole" else [(sources[i], sources[i + 1], 0) for i in range(0, count, 2)]
         load(rows, sem, wait=False)
-    for i in range(depth):
+    ahead = {"use": 0, "keep": total, "stream": DEPTH}[mode]
+    for i in range(ahead):
         fetch(i)
     c, s = rotation(pieces, cos, sin)
     load(rows, sem, start=False)
     part = x.shape[0] // len(outs)
-    for i in range(2 * each):
-        for copy in copies[i]:
-            copy.wait()
-        raw = jnp.dot(x[...], blocks[i % depth], preferred_element_type=F32)
+    for i in range(total):
+        if copies:
+            for copy in copies[i]:
+                copy.wait()
+        raw = jnp.dot(x[...], block(i)[...], preferred_element_type=F32)
         if i < each:
             y = turn(raw + kb[:, i * tile : (i + 1) * tile].astype(F32), c, s)
         else:
             at = (i - each) * tile
             y = (raw + vb[:, at : at + tile].astype(F32)).astype(BF)
         for k, out in enumerate(outs):
-            for j in range(out.shape[0] // part):
-                out[j * part : (j + 1) * part, i * tile : (i + 1) * tile] = y[k * part : (k + 1) * part]
-        if i + depth < 2 * each:
-            fetch(i + depth)
+            out[:, i * tile : (i + 1) * tile] = y[k * part : (k + 1) * part]
+        if mode == "stream" and i + DEPTH < total:
+            fetch(i + DEPTH)
+
+
+DEPTH = 3
 
 
 def cost(m, deep, width, weights):
@@ -208,26 +232,29 @@
     return pltpu.with_memory_space_constraint(x, pltpu.HBM)
 
 
-def wave(name, pieces, kind, sources, wk, wv, rest, split=1, copies=1):
+def wave(name, pieces, kind, sources, wk, wv, rest, split=1, mode="stream"):
     deep, width = wk.shape
     m = sum(2 * PART[part] for _, part in pieces)
-    tile, depth = 256, 3
+    tile = 256
     full = pl.BlockSpec(memory_space=VMEM)
     hbm = pl.BlockSpec(memory_space=ANY)
+    scratch = [VMEM((m, deep), BF), pltpu.SemaphoreType.DMA((2 * len(pieces),))]
+    outs = [VMEM((m // split, 2 * width), BF)] * split
+    if mode != "use":
+        scratch.append(pltpu.SemaphoreType.DMA((4 * width // tile,)))
+    if mode == "stream":
+        scratch.append(VMEM((DEPTH, deep, tile), BF))
+    if mode == "keep":
+        outs += [VMEM((deep, width), BF)] * 2
     return pl.pallas_call(
-        functools.partial(wave_kernel, pieces, kind, len(sources)),
-        out_shape=[VMEM((copies * m // split, 2 * width), BF)] * split,
-        in_specs=[hbm] * (len(sources) + 2) + [full] * 4,
-        out_specs=[full] * split,
-        scratch_shapes=[
-            VMEM((m, deep), BF),
-            VMEM((depth, deep, tile), BF),
-            pltpu.SemaphoreType.DMA((2 * len(pieces),)),
-            pltpu.SemaphoreType.DMA((4 * width // tile,)),
-        ],
+        functools.partial(wave_kernel, pieces, kind, mode, len(sources)),
+        out_shape=outs,
+        in_specs=[hbm] * len(sources) + [full if mode == "use" else hbm] * 2 + [full] * 4,
+        out_specs=[full] * len(outs),
+        scratch_shapes=scratch,
         name=name,
         cost_estimate=cost(m, deep, width, True),
-        compiler_params=pltpu.CompilerParams(vmem_limit_bytes=24 * MIB),
+        compiler_params=pltpu.CompilerParams(vmem_limit_bytes=(18 if mode == "stream" else 6) * MIB),
     )(*sources, wk, wv, *rest)
 
 
@@ -330,34 +357,33 @@
     rest = (k_bias.reshape(1, width), v_bias.reshape(1, width), cos, sin)
 
     wk, wv = in_hbm(k_weight), in_hbm(v_weight)
+    kk, kv = (pltpu.with_memory_space_constraint(w, VMEM) for w in (k_weight, v_weight))
     together = lax.optimization_barrier
-
-    def to_all(p):
-        return [across(p, d) for d in (1, 2, 3)]
-
     (p0,) = wave("wave0", WHOLE, "whole", [own, own_s], wk, wv, rest)
-    far1, near1, p0, lo, hi = together((far1, near1, p0, lo, hi))
-
-    a0 = to_all(p0)
+    far1, near1, p0, lo, hi, own = together((far1, near1, p0, lo, hi, own))
+
     far2, near2 = line(hi, far_pairs), line(hi, near_pairs)
+    x0, y0 = across(p0, 1), across(p0, 2)
     pieces1 = [(2, 0), (1, 0)]
-    (p1,) = wave("wave1", pieces1, "pieces", [far1, sibling(far1), near1, sibling(near1)], wk, wv, rest)
-    a0, far1, far2, near2, p1, own = together((a0, far1, far2, near2, p1, own))
-
-    a1 = to_all(p1)
+    (p1,) = wave("wave1", pieces1, "pieces", [far1, sibling(far1), near1, sibling(near1)], kk, kv, rest, 1, "use")
+    p1, x0, y0 = together((p1, x0, y0))
+    x1, y1 = across(p1, 1), across(p1, 2)
+    x0, x1, y1, far1, far2, near2, p1, own = together((x0, x1, y1, far1, far2, near2, p1, own))
+
     middle, relay = line(own, middle_pairs), line(jnp.concatenate([far1, far2]), near_pairs)
+    d0, d1 = across(x0, 2), across(y1, 1)
     pieces2 = [(2, 1), (1, 1)]
-    p2 = wave("wave2", pieces2, "pieces", [far2, sibling(far2), near2, sibling(near2)], wk, wv, rest, 2)
-    a1, middle, relay, p2 = together((a1, middle, relay, p2))
-
+    p2 = wave("wave2", pieces2, "pieces", [far2, sibling(far2), near2, sibling(near2)], kk, kv, rest, 2, "use")
+    d0, d1, *p2 = together((d0, d1, *p2))
     x2, y2 = [across(p, 1) for p in p2], [across(p, 2) for p in p2]
+    x2, y2, middle, relay = together((x2, y2, middle, relay))
+
+    d2 = [across(x2[0], 2), across(y2[1], 1)]
     sources = [middle, sibling(middle), relay, sibling(relay)]
     pieces3 = [(3, 0), (3, 1)]
-    p3 = wave("wave3", pieces3, "relayed", sources, wk, wv, rest, 2)
-    p3, x2, y2 = together((p3, x2, y2))
+    p3 = wave("wave3", pieces3, "relayed", sources, kk, kv, rest, 2, "use")
+    p3, d2 = together((p3, d2))
     x3, y3 = [across(p, 1) for p in p3], [across(p, 2) for p in p3]
-    d2 = [across(x2[0], 2), across(y2[1], 1)]
-    x3, y3, d2 = together((x3, y3, d2))
     d3 = [across(x3[0], 2), across(y3[1], 1)]
 
     units, arrays = [], []
@@ -377,10 +403,10 @@
                 row += done
             arrays.extend(parts)
 
+    arrived(WHOLE, 1, [[one] for one in (p0, x0, y0, d0)])
+    arrived(pieces1, 1, [[one] for one in (p1, x1, y1, d1)])
     arrived(pieces2, 2, (p2, x2, y2, d2))
     arrived(pieces3, 2, (p3, x3, y3, d3))
-    arrived(WHOLE, 1, [[one] for one in (p0, *a0)])
-    arrived(pieces1, 1, [[one] for one in (p1, *a1)])
     return place(units, arrays, lengths, owner, 1024, width, 2048)
 
 

time: 144 us -> 131 us (0.910)
  Pallas kernels: 60 us -> 37.6 us
  waiting for transfers between devices: 45.1 us -> 50.7 us
  local copies, waits for them, and re-layouts: 4.47 us -> 6.37 us
  starting transfers between devices: 31.7 us -> 33.2 us
    pallas_call x4, Pallas kernels: 51.5 us -> 29.2 us  [wave(): pl.pallas_call(functools.partial(wave_kernel, pieces, kind, mode, len(sou...]
    ppermute x6, waiting for transfers between devices: 14 us -> 18.1 us  [line(): lax.ppermute(x, 'head', [(2 * a + c, 2 * b + c) for a, b in pairs for c i...]
    unnamed x10 -> x30, local copies, waits for them, and re-layouts: 2.03 us -> 4.67 us
    ppermute x7, waiting for transfers between devices: 0.02 us -> 2.17 us  [sibling(): return lax.ppermute(x, 'head', [(i, i ^ 1) for i in range(8)])]
    ppermute x18, starting transfers between devices: 20.3 us -> 21.8 us  [across(): return lax.ppermute(x, 'group', [(i, i ^ bit) for i in range(4)])]
  transfers between devices with their start and end apart: 31 -> 31, of which waited for: 13 -> 18; matrix products, arithmetic and copies ran while one was open for 3% -> 3% of each run, Pallas kernels for 36% -> 22%
where the time goes in v3:
time: 131 us
  waiting for transfers between devices  50.7 us (39%)
  Pallas kernels  37.6 us (29%)
  starting transfers between devices  33.2 us (25%)
  local copies, waits for them, and re-layouts  6.37 us (5%)
  other arithmetic  2.11 us (2%)
    ppermute x18, waiting for transfers between devices, across(): return lax.ppermute(x, 'group', [(i, i ^ bit) for i in range(4)])  30.5 us
    pallas_call x4, Pallas kernels, wave(): pl.pallas_call(functools.partial(wave_kernel, pieces, kind, mode, len(sou...  29.2 us
    ppermute x18, starting transfers between devices, across(): return lax.ppermute(x, 'group', [(i, i ^ bit) for i in range(4)])  21.8 us
    ppermute x6, waiting for transfers between devices, line(): lax.ppermute(x, 'head', [(2 * a + c, 2 * b + c) for a, b in pairs for c i...  18.1 us
    ppermute x6, starting transfers between devices, line(): lax.ppermute(x, 'head', [(2 * a + c, 2 * b + c) for a, b in pairs for c i...  9.4 us
    pallas_call x1, Pallas kernels, place(): pl.pallas_call(functools.partial(place_kernel, units), out_shape=(out, ou...  7.21 us
    unnamed x30, local copies, waits for them, and re-layouts  4.67 us
  transfers between devices with their start and end apart: 31, of which 18 were waited for; matrix products, arithmetic and copies ran while one was open for 3% of the time, Pallas kernels for 22%

profile of v3, /device:TPU:0, one launch (start us, length us, event | category | flops | bytes accessed | tf_op | source)
XLA Modules:
  0.0 130.9 jit_solution(4285173847176499475)
XLA Ops:
  0.6 1.2 copy-done.1
  1.9 0.7 copy-done.6
  2.6 1.2 norm.1
  3.8 0.8 copy-done.9
  4.6 0.5 collective-permute-start.2
  5.0 2.6 %collective-permute-start.1 = (bf16[32,8192]{1,0:T(8,128)(2,1)}, bf16[32,8192]{1,0:T(8,128)(2,1)S(1)}, u32[]{:S(2)}, u32[]{:S(2)}) collective-permute-start(bf16[32,8192]{1,0:T(8,128)(2,1)} %get-tuple-element.39), channel_id=1, source_target_pairs={{0,2},{1,3},{2,0},{3,1},{4,6},{5,7},{6,4},{7,5},{8,10},{9,11},{10,... | collective-permute-start | bytes 1572872 | tf_op jit(solution)/shard_map/ppermute | solution.py:329
  7.6 2.6 %collective-permute-start = (bf16[32,8192]{1,0:T(8,128)(2,1)}, bf16[32,8192]{1,0:T(8,128)(2,1)S(1)}, u32[]{:S(2)}, u32[]{:S(2)}) collective-permute-start(bf16[32,8192]{1,0:T(8,128)(2,1)} %get-tuple-element.39), channel_id=1, source_target_pairs={{0,4},{1,5},{2,6},{3,7},{4,0},{5,1},{6,2},{7,3},{8,12},{9,13},{10,... | collective-permute-start | bytes 1572872 | tf_op jit(solution)/shard_map/ppermute | solution.py:329
  10.2 0.8 dynamic-slice_convert_fusion
  11.0 0.1 reshape.31
  11.1 0.7 reshape.29.refs_4_.refs_6_
  11.8 0.7 reshape.30.refs_5_.refs_7_
  12.5 0.1 reshape.32
  12.7 1.0 fusion
  13.7 0.2 pad_maximum_fusion.1
  14.0 13.9 %wave0.1.refs_0_ = bf16[128,2048]{1,0:T(8,128)(2,1)S(1)} custom-call(bf16[64,8192]{1,0:T(8,128)(2,1)S(1)} %get-tuple-element.62.refs_0_, bf16[64,8192]{1,0:T(8,128)(2,1)S(1)} %collective-permute-done.2.refs_1_, bf16[8192,1024]{1,0:T(8,128)(2,1)} %refs_4_.5, bf16[8192,1024]{1,0:T(8,128)(2,1)} %refs_5_.5, bf16[1,1024]{1,0:T(2,128)(2,1)S(1)} %reshape.29.refs_4_.refs_6_, ...), custom_call_target="tpu_custom_call" | custom-call | flops 131072 | bytes 262144 | tf_op jit(solution)/shard_map/wave0/pallas_call | solution.py:249
  27.9 3.6 %collective-permute-done.1.refs_2_ = bf16[32,8192]{1,0:T(8,128)(2,1)S(1)} collective-permute-done((bf16[32,8192]{1,0:T(8,128)(2,1)}, bf16[32,8192]{1,0:T(8,128)(2,1)S(1)}, u32[]{:S(2)}, u32[]{:S(2)}) %collective-permute-start.1) | collective-permute-done | bytes 524320 | tf_op jit(solution)/shard_map/ppermute | solution.py:329
  31.5 2.6 %collective-permute-done.refs_0_ = bf16[32,8192]{1,0:T(8,128)(2,1)S(1)} collective-permute-done((bf16[32,8192]{1,0:T(8,128)(2,1)}, bf16[32,8192]{1,0:T(8,128)(2,1)S(1)}, u32[]{:S(2)}, u32[]{:S(2)}) %collective-permute-start) | collective-permute-done | bytes 524320 | tf_op jit(solution)/shard_map/ppermute | solution.py:329
  34.1 0.5 collective-permute-start.3
  34.6 1.5 %collective-permute-start.6 = (bf16[128,2048]{1,0:T(8,128)(2,1)S(1)}, bf16[128,2048]{1,0:T(8,128)(2,1)S(1)}, u32[]{:S(2)}, u32[]{:S(2)}) collective-permute-start(bf16[128,2048]{1,0:T(8,128)(2,1)S(1)} %wave0.1.refs_0_), channel_id=1, source_target_pairs={{0,16},{8,24},{16,0},{24,8},{1,17},{9,25},{17,1},{25,9},{2,18},{10... | collective-permute-start | bytes 1572872 | tf_op jit(solution)/shard_map/ppermute | solution.py:335
  36.1 1.5 %collective-permute-start.5 = (bf16[128,2048]{1,0:T(8,128)(2,1)S(1)}, bf16[128,2048]{1,0:T(8,128)(2,1)S(1)}, u32[]{:S(2)}, u32[]{:S(2)}) collective-permute-start(bf16[128,2048]{1,0:T(8,128)(2,1)S(1)} %wave0.1.refs_0_), channel_id=1, source_target_pairs={{0,8},{8,0},{16,24},{24,16},{1,9},{9,1},{17,25},{25,17},{2,10},{10... | collective-permute-start | bytes 1572872 | tf_op jit(solution)/shard_map/ppermute | solution.py:335
  37.6 0.4 collective-permute-start.10
  38.0 2.6 %collective-permute-start.9 = (bf16[32,8192]{1,0:T(8,128)(2,1)S(1)}, bf16[32,8192]{1,0:T(8,128)(2,1)S(1)}, u32[]{:S(2)}, u32[]{:S(2)}) collective-permute-start(bf16[32,8192]{1,0:T(8,128)(2,1)S(1)} %copy-done.10), channel_id=1, source_target_pairs={{0,4},{1,5},{2,6},{3,7},{4,0},{5,1},{6,2},{7,3},{8,12},{9,13},{10,... | collective-permute-start | bytes 1572872 | tf_op jit(solution)/shard_map/ppermute | solution.py:329
  40.7 5.2 %wave1.1.refs_4_ = bf16[128,2048]{1,0:T(8,128)(2,1)S(1)} custom-call(bf16[32,8192]{1,0:T(8,128)(2,1)S(1)} %collective-permute-done.refs_0_, bf16[32,8192]{1,0:T(8,128)(2,1)S(1)} %collective-permute-done.3.refs_1_, bf16[32,8192]{1,0:T(8,128)(2,1)S(1)} %collective-permute-done.1.refs_2_, bf16[32,8192]{1,0:T(8,128)(2,1)S(1)} %collective-permute-done.4.refs_3_, ...), custom_call_target="tpu_custom_call" | custom-call | flops 131072 | bytes 262144 | tf_op jit(solution)/shard_map/wave1/pallas_call | solution.py:249
  45.8 2.6 %collective-permute-done.6.refs_2_ = bf16[128,2048]{1,0:T(8,128)(2,1)S(1)} collective-permute-done((bf16[128,2048]{1,0:T(8,128)(2,1)S(1)}, bf16[128,2048]{1,0:T(8,128)(2,1)S(1)}, u32[]{:S(2)}, u32[]{:S(2)}) %collective-permute-start.6) | collective-permute-done | bytes 524320 | tf_op jit(solution)/shard_map/ppermute | solution.py:335
  48.4 1.2 collective-permute-done.5.refs_1_
  49.7 0.5 collective-permute-start.8
  50.2 1.5 %collective-permute-start.7 = (bf16[128,2048]{1,0:T(8,128)(2,1)S(1)}, bf16[128,2048]{1,0:T(8,128)(2,1)S(1)}, u32[]{:S(2)}, u32[]{:S(2)}) collective-permute-start(bf16[128,2048]{1,0:T(8,128)(2,1)S(1)} %wave1.1.refs_4_), channel_id=1, source_target_pairs={{0,8},{8,0},{16,24},{24,16},{1,9},{9,1},{17,25},{25,17},{2,10},{10... | collective-permute-start | bytes 1572872 | tf_op jit(solution)/shard_map/ppermute | solution.py:335
  51.7 10.2 %collective-permute-done.10.refs_2_ = bf16[32,8192]{1,0:T(8,128)(2,1)S(1)} collective-permute-done((bf16[32,8192]{1,0:T(8,128)(2,1)S(1)}, bf16[32,8192]{1,0:T(8,128)(2,1)S(1)}, u32[]{:S(2)}, u32[]{:S(2)}) %collective-permute-start.10) | collective-permute-done | bytes 524320 | tf_op jit(solution)/shard_map/ppermute | solution.py:329
  61.8 1.4 %collective-permute-done.9.refs_0_ = bf16[32,8192]{1,0:T(8,128)(2,1)S(1)} collective-permute-done((bf16[32,8192]{1,0:T(8,128)(2,1)S(1)}, bf16[32,8192]{1,0:T(8,128)(2,1)S(1)}, u32[]{:S(2)}, u32[]{:S(2)}) %collective-permute-start.9) | collective-permute-done | bytes 524320 | tf_op jit(solution)/shard_map/ppermute | solution.py:329
  63.2 0.8 collective-permute-start.11
  64.1 1.5 %collective-permute-start.12 = (bf16[128,2048]{1,0:T(8,128)(2,1)S(1)}, bf16[128,2048]{1,0:T(8,128)(2,1)S(1)}, u32[]{:S(2)}, u32[]{:S(2)}) collective-permute-start(bf16[128,2048]{1,0:T(8,128)(2,1)S(1)} %collective-permute-done.8.refs_6_), channel_id=1, source_target_pairs={{0,8},{8,0},{16,24},{24,16},{1,9},{9,1},{17,25},{25,17},{2,10},{10... | collective-permute-start | bytes 1572872 | tf_op jit(solution)/shard_map/ppermute | solution.py:335
  65.6 0.5 collective-permute-start.13
  66.1 0.5 collective-permute-start.20
  66.6 0.8 collective-permute-done.14.refs_3_
  67.5 0.7 collective-permute-start.19
  68.2 5.0 %wave2.1 = (bf16[64,2048]{1,0:T(8,128)(2,1)S(1)}, bf16[64,2048]{1,0:T(8,128)(2,1)S(1)}) custom-call(bf16[32,8192]{1,0:T(8,128)(2,1)S(1)} %collective-permute-done.9.refs_0_, bf16[32,8192]{1,0:T(8,128)(2,1)S(1)} %collective-permute-done.13.refs_1_, bf16[32,8192]{1,0:T(8,128)(2,1)S(1)} %collective-permute-done.10.refs_2_, ...), custom_call_target="tpu_custom_call" | custom-call | flops 131072 | bytes 262144 | tf_op jit(solution)/shard_map/wave2/pallas_call | solution.py:249
  73.2 1.4 %collective-permute-done.11.refs_3_ = bf16[128,2048]{1,0:T(8,128)(2,1)S(1)} collective-permute-done((bf16[128,2048]{1,0:T(8,128)(2,1)S(1)}, bf16[128,2048]{1,0:T(8,128)(2,1)S(1)}, u32[]{:S(2)}, u32[]{:S(2)}) %collective-permute-start.11) | collective-permute-done | bytes 524320 | tf_op jit(solution)/shard_map/ppermute | solution.py:335
  74.6 1.6 %collective-permute-done.12.refs_7_ = bf16[128,2048]{1,0:T(8,128)(2,1)S(1)} collective-permute-done((bf16[128,2048]{1,0:T(8,128)(2,1)S(1)}, bf16[128,2048]{1,0:T(8,128)(2,1)S(1)}, u32[]{:S(2)}, u32[]{:S(2)}) %collective-permute-start.12) | collective-permute-done | bytes 524320 | tf_op jit(solution)/shard_map/ppermute | solution.py:335
  76.2 0.4 collective-permute-start.17
  76.5 1.7 %collective-permute-start.15 = (bf16[64,2048]{1,0:T(8,128)(2,1)S(1)}, bf16[64,2048]{1,0:T(8,128)(2,1)S(1)}, u32[]{:S(2)}, u32[]{:S(2)}) collective-permute-start(bf16[64,2048]{1,0:T(8,128)(2,1)S(1)} %get-tuple-element.60.refs_8_), channel_id=1, source_target_pairs={{0,8},{8,0},{16,24},{24,16},{1,9},{9,1},{17,25},{25,17},{2,10},{10... | collective-permute-start | bytes 786440 | tf_op jit(solution)/shard_map/ppermute | solution.py:335
  78.3 1.7 %collective-permute-start.18 = (bf16[64,2048]{1,0:T(8,128)(2,1)S(1)}, bf16[64,2048]{1,0:T(8,128)(2,1)S(1)}, u32[]{:S(2)}, u32[]{:S(2)}) collective-permute-start(bf16[64,2048]{1,0:T(8,128)(2,1)S(1)} %get-tuple-element.61.refs_9_), channel_id=1, source_target_pairs={{0,16},{8,24},{16,0},{24,8},{1,17},{9,25},{17,1},{25,9},{2,18},{10... | collective-permute-start | bytes 786440 | tf_op jit(solution)/shard_map/ppermute | solution.py:335
  79.9 4.6 %collective-permute-done.17.refs_12_ = bf16[64,2048]{1,0:T(8,128)(2,1)S(1)} collective-permute-done((bf16[64,2048]{1,0:T(8,128)(2,1)S(1)}, bf16[64,2048]{1,0:T(8,128)(2,1)S(1)}, u32[]{:S(2)}, u32[]{:S(2)}) %collective-permute-start.17) | collective-permute-done | bytes 262176 | tf_op jit(solution)/shard_map/ppermute | solution.py:335
  84.5 2.0 %collective-permute-start.16 = (bf16[64,2048]{1,0:T(8,128)(2,1)S(1)}, bf16[64,2048]{1,0:T(8,128)(2,1)S(1)}, u32[]{:S(2)}, u32[]{:S(2)}) collective-permute-start(bf16[64,2048]{1,0:T(8,128)(2,1)S(1)} %get-tuple-element.61.refs_9_), channel_id=1, source_target_pairs={{0,8},{8,0},{16,24},{24,16},{1,9},{9,1},{17,25},{25,17},{2,10},{10... | collective-permute-start | bytes 786440 | tf_op jit(solution)/shard_map/ppermute | solution.py:335
  86.5 0.8 collective-permute-done.18.refs_13_
  87.4 3.6 %collective-permute-done.16.refs_11_ = bf16[64,2048]{1,0:T(8,128)(2,1)S(1)} collective-permute-done((bf16[64,2048]{1,0:T(8,128)(2,1)S(1)}, bf16[64,2048]{1,0:T(8,128)(2,1)S(1)}, u32[]{:S(2)}, u32[]{:S(2)}) %collective-permute-start.16) | collective-permute-done | bytes 262176 | tf_op jit(solution)/shard_map/ppermute | solution.py:335
  90.9 0.3 collective-permute-done.20.refs_2_
  91.3 0.5 collective-permute-start.22
  91.8 0.6 collective-permute-start.23
  92.4 1.7 %collective-permute-start.24 = (bf16[64,2048]{1,0:T(8,128)(2,1)S(1)}, bf16[64,2048]{1,0:T(8,128)(2,1)S(1)}, u32[]{:S(2)}, u32[]{:S(2)}) collective-permute-start(bf16[64,2048]{1,0:T(8,128)(2,1)S(1)} %collective-permute-done.18.refs_13_), channel_id=1, source_target_pairs={{0,8},{8,0},{16,24},{24,16},{1,9},{9,1},{17,25},{25,17},{2,10},{10... | collective-permute-start | bytes 786440 | tf_op jit(solution)/shard_map/ppermute | solution.py:335
  94.1 1.3 collective-permute-done.22.refs_3_
  95.4 5.2 %wave3.1 = (bf16[64,2048]{1,0:T(8,128)(2,1)S(1)}, bf16[64,2048]{1,0:T(8,128)(2,1)S(1)}) custom-call(bf16[64,8192]{1,0:T(8,128)(2,1)S(1)} %collective-permute-done.19.refs_0_, bf16[64,8192]{1,0:T(8,128)(2,1)S(1)} %collective-permute-done.21.refs_1_, bf16[64,8192]{1,0:T(8,128)(2,1)S(1)} %collective-permute-done.20.refs_2_, ...), custom_call_target="tpu_custom_call" | custom-call | flops 131072 | bytes 262144 | tf_op jit(solution)/shard_map/wave3/pallas_call | solution.py:249
  100.7 1.8 %collective-permute-start.25 = (bf16[64,2048]{1,0:T(8,128)(2,1)S(1)}, bf16[64,2048]{1,0:T(8,128)(2,1)S(1)}, u32[]{:S(2)}, u32[]{:S(2)}) collective-permute-start(bf16[64,2048]{1,0:T(8,128)(2,1)S(1)} %get-tuple-element.74.refs_16_), channel_id=1, source_target_pairs={{0,8},{8,0},{16,24},{24,16},{1,9},{9,1},{17,25},{25,17},{2,10},{10... | collective-permute-start | bytes 786440 | tf_op jit(solution)/shard_map/ppermute | solution.py:335
  102.5 1.1 collective-permute-start.28
  103.5 1.0 collective-permute-start.27
  104.5 0.3 collective-permute-start.26
  104.8 5.1 %collective-permute-done.25.refs_18_ = bf16[64,2048]{1,0:T(8,128)(2,1)S(1)} collective-permute-done((bf16[64,2048]{1,0:T(8,128)(2,1)S(1)}, bf16[64,2048]{1,0:T(8,128)(2,1)S(1)}, u32[]{:S(2)}, u32[]{:S(2)}) %collective-permute-start.25) | collective-permute-done | bytes 262176 | tf_op jit(solution)/shard_map/ppermute | solution.py:335
  109.9 1.1 collective-permute-start.29
  111.0 0.6 collective-permute-done.28.refs_21_
  111.7 1.1 collective-permute-start.30
  112.8 4.5 %collective-permute-done.27.refs_20_ = bf16[64,2048]{1,0:T(8,128)(2,1)S(1)} collective-permute-done((bf16[64,2048]{1,0:T(8,128)(2,1)S(1)}, bf16[64,2048]{1,0:T(8,128)(2,1)S(1)}, u32[]{:S(2)}, u32[]{:S(2)}) %collective-permute-start.27) | collective-permute-done | bytes 262176 | tf_op jit(solution)/shard_map/ppermute | solution.py:335
  117.3 4.5 %collective-permute-done.29.refs_22_ = bf16[64,2048]{1,0:T(8,128)(2,1)S(1)} collective-permute-done((bf16[64,2048]{1,0:T(8,128)(2,1)S(1)}, bf16[64,2048]{1,0:T(8,128)(2,1)S(1)}, u32[]{:S(2)}, u32[]{:S(2)}) %collective-permute-start.29) | collective-permute-done | bytes 262176 | tf_op jit(solution)/shard_map/ppermute | solution.py:335
  121.8 0.9 copy-done.3
  122.7 0.9 copy-done.5
  123.7 7.2 %place.1 = (bf16[1024,1024]{1,0:T(8,128)(2,1)}, bf16[1024,1024]{1,0:T(8,128)(2,1)}) custom-call(s32[16]{0:T(128)S(1)} %copy-done.7, s32[16]{0:T(128)S(1)} %copy-done.8, bf16[128,2048]{1,0:T(8,128)(2,1)S(1)} %wave0.1.refs_0_, bf16[128,2048]{1,0:T(8,128)(2,1)S(1)} %collective-permute-done.5.refs_1_, bf16[128,2048]{1,0:T(8,128)(2,1)S(1)} %collective-permute-done.6.refs_2_, ...), custom_call_target="tpu_custom_call" | custom-call | bytes 20971520 | tf_op jit(solution)/shard_map/place/pallas_call | solution.py:312
  (47 shorter events, 0.4 us)
Async XLA Ops:
  0.6 1.2 copy-start.1
  1.9 0.7 copy-start.6
  3.8 0.8 copy-start.9
  4.6 9.4 %collective-permute-start.2 = (bf16[64,8192]{1,0:T(8,128)(2,1)S(1)}, bf16[64,8192]{1,0:T(8,128)(2,1)S(1)}, u32[]{:S(2)}, u32[]{:S(2)}) collective-permute-start(bf16[64,8192]{1,0:T(8,128)(2,1)S(1)} %get-tuple-element.62.refs_0_), channel_id=1, source_target_pairs={{0,1},{1,0},{2,3},{3,2},{4,5},{5,4},{6,7},{7,6},{8,9},{9,8},{10,11... | collective-permute-start | bytes 3145736 | tf_op jit(solution)/shard_map/ppermute | solution.py:332
  5.0 26.5 %collective-permute-start.1 = (bf16[32,8192]{1,0:T(8,128)(2,1)}, bf16[32,8192]{1,0:T(8,128)(2,1)S(1)}, u32[]{:S(2)}, u32[]{:S(2)}) collective-permute-start(bf16[32,8192]{1,0:T(8,128)(2,1)} %get-tuple-element.39), channel_id=1, source_target_pairs={{0,2},{1,3},{2,0},{3,1},{4,6},{5,7},{6,4},{7,5},{8,10},{9,11},{10,... | collective-permute-start | bytes 1572872 | tf_op jit(solution)/shard_map/ppermute | solution.py:329
  7.6 26.5 %collective-permute-start = (bf16[32,8192]{1,0:T(8,128)(2,1)}, bf16[32,8192]{1,0:T(8,128)(2,1)S(1)}, u32[]{:S(2)}, u32[]{:S(2)}) collective-permute-start(bf16[32,8192]{1,0:T(8,128)(2,1)} %get-tuple-element.39), channel_id=1, source_target_pairs={{0,4},{1,5},{2,6},{3,7},{4,0},{5,1},{6,2},{7,3},{8,12},{9,13},{10,... | collective-permute-start | bytes 1572872 | tf_op jit(solution)/shard_map/ppermute | solution.py:329
  14.0 26.7 %slice-start = ((s8[16777216]{0:T(1024)(128)(4,1)}), s8[4194304]{0:T(1024)(128)(4,1)S(1)}, s32[]{:S(2)}) async-start(s8[16777216]{0:T(1024)(128)(4,1)} %bitcast.3), calls=%async_computation | async-start | bytes 8388608
  14.0 23.6 %copy-start.10 = (bf16[32,8192]{1,0:T(8,128)(2,1)S(1)}, bf16[32,8192]{1,0:T(8,128)(2,1)}, u32[]{:S(2)}) copy-start(bf16[32,8192]{1,0:T(8,128)(2,1)} %copy-done.9) | copy-start | bytes 1572868
  14.0 26.6 %slice-start.1 = ((s8[16777216]{0:T(1024)(128)(4,1)}), s8[4194304]{0:T(1024)(128)(4,1)S(1)}, s32[]{:S(2)}) async-start(s8[16777216]{0:T(1024)(128)(4,1)} %bitcast.3), calls=%async_computation.1 | async-start | bytes 8388608
  14.0 26.6 %slice-start.2 = ((s8[16777216]{0:T(1024)(128)(4,1)}), s8[4194304]{0:T(1024)(128)(4,1)S(1)}, s32[]{:S(2)}) async-start(s8[16777216]{0:T(1024)(128)(4,1)} %bitcast.3), calls=%async_computation.2 | async-start | bytes 8388608
  14.0 26.6 %slice-start.3 = ((s8[16777216]{0:T(1024)(128)(4,1)}), s8[4194304]{0:T(1024)(128)(4,1)S(1)}, s32[]{:S(2)}) async-start(s8[16777216]{0:T(1024)(128)(4,1)} %bitcast.3), calls=%async_computation.3 | async-start | bytes 8388608
  14.0 26.6 %copy-start = (bf16[8192,1024]{1,0:T(8,128)(2,1)S(1)}, bf16[8192,1024]{1,0:T(8,128)(2,1)}, u32[]{:S(2)}) copy-start(bf16[8192,1024]{1,0:T(8,128)(2,1)} %refs_5_.5) | copy-start | bytes 50331652
  34.1 4.0 %collective-permute-start.4 = (bf16[32,8192]{1,0:T(8,128)(2,1)S(1)}, bf16[32,8192]{1,0:T(8,128)(2,1)S(1)}, u32[]{:S(2)}, u32[]{:S(2)}) collective-permute-start(bf16[32,8192]{1,0:T(8,128)(2,1)S(1)} %collective-permute-done.1.refs_2_), channel_id=1, source_target_pairs={{0,1},{1,0},{2,3},{3,2},{4,5},{5,4},{6,7},{7,6},{8,9},{9,8},{10,11... | collective-permute-start | bytes 1572872 | tf_op jit(solution)/shard_map/ppermute | solution.py:332
  34.1 6.5 %collective-permute-start.3 = (bf16[32,8192]{1,0:T(8,128)(2,1)S(1)}, bf16[32,8192]{1,0:T(8,128)(2,1)S(1)}, u32[]{:S(2)}, u32[]{:S(2)}) collective-permute-start(bf16[32,8192]{1,0:T(8,128)(2,1)S(1)} %collective-permute-done.refs_0_), channel_id=1, source_target_pairs={{0,1},{1,0},{2,3},{3,2},{4,5},{5,4},{6,7},{7,6},{8,9},{9,8},{10,11... | collective-permute-start | bytes 1572872 | tf_op jit(solution)/shard_map/ppermute | solution.py:332
  34.6 13.8 %collective-permute-start.6 = (bf16[128,2048]{1,0:T(8,128)(2,1)S(1)}, bf16[128,2048]{1,0:T(8,128)(2,1)S(1)}, u32[]{:S(2)}, u32[]{:S(2)}) collective-permute-start(bf16[128,2048]{1,0:T(8,128)(2,1)S(1)} %wave0.1.refs_0_), channel_id=1, source_target_pairs={{0,16},{8,24},{16,0},{24,8},{1,17},{9,25},{17,1},{25,9},{2,18},{10... | collective-permute-start | bytes 1572872 | tf_op jit(solution)/shard_map/ppermute | solution.py:335
  36.1 13.6 %collective-permute-start.5 = (bf16[128,2048]{1,0:T(8,128)(2,1)S(1)}, bf16[128,2048]{1,0:T(8,128)(2,1)S(1)}, u32[]{:S(2)}, u32[]{:S(2)}) collective-permute-start(bf16[128,2048]{1,0:T(8,128)(2,1)S(1)} %wave0.1.refs_0_), channel_id=1, source_target_pairs={{0,8},{8,0},{16,24},{24,16},{1,9},{9,1},{17,25},{25,17},{2,10},{10... | collective-permute-start | bytes 1572872 | tf_op jit(solution)/shard_map/ppermute | solution.py:335
  37.6 24.2 %collective-permute-start.10 = (bf16[32,8192]{1,0:T(8,128)(2,1)S(1)}, bf16[32,8192]{1,0:T(8,128)(2,1)S(1)}, u32[]{:S(2)}, u32[]{:S(2)}) collective-permute-start(bf16[32,8192]{1,0:T(8,128)(2,1)S(1)} %copy-done.10), channel_id=1, source_target_pairs={{0,2},{1,3},{2,0},{3,1},{4,6},{5,7},{6,4},{7,5},{8,10},{9,11},{10,... | collective-permute-start | bytes 1572872 | tf_op jit(solution)/shard_map/ppermute | solution.py:329
  38.0 25.2 %collective-permute-start.9 = (bf16[32,8192]{1,0:T(8,128)(2,1)S(1)}, bf16[32,8192]{1,0:T(8,128)(2,1)S(1)}, u32[]{:S(2)}, u32[]{:S(2)}) collective-permute-start(bf16[32,8192]{1,0:T(8,128)(2,1)S(1)} %copy-done.10), channel_id=1, source_target_pairs={{0,4},{1,5},{2,6},{3,7},{4,0},{5,1},{6,2},{7,3},{8,12},{9,13},{10,... | collective-permute-start | bytes 1572872 | tf_op jit(solution)/shard_map/ppermute | solution.py:329
  49.7 13.6 %collective-permute-start.8 = (bf16[128,2048]{1,0:T(8,128)(2,1)S(1)}, bf16[128,2048]{1,0:T(8,128)(2,1)S(1)}, u32[]{:S(2)}, u32[]{:S(2)}) collective-permute-start(bf16[128,2048]{1,0:T(8,128)(2,1)S(1)} %wave1.1.refs_4_), channel_id=1, source_target_pairs={{0,16},{8,24},{16,0},{24,8},{1,17},{9,25},{17,1},{25,9},{2,18},{10... | collective-permute-start | bytes 1572872 | tf_op jit(solution)/shard_map/ppermute | solution.py:335
  50.2 13.1 %collective-permute-start.7 = (bf16[128,2048]{1,0:T(8,128)(2,1)S(1)}, bf16[128,2048]{1,0:T(8,128)(2,1)S(1)}, u32[]{:S(2)}, u32[]{:S(2)}) collective-permute-start(bf16[128,2048]{1,0:T(8,128)(2,1)S(1)} %wave1.1.refs_4_), channel_id=1, source_target_pairs={{0,8},{8,0},{16,24},{24,16},{1,9},{9,1},{17,25},{25,17},{2,10},{10... | collective-permute-start | bytes 1572872 | tf_op jit(solution)/shard_map/ppermute | solution.py:335
  63.2 11.4 %collective-permute-start.11 = (bf16[128,2048]{1,0:T(8,128)(2,1)S(1)}, bf16[128,2048]{1,0:T(8,128)(2,1)S(1)}, u32[]{:S(2)}, u32[]{:S(2)}) collective-permute-start(bf16[128,2048]{1,0:T(8,128)(2,1)S(1)} %collective-permute-done.5.refs_1_), channel_id=1, source_target_pairs={{0,16},{8,24},{16,0},{24,8},{1,17},{9,25},{17,1},{25,9},{2,18},{10... | collective-permute-start | bytes 1572872 | tf_op jit(solution)/shard_map/ppermute | solution.py:335
  64.1 12.1 %collective-permute-start.12 = (bf16[128,2048]{1,0:T(8,128)(2,1)S(1)}, bf16[128,2048]{1,0:T(8,128)(2,1)S(1)}, u32[]{:S(2)}, u32[]{:S(2)}) collective-permute-start(bf16[128,2048]{1,0:T(8,128)(2,1)S(1)} %collective-permute-done.8.refs_6_), channel_id=1, source_target_pairs={{0,8},{8,0},{16,24},{24,16},{1,9},{9,1},{17,25},{25,17},{2,10},{10... | collective-permute-start | bytes 1572872 | tf_op jit(solution)/shard_map/ppermute | solution.py:335
  65.6 1.9 %collective-permute-start.14 = (bf16[32,8192]{1,0:T(8,128)(2,1)S(1)}, bf16[32,8192]{1,0:T(8,128)(2,1)S(1)}, u32[]{:S(2)}, u32[]{:S(2)}) collective-permute-start(bf16[32,8192]{1,0:T(8,128)(2,1)S(1)} %collective-permute-done.10.refs_2_), channel_id=1, source_target_pairs={{0,1},{1,0},{2,3},{3,2},{4,5},{5,4},{6,7},{7,6},{8,9},{9,8},{10,11... | collective-permute-start | bytes 1572872 | tf_op jit(solution)/shard_map/ppermute | solution.py:332
  65.6 2.7 %collective-permute-start.13 = (bf16[32,8192]{1,0:T(8,128)(2,1)S(1)}, bf16[32,8192]{1,0:T(8,128)(2,1)S(1)}, u32[]{:S(2)}, u32[]{:S(2)}) collective-permute-start(bf16[32,8192]{1,0:T(8,128)(2,1)S(1)} %collective-permute-done.9.refs_0_), channel_id=1, source_target_pairs={{0,1},{1,0},{2,3},{3,2},{4,5},{5,4},{6,7},{7,6},{8,9},{9,8},{10,11... | collective-permute-start | bytes 1572872 | tf_op jit(solution)/shard_map/ppermute | solution.py:332
  66.1 25.1 %collective-permute-start.20 = (bf16[64,8192]{1,0:T(8,128)(2,1)S(1)}, bf16[64,8192]{1,0:T(8,128)(2,1)S(1)}, u32[]{:S(2)}, u32[]{:S(2)}) collective-permute-start(bf16[64,8192]{1,0:T(8,128)(2,1)S(1)} %pad_maximum_fusion), channel_id=1, source_target_pairs={{0,2},{1,3},{2,0},{3,1},{4,6},{5,7},{6,4},{7,5},{8,10},{9,11},{10,... | collective-permute-start | bytes 3145736 | tf_op jit(solution)/shard_map/ppermute | solution.py:329
  67.5 23.8 %collective-permute-start.19 = (bf16[64,8192]{1,0:T(8,128)(2,1)S(1)}, bf16[64,8192]{1,0:T(8,128)(2,1)S(1)}, u32[]{:S(2)}, u32[]{:S(2)}) collective-permute-start(bf16[64,8192]{1,0:T(8,128)(2,1)S(1)} %get-tuple-element.62.refs_0_), channel_id=1, source_target_pairs={{2,4},{3,5},{4,2},{5,3},{10,12},{11,13},{12,10},{13,11},{18,20},{1... | collective-permute-start | bytes 3145736 | tf_op jit(solution)/shard_map/ppermute | solution.py:329
  76.2 45.6 %copy-start.7 = (s32[16]{0:T(128)S(1)}, s32[16]{0:T(128)}, u32[]{:S(2)}) copy-start(s32[16]{0:T(128)} %lengths.1) | copy-start | bytes 196
  76.2 45.6 %copy-start.8 = (s32[16]{0:T(128)S(1)}, s32[16]{0:T(128)}, u32[]{:S(2)}) copy-start(s32[16]{0:T(128)} %owner.1) | copy-start | bytes 196
  76.2 8.4 %collective-permute-start.17 = (bf16[64,2048]{1,0:T(8,128)(2,1)S(1)}, bf16[64,2048]{1,0:T(8,128)(2,1)S(1)}, u32[]{:S(2)}, u32[]{:S(2)}) collective-permute-start(bf16[64,2048]{1,0:T(8,128)(2,1)S(1)} %get-tuple-element.60.refs_8_), channel_id=1, source_target_pairs={{0,16},{8,24},{16,0},{24,8},{1,17},{9,25},{17,1},{25,9},{2,18},{10... | collective-permute-start | bytes 786440 | tf_op jit(solution)/shard_map/ppermute | solution.py:335
  76.5 10.0 %collective-permute-start.15 = (bf16[64,2048]{1,0:T(8,128)(2,1)S(1)}, bf16[64,2048]{1,0:T(8,128)(2,1)S(1)}, u32[]{:S(2)}, u32[]{:S(2)}) collective-permute-start(bf16[64,2048]{1,0:T(8,128)(2,1)S(1)} %get-tuple-element.60.refs_8_), channel_id=1, source_target_pairs={{0,8},{8,0},{16,24},{24,16},{1,9},{9,1},{17,25},{25,17},{2,10},{10... | collective-permute-start | bytes 786440 | tf_op jit(solution)/shard_map/ppermute | solution.py:335
  78.3 9.1 %collective-permute-start.18 = (bf16[64,2048]{1,0:T(8,128)(2,1)S(1)}, bf16[64,2048]{1,0:T(8,128)(2,1)S(1)}, u32[]{:S(2)}, u32[]{:S(2)}) collective-permute-start(bf16[64,2048]{1,0:T(8,128)(2,1)S(1)} %get-tuple-element.61.refs_9_), channel_id=1, source_target_pairs={{0,16},{8,24},{16,0},{24,8},{1,17},{9,25},{17,1},{25,9},{2,18},{10... | collective-permute-start | bytes 786440 | tf_op jit(solution)/shard_map/ppermute | solution.py:335
  84.5 6.4 %collective-permute-start.16 = (bf16[64,2048]{1,0:T(8,128)(2,1)S(1)}, bf16[64,2048]{1,0:T(8,128)(2,1)S(1)}, u32[]{:S(2)}, u32[]{:S(2)}) collective-permute-start(bf16[64,2048]{1,0:T(8,128)(2,1)S(1)} %get-tuple-element.61.refs_9_), channel_id=1, source_target_pairs={{0,8},{8,0},{16,24},{24,16},{1,9},{9,1},{17,25},{25,17},{2,10},{10... | collective-permute-start | bytes 786440 | tf_op jit(solution)/shard_map/ppermute | solution.py:335
  87.4 13.3 %copy-start.2 = (bf16[64,2048]{1,0:T(8,128)(2,1)}, bf16[64,2048]{1,0:T(8,128)(2,1)S(1)}, u32[]{:S(2)}) copy-start(bf16[64,2048]{1,0:T(8,128)(2,1)S(1)} %collective-permute-done.18.refs_13_) | copy-start | bytes 786436
  90.9 9.7 %copy-start.4 = (bf16[64,2048]{1,0:T(8,128)(2,1)}, bf16[64,2048]{1,0:T(8,128)(2,1)S(1)}, u32[]{:S(2)}) copy-start(bf16[64,2048]{1,0:T(8,128)(2,1)S(1)} %collective-permute-done.16.refs_11_) | copy-start | bytes 786436
  91.3 2.9 %collective-permute-start.21 = (bf16[64,8192]{1,0:T(8,128)(2,1)S(1)}, bf16[64,8192]{1,0:T(8,128)(2,1)S(1)}, u32[]{:S(2)}, u32[]{:S(2)}) collective-permute-start(bf16[64,8192]{1,0:T(8,128)(2,1)S(1)} %collective-permute-done.19.refs_0_), channel_id=1, source_target_pairs={{0,1},{1,0},{2,3},{3,2},{4,5},{5,4},{6,7},{7,6},{8,9},{9,8},{10,11... | collective-permute-start | bytes 3145736 | tf_op jit(solution)/shard_map/ppermute | solution.py:332
  91.3 4.2 %collective-permute-start.22 = (bf16[64,8192]{1,0:T(8,128)(2,1)S(1)}, bf16[64,8192]{1,0:T(8,128)(2,1)S(1)}, u32[]{:S(2)}, u32[]{:S(2)}) collective-permute-start(bf16[64,8192]{1,0:T(8,128)(2,1)S(1)} %collective-permute-done.20.refs_2_), channel_id=1, source_target_pairs={{0,1},{1,0},{2,3},{3,2},{4,5},{5,4},{6,7},{7,6},{8,9},{9,8},{10,11... | collective-permute-start | bytes 3145736 | tf_op jit(solution)/shard_map/ppermute | solution.py:332
  91.8 8.9 %collective-permute-start.23 = (bf16[64,2048]{1,0:T(8,128)(2,1)S(1)}, bf16[64,2048]{1,0:T(8,128)(2,1)S(1)}, u32[]{:S(2)}, u32[]{:S(2)}) collective-permute-start(bf16[64,2048]{1,0:T(8,128)(2,1)S(1)} %collective-permute-done.15.refs_10_), channel_id=1, source_target_pairs={{0,16},{8,24},{16,0},{24,8},{1,17},{9,25},{17,1},{25,9},{2,18},{10... | collective-permute-start | bytes 786440 | tf_op jit(solution)/shard_map/ppermute | solution.py:335
  92.4 8.3 %collective-permute-start.24 = (bf16[64,2048]{1,0:T(8,128)(2,1)S(1)}, bf16[64,2048]{1,0:T(8,128)(2,1)S(1)}, u32[]{:S(2)}, u32[]{:S(2)}) collective-permute-start(bf16[64,2048]{1,0:T(8,128)(2,1)S(1)} %collective-permute-done.18.refs_13_), channel_id=1, source_target_pairs={{0,8},{8,0},{16,24},{24,16},{1,9},{9,1},{17,25},{25,17},{2,10},{10... | collective-permute-start | bytes 786440 | tf_op jit(solution)/shard_map/ppermute | solution.py:335
  100.7 9.2 %collective-permute-start.25 = (bf16[64,2048]{1,0:T(8,128)(2,1)S(1)}, bf16[64,2048]{1,0:T(8,128)(2,1)S(1)}, u32[]{:S(2)}, u32[]{:S(2)}) collective-permute-start(bf16[64,2048]{1,0:T(8,128)(2,1)S(1)} %get-tuple-element.74.refs_16_), channel_id=1, source_target_pairs={{0,8},{8,0},{16,24},{24,16},{1,9},{9,1},{17,25},{25,17},{2,10},{10... | collective-permute-start | bytes 786440 | tf_op jit(solution)/shard_map/ppermute | solution.py:335
  102.5 9.2 %collective-permute-start.28 = (bf16[64,2048]{1,0:T(8,128)(2,1)S(1)}, bf16[64,2048]{1,0:T(8,128)(2,1)S(1)}, u32[]{:S(2)}, u32[]{:S(2)}) collective-permute-start(bf16[64,2048]{1,0:T(8,128)(2,1)S(1)} %get-tuple-element.75.refs_17_), channel_id=1, source_target_pairs={{0,16},{8,24},{16,0},{24,8},{1,17},{9,25},{17,1},{25,9},{2,18},{10... | collective-permute-start | bytes 786440 | tf_op jit(solution)/shard_map/ppermute | solution.py:335
  103.5 13.7 %collective-permute-start.27 = (bf16[64,2048]{1,0:T(8,128)(2,1)S(1)}, bf16[64,2048]{1,0:T(8,128)(2,1)S(1)}, u32[]{:S(2)}, u32[]{:S(2)}) collective-permute-start(bf16[64,2048]{1,0:T(8,128)(2,1)S(1)} %get-tuple-element.74.refs_16_), channel_id=1, source_target_pairs={{0,16},{8,24},{16,0},{24,8},{1,17},{9,25},{17,1},{25,9},{2,18},{10... | collective-permute-start | bytes 786440 | tf_op jit(solution)/shard_map/ppermute | solution.py:335
  104.5 12.8 %collective-permute-start.26 = (bf16[64,2048]{1,0:T(8,128)(2,1)S(1)}, bf16[64,2048]{1,0:T(8,128)(2,1)S(1)}, u32[]{:S(2)}, u32[]{:S(2)}) collective-permute-start(bf16[64,2048]{1,0:T(8,128)(2,1)S(1)} %get-tuple-element.75.refs_17_), channel_id=1, source_target_pairs={{0,8},{8,0},{16,24},{24,16},{1,9},{9,1},{17,25},{25,17},{2,10},{10... | collective-permute-start | bytes 786440 | tf_op jit(solution)/shard_map/ppermute | solution.py:335
  109.9 11.9 %collective-permute-start.29 = (bf16[64,2048]{1,0:T(8,128)(2,1)S(1)}, bf16[64,2048]{1,0:T(8,128)(2,1)S(1)}, u32[]{:S(2)}, u32[]{:S(2)}) collective-permute-start(bf16[64,2048]{1,0:T(8,128)(2,1)S(1)} %collective-permute-done.25.refs_18_), channel_id=1, source_target_pairs={{0,16},{8,24},{16,0},{24,8},{1,17},{9,25},{17,1},{25,9},{2,18},{10... | collective-permute-start | bytes 786440 | tf_op jit(solution)/shard_map/ppermute | solution.py:335
  111.7 10.1 %collective-permute-start.30 = (bf16[64,2048]{1,0:T(8,128)(2,1)S(1)}, bf16[64,2048]{1,0:T(8,128)(2,1)S(1)}, u32[]{:S(2)}, u32[]{:S(2)}) collective-permute-start(bf16[64,2048]{1,0:T(8,128)(2,1)S(1)} %collective-permute-done.28.refs_21_), channel_id=1, source_target_pairs={{0,8},{8,0},{16,24},{24,16},{1,9},{9,1},{17,25},{25,17},{2,10},{10... | collective-permute-start | bytes 786440 | tf_op jit(solution)/shard_map/ppermute | solution.py:335
  121.8 1.0 copy-start.3
  122.7 0.9 copy-start.5

commit v4 on v3

--- a/solution.py
+++ b/solution.py
@@ -70,11 +70,22 @@
     return (key_cache, value_cache)
 
 
-def norm_kernel(x_ref, gain_ref, out_ref, lo_ref, hi_ref):
+def norm_kernel(x_hbm, gain_hbm, out_ref, lo_ref, hi_ref, x_ref, gain_ref, sem):
     step = 16
     first = lo_ref.shape[0]
+    rows = x_ref.shape[0]
+    gain_copy = pltpu.make_async_copy(gain_hbm, gain_ref, sem.at[0])
+    copies = [
+        pltpu.make_async_copy(x_hbm.at[pl.ds(at, step)], x_ref.at[pl.ds(at, step)], sem.at[1 + at // step])
+        for at in range(0, rows, step)
+    ]
+    for copy in copies:
+        copy.start()
+    gain_copy.start()
+    gain_copy.wait()
     gain = gain_ref[...].astype(F32)
-    for at in range(0, x_ref.shape[0], step):
+    for at, copy in zip(range(0, rows, step), copies):
+        copy.wait()
         x = x_ref[at : at + step, :].astype(F32)
         x = x * lax.rsqrt(jnp.mean(x * x, axis=1, keepdims=True) + 1e-06)
         y = [x[:, i * HD : (i + 1) * HD] * gain[i : i + 1, :] for i in range(gain.shape[0])]
@@ -88,13 +99,20 @@
 
 def normalise(hidden, gain):
     rows, wide = hidden.shape
+    hbm = pl.BlockSpec(memory_space=ANY)
     return pl.pallas_call(
         norm_kernel,
-        out_shape=tuple(VMEM((n, wide), BF) for n in (rows, *PART)),
+        out_shape=(VMEM((rows, wide), BF), VMEM((PART[0], wide), BF), pltpu.HBM((PART[1], wide), BF)),
+        in_specs=[hbm, hbm],
+        scratch_shapes=[
+            VMEM((rows, wide), BF),
+            VMEM((wide // HD, HD), BF),
+            pltpu.SemaphoreType.DMA((1 + rows // 16,)),
+        ],
         name="norm",
         cost_estimate=pl.CostEstimate(flops=rows * wide, bytes_accessed=rows, transcendentals=rows),
         compiler_params=pltpu.CompilerParams(vmem_limit_bytes=16 * MIB),
-    )(hidden, gain.reshape(wide // HD, HD))
+    )(in_hbm(hidden), in_hbm(gain.reshape(wide // HD, HD)))
 
 
 PART = (32, 32)
@@ -258,31 +276,68 @@
     )(*sources, wk, wv, *rest)
 
 
-def place_kernel(units, lengths, owner, *refs):
+def place_kernel(units, own, lengths, owner, *refs):
     count = max(unit[3] for unit in units) + 1
     sources = refs[:count]
-    key_out, value_out, rows = refs[count:]
+    key_out, value_out, rows, cache, held, sem, out_sem = refs[count:]
     width = key_out.shape[1]
     group = lax.axis_index("group")
     chip = lax.axis_index("head") // 2
+    copies = []
+
+    def target(d, step, at, n):
+        to = pl.multiple_of((group ^ d) * 512 + (chip ^ step) * 128 + at, 16)
+        return rows.at[pl.ds(to, n)]
+
     for d, step, at, a, row, n in units:
-        whose = d[0] if isinstance(d, tuple) else group ^ d
-        to = pl.multiple_of(whose * 512 + (chip ^ step) * 128 + at, 16)
-        rows[pl.ds(to, n), :] = sources[a][row : row + n, :]
-    key_out[...] = jnp.zeros_like(key_out)
-    value_out[...] = jnp.zeros_like(value_out)
+        if a in own:
+            copies.append(
+                pltpu.make_async_copy(sources[a].at[pl.ds(row, n)], target(d, step, at, n), sem.at[len(copies)])
+            )
+            copies[-1].start()
+    for d, step, at, a, row, n in units:
+        if a not in own:
+            target(d, step, at, n)[...] = sources[a][row : row + n, :]
+
+    def request(q, carry):
+        start, local, mine = carry
+        length = lengths[q]
+        hit = owner[q] == group
+
+        @pl.when(hit)
+        def _():
+            held[0, mine] = start
+            held[1, mine] = local
+            held[2, mine] = length
+
+        return (start + length, local + jnp.where(hit, length, 0), mine + jnp.where(hit, 1, 0))
+
+    zero = jnp.int32(0)
+    _, _, requests = lax.fori_loop(0, lengths.shape[0], request, (zero, zero, zero))
+    for copy in copies:
+        copy.wait()
     tile, window = 128, 256
     total = rows.shape[0]
-
-    def request(q, carry):
-        start, local = carry
-        length = lengths[q]
-        mine = owner[q] == group
-
-        @pl.when(mine)
-        def _():
-            def step(t, c):
-                top = pl.multiple_of(t * tile, tile)
+    tiles = cache.shape[0] // tile
+
+    def writes(t):
+        top = pl.multiple_of(t * tile, tile)
+        return [
+            pltpu.make_async_copy(
+                cache.at[pl.ds(top, tile), pl.ds(part * width, width)], out.at[pl.ds(top, tile)], out_sem.at[t, part]
+            )
+            for part, out in enumerate((key_out, value_out))
+        ]
+
+    def fill(t, carry):
+        top = pl.multiple_of(t * tile, tile)
+        cache[pl.ds(top, tile), :] = jnp.zeros((tile, cache.shape[1]), BF)
+
+        def add(q, c):
+            start, local, length = held[0, q], held[1, q], held[2, q]
+
+            @pl.when((local < top + tile) & (local + length > top))
+            def _():
                 base = start + top - local
                 at = pl.multiple_of(jnp.clip((base >> 7) << 7, 0, total - window), 128)
                 lane = lax.broadcasted_iota(jnp.int32, (tile, window), 1)
@@ -293,31 +348,48 @@
                 dst = base + lax.broadcasted_iota(jnp.int32, (tile, window), 0)
                 hit = (src == dst) & (src >= start) & (src < start + length)
                 pick = jnp.where(hit, 1.0, 0.0).astype(BF)
-                for part, out in ((0, key_out), (1, value_out)):
-                    moved = jnp.dot(pick, rows[pl.ds(at, window), part * width : (part + 1) * width], preferred_element_type=F32)
-                    out[pl.ds(top, tile), :] += moved.astype(BF)
-                return c
-
-            lax.fori_loop(local // tile, (local + length - 1) // tile + 1, step, 0)
-
-        return (start + length, local + jnp.where(mine, length, 0))
-
-    lax.fori_loop(0, lengths.shape[0], request, (jnp.int32(0), jnp.int32(0)))
-
-
-def place(units, arrays, lengths, owner, cap, width, total):
+                for i in range(2):
+                    cols = slice(i * width, (i + 1) * width)
+                    moved = jnp.dot(pick, rows[pl.ds(at, window), cols], preferred_element_type=F32)
+                    cache[pl.ds(top, tile), cols] += moved.astype(BF)
+
+            return c
+
+        lax.fori_loop(0, requests, add, 0)
+        for write in writes(t):
+            write.start()
+        return carry
+
+    lax.fori_loop(0, tiles, fill, 0)
+
+    def finish(t, carry):
+        for write in writes(t):
+            write.wait()
+        return carry
+
+    lax.fori_loop(0, tiles, finish, 0)
+
+
+def place(units, own, arrays, lengths, owner, cap, width, total):
     out = jax.ShapeDtypeStruct((cap, width), BF)
     smem = pl.BlockSpec(memory_space=pltpu.SMEM)
     full = pl.BlockSpec(memory_space=VMEM)
+    hbm = pl.BlockSpec(memory_space=ANY)
     return pl.pallas_call(
-        functools.partial(place_kernel, units),
+        functools.partial(place_kernel, units, own),
         out_shape=(out, out),
-        in_specs=[smem, smem] + [full] * len(arrays),
-        out_specs=(full, full),
-        scratch_shapes=[VMEM((total, 2 * width), BF)],
+        in_specs=[smem, smem] + [hbm if i in own else full for i in range(len(arrays))],
+        out_specs=(hbm, hbm),
+        scratch_shapes=[
+            VMEM((total, 2 * width), BF),
+            VMEM((cap, 2 * width), BF),
+            pltpu.SMEM((3, lengths.shape[0]), jnp.int32),
+            pltpu.SemaphoreType.DMA((sum(unit[3] in own for unit in units),)),
+            pltpu.SemaphoreType.DMA((cap // 128, 2)),
+        ],
         name="place",
         cost_estimate=pl.CostEstimate(flops=0, bytes_accessed=20 * MIB, transcendentals=0),
-        compiler_params=pltpu.CompilerParams(vmem_limit_bytes=28 * MIB),
+        compiler_params=pltpu.CompilerParams(vmem_limit_bytes=24 * MIB),
     )(lengths, owner, *arrays)
 
 
@@ -386,13 +458,18 @@
     x3, y3 = [across(p, 1) for p in p3], [across(p, 2) for p in p3]
     d3 = [across(x3[0], 2), across(y3[1], 1)]
 
-    units, arrays = [], []
-
-    def arrived(pieces, split, got):
+    units, arrays, mine = [], [], set()
+
+    def arrived(pieces, split, got, early=False):
         total = sum(2 * PART[part] for _, part in pieces)
         each = total // split
         for d, parts in enumerate(got):
             row = 0
+            if d == 0:
+                mine.update(range(len(arrays), len(arrays) + split))
+            if early and d in (1, 2):
+                mine.add(len(arrays) + split - 1)
+                parts = [*parts[:-1], in_hbm(parts[-1])]
             for step, part in pieces:
                 done = 0
                 while done < 2 * PART[part]:
@@ -405,9 +482,9 @@
 
     arrived(WHOLE, 1, [[one] for one in (p0, x0, y0, d0)])
     arrived(pieces1, 1, [[one] for one in (p1, x1, y1, d1)])
-    arrived(pieces2, 2, (p2, x2, y2, d2))
+    arrived(pieces2, 2, (p2, x2, y2, d2), True)
     arrived(pieces3, 2, (p3, x3, y3, d3))
-    return place(units, arrays, lengths, owner, 1024, width, 2048)
+    return place(units, sorted(mine), arrays, lengths, owner, 1024, width, 2048)
 
 
 def solution(mesh):

time: 131 us -> 127 us (0.969)
  local copies, waits for them, and re-layouts: 6.37 us -> 1.75 us
    unnamed x30 -> x20, local copies, waits for them, and re-layouts: 4.67 us -> 0.05 us
  transfers between devices with their start and end apart: 31 -> 31, of which waited for: 18 -> 18; matrix products, arithmetic and copies ran while one was open for 3% -> 3% of each run, Pallas kernels for 22% -> 23%
where the time goes in v4:
time: 127 us; the launch traced here: 126 us
  waiting for transfers between devices  50.7 us (40%)
  Pallas kernels  37.6 us (30%)
  starting transfers between devices  33.3 us (26%)
  other arithmetic  2.11 us (2%)
  local copies, waits for them, and re-layouts  1.75 us (1%)
    ppermute x18, waiting for transfers between devices, across(): return lax.ppermute(x, 'group', [(i, i ^ bit) for i in range(4)])  30.5 us
    pallas_call x4, Pallas kernels, wave(): pl.pallas_call(functools.partial(wave_kernel, pieces, kind, mode, len(sou...  29.2 us
    ppermute x18, starting transfers between devices, across(): return lax.ppermute(x, 'group', [(i, i ^ bit) for i in range(4)])  21.8 us
    ppermute x6, waiting for transfers between devices, line(): lax.ppermute(x, 'head', [(2 * a + c, 2 * b + c) for a, b in pairs for c i...  18 us
    ppermute x6, starting transfers between devices, line(): lax.ppermute(x, 'head', [(2 * a + c, 2 * b + c) for a, b in pairs for c i...  9.47 us
    pallas_call x1, Pallas kernels, place(): pl.pallas_call(functools.partial(place_kernel, units, own), out_shape=(ou...  5.5 us
    pallas_call x1, Pallas kernels, normalise(): pl.pallas_call(norm_kernel, out_shape=(VMEM((rows, wide), BF), VMEM((PART...  2.89 us
  transfers between devices with their start and end apart: 31, of which 18 were waited for; matrix products, arithmetic and copies ran while one was open for 3% of the time, Pallas kernels for 23%

profile of v4, /device:TPU:0, one launch (start us, length us, event | category | flops | bytes accessed | tf_op | source)
XLA Modules:
  0.0 126.5 jit_solution(16050855116051720455)
XLA Ops:
  0.6 2.9 %norm.1 = (bf16[64,8192]{1,0:T(8,128)(2,1)S(1)}, bf16[32,8192]{1,0:T(8,128)(2,1)}, bf16[32,8192]{1,0:T(8,128)(2,1)}) custom-call(bf16[64,8192]{1,0:T(8,128)(2,1)} %x_hbm.1, bf16[64,128]{1,0:T(8,128)(2,1)} %bitcast.5), custom_call_target="tpu_custom_call" | custom-call | flops 524288 | bytes 64 | tf_op jit(solution)/shard_map/norm/pallas_call | solution.py:103
  3.5 0.5 collective-permute-start.2
  4.0 2.6 %collective-permute-start.1 = (bf16[32,8192]{1,0:T(8,128)(2,1)}, bf16[32,8192]{1,0:T(8,128)(2,1)S(1)}, u32[]{:S(2)}, u32[]{:S(2)}) collective-permute-start(bf16[32,8192]{1,0:T(8,128)(2,1)} %get-tuple-element.39), channel_id=1, source_target_pairs={{0,2},{1,3},{2,0},{3,1},{4,6},{5,7},{6,4},{7,5},{8,10},{9,11},{10,... | collective-permute-start | bytes 1572872 | tf_op jit(solution)/shard_map/ppermute | solution.py:401
  6.7 2.6 %collective-permute-start = (bf16[32,8192]{1,0:T(8,128)(2,1)}, bf16[32,8192]{1,0:T(8,128)(2,1)S(1)}, u32[]{:S(2)}, u32[]{:S(2)}) collective-permute-start(bf16[32,8192]{1,0:T(8,128)(2,1)} %get-tuple-element.39), channel_id=1, source_target_pairs={{0,4},{1,5},{2,6},{3,7},{4,0},{5,1},{6,2},{7,3},{8,12},{9,13},{10,... | collective-permute-start | bytes 1572872 | tf_op jit(solution)/shard_map/ppermute | solution.py:401
  9.3 0.8 dynamic-slice_convert_fusion
  10.0 0.1 reshape.31
  10.1 0.1 fusion.1
  10.2 0.7 reshape.29.refs_4_.refs_6_
  10.9 0.7 reshape.30.refs_5_.refs_7_
  11.6 0.1 reshape.32
  11.7 0.1 reshape.33
  11.8 0.1 maximum_bitcast_fusion
  11.8 1.0 fusion
  12.8 0.2 pad_maximum_fusion.1
  13.1 13.9 %wave0.1.refs_0_ = bf16[128,2048]{1,0:T(8,128)(2,1)S(1)} custom-call(bf16[64,8192]{1,0:T(8,128)(2,1)S(1)} %get-tuple-element.62.refs_0_, bf16[64,8192]{1,0:T(8,128)(2,1)S(1)} %collective-permute-done.2.refs_1_, bf16[8192,1024]{1,0:T(8,128)(2,1)} %refs_4_.5, bf16[8192,1024]{1,0:T(8,128)(2,1)} %refs_5_.5, bf16[1,1024]{1,0:T(2,128)(2,1)S(1)} %reshape.29.refs_4_.refs_6_, ...), custom_call_target="tpu_custom_call" | custom-call | flops 131072 | bytes 262144 | tf_op jit(solution)/shard_map/wave0/pallas_call | solution.py:267
  27.0 3.5 %collective-permute-done.1.refs_2_ = bf16[32,8192]{1,0:T(8,128)(2,1)S(1)} collective-permute-done((bf16[32,8192]{1,0:T(8,128)(2,1)}, bf16[32,8192]{1,0:T(8,128)(2,1)S(1)}, u32[]{:S(2)}, u32[]{:S(2)}) %collective-permute-start.1) | collective-permute-done | bytes 524320 | tf_op jit(solution)/shard_map/ppermute | solution.py:401
  30.5 2.6 %collective-permute-done.refs_0_ = bf16[32,8192]{1,0:T(8,128)(2,1)S(1)} collective-permute-done((bf16[32,8192]{1,0:T(8,128)(2,1)}, bf16[32,8192]{1,0:T(8,128)(2,1)S(1)}, u32[]{:S(2)}, u32[]{:S(2)}) %collective-permute-start) | collective-permute-done | bytes 524320 | tf_op jit(solution)/shard_map/ppermute | solution.py:401
  33.1 0.5 collective-permute-start.3
  33.6 1.5 %collective-permute-start.6 = (bf16[128,2048]{1,0:T(8,128)(2,1)S(1)}, bf16[128,2048]{1,0:T(8,128)(2,1)S(1)}, u32[]{:S(2)}, u32[]{:S(2)}) collective-permute-start(bf16[128,2048]{1,0:T(8,128)(2,1)S(1)} %wave0.1.refs_0_), channel_id=1, source_target_pairs={{0,16},{8,24},{16,0},{24,8},{1,17},{9,25},{17,1},{25,9},{2,18},{10... | collective-permute-start | bytes 1572872 | tf_op jit(solution)/shard_map/ppermute | solution.py:407
  35.1 1.5 %collective-permute-start.5 = (bf16[128,2048]{1,0:T(8,128)(2,1)S(1)}, bf16[128,2048]{1,0:T(8,128)(2,1)S(1)}, u32[]{:S(2)}, u32[]{:S(2)}) collective-permute-start(bf16[128,2048]{1,0:T(8,128)(2,1)S(1)} %wave0.1.refs_0_), channel_id=1, source_target_pairs={{0,8},{8,0},{16,24},{24,16},{1,9},{9,1},{17,25},{25,17},{2,10},{10... | collective-permute-start | bytes 1572872 | tf_op jit(solution)/shard_map/ppermute | solution.py:407
  36.6 0.4 collective-permute-start.10
  37.1 2.6 %collective-permute-start.9 = (bf16[32,8192]{1,0:T(8,128)(2,1)S(1)}, bf16[32,8192]{1,0:T(8,128)(2,1)S(1)}, u32[]{:S(2)}, u32[]{:S(2)}) collective-permute-start(bf16[32,8192]{1,0:T(8,128)(2,1)S(1)} %copy-done.5), channel_id=1, source_target_pairs={{0,4},{1,5},{2,6},{3,7},{4,0},{5,1},{6,2},{7,3},{8,12},{9,13},{10,... | collective-permute-start | bytes 1572872 | tf_op jit(solution)/shard_map/ppermute | solution.py:401
  39.7 5.2 %wave1.1.refs_4_ = bf16[128,2048]{1,0:T(8,128)(2,1)S(1)} custom-call(bf16[32,8192]{1,0:T(8,128)(2,1)S(1)} %collective-permute-done.refs_0_, bf16[32,8192]{1,0:T(8,128)(2,1)S(1)} %collective-permute-done.3.refs_1_, bf16[32,8192]{1,0:T(8,128)(2,1)S(1)} %collective-permute-done.1.refs_2_, bf16[32,8192]{1,0:T(8,128)(2,1)S(1)} %collective-permute-done.4.refs_3_, ...), custom_call_target="tpu_custom_call" | custom-call | flops 131072 | bytes 262144 | tf_op jit(solution)/shard_map/wave1/pallas_call | solution.py:267
  44.9 2.6 %collective-permute-done.6.refs_2_ = bf16[128,2048]{1,0:T(8,128)(2,1)S(1)} collective-permute-done((bf16[128,2048]{1,0:T(8,128)(2,1)S(1)}, bf16[128,2048]{1,0:T(8,128)(2,1)S(1)}, u32[]{:S(2)}, u32[]{:S(2)}) %collective-permute-start.6) | collective-permute-done | bytes 524320 | tf_op jit(solution)/shard_map/ppermute | solution.py:407
  47.4 1.2 collective-permute-done.5.refs_1_
  48.7 0.5 collective-permute-start.8
  49.2 1.5 %collective-permute-start.7 = (bf16[128,2048]{1,0:T(8,128)(2,1)S(1)}, bf16[128,2048]{1,0:T(8,128)(2,1)S(1)}, u32[]{:S(2)}, u32[]{:S(2)}) collective-permute-start(bf16[128,2048]{1,0:T(8,128)(2,1)S(1)} %wave1.1.refs_4_), channel_id=1, source_target_pairs={{0,8},{8,0},{16,24},{24,16},{1,9},{9,1},{17,25},{25,17},{2,10},{10... | collective-permute-start | bytes 1572872 | tf_op jit(solution)/shard_map/ppermute | solution.py:407
  50.7 10.2 %collective-permute-done.10.refs_2_ = bf16[32,8192]{1,0:T(8,128)(2,1)S(1)} collective-permute-done((bf16[32,8192]{1,0:T(8,128)(2,1)S(1)}, bf16[32,8192]{1,0:T(8,128)(2,1)S(1)}, u32[]{:S(2)}, u32[]{:S(2)}) %collective-permute-start.10) | collective-permute-done | bytes 524320 | tf_op jit(solution)/shard_map/ppermute | solution.py:401
  60.8 1.4 %collective-permute-done.9.refs_0_ = bf16[32,8192]{1,0:T(8,128)(2,1)S(1)} collective-permute-done((bf16[32,8192]{1,0:T(8,128)(2,1)S(1)}, bf16[32,8192]{1,0:T(8,128)(2,1)S(1)}, u32[]{:S(2)}, u32[]{:S(2)}) %collective-permute-start.9) | collective-permute-done | bytes 524320 | tf_op jit(solution)/shard_map/ppermute | solution.py:401
  62.2 0.8 collective-permute-start.11
  63.1 1.5 %collective-permute-start.12 = (bf16[128,2048]{1,0:T(8,128)(2,1)S(1)}, bf16[128,2048]{1,0:T(8,128)(2,1)S(1)}, u32[]{:S(2)}, u32[]{:S(2)}) collective-permute-start(bf16[128,2048]{1,0:T(8,128)(2,1)S(1)} %collective-permute-done.8.refs_6_), channel_id=1, source_target_pairs={{0,8},{8,0},{16,24},{24,16},{1,9},{9,1},{17,25},{25,17},{2,10},{10... | collective-permute-start | bytes 1572872 | tf_op jit(solution)/shard_map/ppermute | solution.py:407
  64.6 0.5 collective-permute-start.13
  65.1 0.1 pad_maximum_fusion
  65.2 0.5 collective-permute-start.20
  65.7 0.8 collective-permute-done.14.refs_3_
  66.5 0.7 collective-permute-start.19
  67.2 0.0 collective-permute-done.13.refs_1_
  67.2 5.0 %wave2.1 = (bf16[64,2048]{1,0:T(8,128)(2,1)S(1)}, bf16[64,2048]{1,0:T(8,128)(2,1)S(1)}) custom-call(bf16[32,8192]{1,0:T(8,128)(2,1)S(1)} %collective-permute-done.9.refs_0_, bf16[32,8192]{1,0:T(8,128)(2,1)S(1)} %collective-permute-done.13.refs_1_, bf16[32,8192]{1,0:T(8,128)(2,1)S(1)} %collective-permute-done.10.refs_2_, ...), custom_call_target="tpu_custom_call" | custom-call | flops 131072 | bytes 262144 | tf_op jit(solution)/shard_map/wave2/pallas_call | solution.py:267
  72.2 1.4 %collective-permute-done.11.refs_3_ = bf16[128,2048]{1,0:T(8,128)(2,1)S(1)} collective-permute-done((bf16[128,2048]{1,0:T(8,128)(2,1)S(1)}, bf16[128,2048]{1,0:T(8,128)(2,1)S(1)}, u32[]{:S(2)}, u32[]{:S(2)}) %collective-permute-start.11) | collective-permute-done | bytes 524320 | tf_op jit(solution)/shard_map/ppermute | solution.py:407
  73.6 1.6 %collective-permute-done.12.refs_7_ = bf16[128,2048]{1,0:T(8,128)(2,1)S(1)} collective-permute-done((bf16[128,2048]{1,0:T(8,128)(2,1)S(1)}, bf16[128,2048]{1,0:T(8,128)(2,1)S(1)}, u32[]{:S(2)}, u32[]{:S(2)}) %collective-permute-start.12) | collective-permute-done | bytes 524320 | tf_op jit(solution)/shard_map/ppermute | solution.py:407
  75.2 0.4 collective-permute-start.17
  75.6 1.7 %collective-permute-start.15 = (bf16[64,2048]{1,0:T(8,128)(2,1)S(1)}, bf16[64,2048]{1,0:T(8,128)(2,1)S(1)}, u32[]{:S(2)}, u32[]{:S(2)}) collective-permute-start(bf16[64,2048]{1,0:T(8,128)(2,1)S(1)} %get-tuple-element.60.refs_8_), channel_id=1, source_target_pairs={{0,8},{8,0},{16,24},{24,16},{1,9},{9,1},{17,25},{25,17},{2,10},{10... | collective-permute-start | bytes 786440 | tf_op jit(solution)/shard_map/ppermute | solution.py:407
  77.3 1.7 %collective-permute-start.18 = (bf16[64,2048]{1,0:T(8,128)(2,1)S(1)}, bf16[64,2048]{1,0:T(8,128)(2,1)S(1)}, u32[]{:S(2)}, u32[]{:S(2)}) collective-permute-start(bf16[64,2048]{1,0:T(8,128)(2,1)S(1)} %get-tuple-element.61.refs_9_), channel_id=1, source_target_pairs={{0,16},{8,24},{16,0},{24,8},{1,17},{9,25},{17,1},{25,9},{2,18},{10... | collective-permute-start | bytes 786440 | tf_op jit(solution)/shard_map/ppermute | solution.py:407
  79.0 4.6 %collective-permute-done.17.refs_12_ = bf16[64,2048]{1,0:T(8,128)(2,1)S(1)} collective-permute-done((bf16[64,2048]{1,0:T(8,128)(2,1)S(1)}, bf16[64,2048]{1,0:T(8,128)(2,1)S(1)}, u32[]{:S(2)}, u32[]{:S(2)}) %collective-permute-start.17) | collective-permute-done | bytes 262176 | tf_op jit(solution)/shard_map/ppermute | solution.py:407
  83.6 2.0 %collective-permute-start.16 = (bf16[64,2048]{1,0:T(8,128)(2,1)S(1)}, bf16[64,2048]{1,0:T(8,128)(2,1)S(1)}, u32[]{:S(2)}, u32[]{:S(2)}) collective-permute-start(bf16[64,2048]{1,0:T(8,128)(2,1)S(1)} %get-tuple-element.61.refs_9_), channel_id=1, source_target_pairs={{0,8},{8,0},{16,24},{24,16},{1,9},{9,1},{17,25},{25,17},{2,10},{10... | collective-permute-start | bytes 786440 | tf_op jit(solution)/shard_map/ppermute | solution.py:407
  85.6 0.8 collective-permute-done.18.refs_13_
  86.4 3.6 %collective-permute-done.16.refs_11_ = bf16[64,2048]{1,0:T(8,128)(2,1)S(1)} collective-permute-done((bf16[64,2048]{1,0:T(8,128)(2,1)S(1)}, bf16[64,2048]{1,0:T(8,128)(2,1)S(1)}, u32[]{:S(2)}, u32[]{:S(2)}) %collective-permute-start.16) | collective-permute-done | bytes 262176 | tf_op jit(solution)/shard_map/ppermute | solution.py:407
  90.0 0.3 collective-permute-done.20.refs_2_
  90.3 0.5 collective-permute-start.22
  90.8 0.6 collective-permute-start.23
  91.4 1.7 %collective-permute-start.24 = (bf16[64,2048]{1,0:T(8,128)(2,1)S(1)}, bf16[64,2048]{1,0:T(8,128)(2,1)S(1)}, u32[]{:S(2)}, u32[]{:S(2)}) collective-permute-start(bf16[64,2048]{1,0:T(8,128)(2,1)S(1)} %collective-permute-done.18.refs_13_), channel_id=1, source_target_pairs={{0,8},{8,0},{16,24},{24,16},{1,9},{9,1},{17,25},{25,17},{2,10},{10... | collective-permute-start | bytes 786440 | tf_op jit(solution)/shard_map/ppermute | solution.py:407
  93.2 1.3 %collective-permute-done.22.refs_3_ = bf16[64,8192]{1,0:T(8,128)(2,1)S(1)} collective-permute-done((bf16[64,8192]{1,0:T(8,128)(2,1)S(1)}, bf16[64,8192]{1,0:T(8,128)(2,1)S(1)}, u32[]{:S(2)}, u32[]{:S(2)}) %collective-permute-start.22) | collective-permute-done | bytes 1048608 | tf_op jit(solution)/shard_map/ppermute | solution.py:404
  94.5 5.2 %wave3.1 = (bf16[64,2048]{1,0:T(8,128)(2,1)S(1)}, bf16[64,2048]{1,0:T(8,128)(2,1)S(1)}) custom-call(bf16[64,8192]{1,0:T(8,128)(2,1)S(1)} %collective-permute-done.19.refs_0_, bf16[64,8192]{1,0:T(8,128)(2,1)S(1)} %collective-permute-done.21.refs_1_, bf16[64,8192]{1,0:T(8,128)(2,1)S(1)} %collective-permute-done.20.refs_2_, ...), custom_call_target="tpu_custom_call" | custom-call | flops 131072 | bytes 262144 | tf_op jit(solution)/shard_map/wave3/pallas_call | solution.py:267
  99.7 1.8 %collective-permute-start.25 = (bf16[64,2048]{1,0:T(8,128)(2,1)S(1)}, bf16[64,2048]{1,0:T(8,128)(2,1)S(1)}, u32[]{:S(2)}, u32[]{:S(2)}) collective-permute-start(bf16[64,2048]{1,0:T(8,128)(2,1)S(1)} %get-tuple-element.74.refs_16_), channel_id=1, source_target_pairs={{0,8},{8,0},{16,24},{24,16},{1,9},{9,1},{17,25},{25,17},{2,10},{10... | collective-permute-start | bytes 786440 | tf_op jit(solution)/shard_map/ppermute | solution.py:407
  101.5 1.1 collective-permute-start.28
  102.6 1.0 collective-permute-start.27
  103.5 0.3 collective-permute-start.26
  103.8 5.1 %collective-permute-done.25.refs_18_ = bf16[64,2048]{1,0:T(8,128)(2,1)S(1)} collective-permute-done((bf16[64,2048]{1,0:T(8,128)(2,1)S(1)}, bf16[64,2048]{1,0:T(8,128)(2,1)S(1)}, u32[]{:S(2)}, u32[]{:S(2)}) %collective-permute-start.25) | collective-permute-done | bytes 262176 | tf_op jit(solution)/shard_map/ppermute | solution.py:407
  108.9 1.1 collective-permute-start.29
  110.0 0.6 collective-permute-done.28.refs_21_
  110.7 1.1 collective-permute-start.30
  111.8 4.5 %collective-permute-done.27.refs_20_ = bf16[64,2048]{1,0:T(8,128)(2,1)S(1)} collective-permute-done((bf16[64,2048]{1,0:T(8,128)(2,1)S(1)}, bf16[64,2048]{1,0:T(8,128)(2,1)S(1)}, u32[]{:S(2)}, u32[]{:S(2)}) %collective-permute-start.27) | collective-permute-done | bytes 262176 | tf_op jit(solution)/shard_map/ppermute | solution.py:407
  116.3 4.5 %collective-permute-done.29.refs_22_ = bf16[64,2048]{1,0:T(8,128)(2,1)S(1)} collective-permute-done((bf16[64,2048]{1,0:T(8,128)(2,1)S(1)}, bf16[64,2048]{1,0:T(8,128)(2,1)S(1)}, u32[]{:S(2)}, u32[]{:S(2)}) %collective-permute-start.29) | collective-permute-done | bytes 262176 | tf_op jit(solution)/shard_map/ppermute | solution.py:407
  120.8 5.5 %place.1 = (bf16[1024,1024]{1,0:T(8,128)(2,1)}, bf16[1024,1024]{1,0:T(8,128)(2,1)}) custom-call(s32[16]{0:T(128)S(1)} %copy-done.1, s32[16]{0:T(128)S(1)} %copy-done.2, bf16[128,2048]{1,0:T(8,128)(2,1)S(1)} %wave0.1.refs_0_, bf16[128,2048]{1,0:T(8,128)(2,1)S(1)} %collective-permute-done.5.refs_1_, bf16[128,2048]{1,0:T(8,128)(2,1)S(1)} %collective-permute-done.6.refs_2_, ...), custom_call_target="tpu_custom_call" | custom-call | bytes 20971520 | tf_op jit(solution)/shard_map/place/pallas_call | solution.py:378
  (37 shorter events, 0.1 us)
Async XLA Ops:
  3.5 9.5 %collective-permute-start.2 = (bf16[64,8192]{1,0:T(8,128)(2,1)S(1)}, bf16[64,8192]{1,0:T(8,128)(2,1)S(1)}, u32[]{:S(2)}, u32[]{:S(2)}) collective-permute-start(bf16[64,8192]{1,0:T(8,128)(2,1)S(1)} %get-tuple-element.62.refs_0_), channel_id=1, source_target_pairs={{0,1},{1,0},{2,3},{3,2},{4,5},{5,4},{6,7},{7,6},{8,9},{9,8},{10,11... | collective-permute-start | bytes 3145736 | tf_op jit(solution)/shard_map/ppermute | solution.py:404
  4.0 26.5 %collective-permute-start.1 = (bf16[32,8192]{1,0:T(8,128)(2,1)}, bf16[32,8192]{1,0:T(8,128)(2,1)S(1)}, u32[]{:S(2)}, u32[]{:S(2)}) collective-permute-start(bf16[32,8192]{1,0:T(8,128)(2,1)} %get-tuple-element.39), channel_id=1, source_target_pairs={{0,2},{1,3},{2,0},{3,1},{4,6},{5,7},{6,4},{7,5},{8,10},{9,11},{10,... | collective-permute-start | bytes 1572872 | tf_op jit(solution)/shard_map/ppermute | solution.py:401
  6.7 26.4 %collective-permute-start = (bf16[32,8192]{1,0:T(8,128)(2,1)}, bf16[32,8192]{1,0:T(8,128)(2,1)S(1)}, u32[]{:S(2)}, u32[]{:S(2)}) collective-permute-start(bf16[32,8192]{1,0:T(8,128)(2,1)} %get-tuple-element.39), channel_id=1, source_target_pairs={{0,4},{1,5},{2,6},{3,7},{4,0},{5,1},{6,2},{7,3},{8,12},{9,13},{10,... | collective-permute-start | bytes 1572872 | tf_op jit(solution)/shard_map/ppermute | solution.py:401
  13.1 26.6 %slice-start = ((s8[16777216]{0:T(1024)(128)(4,1)}), s8[4194304]{0:T(1024)(128)(4,1)S(1)}, s32[]{:S(2)}) async-start(s8[16777216]{0:T(1024)(128)(4,1)} %bitcast.3), calls=%async_computation | async-start | bytes 8388608
  13.1 23.6 %copy-start.5 = (bf16[32,8192]{1,0:T(8,128)(2,1)S(1)}, bf16[32,8192]{1,0:T(8,128)(2,1)}, u32[]{:S(2)}) copy-start(bf16[32,8192]{1,0:T(8,128)(2,1)} %get-tuple-element.47) | copy-start | bytes 1572868
  13.1 26.6 %slice-start.1 = ((s8[16777216]{0:T(1024)(128)(4,1)}), s8[4194304]{0:T(1024)(128)(4,1)S(1)}, s32[]{:S(2)}) async-start(s8[16777216]{0:T(1024)(128)(4,1)} %bitcast.3), calls=%async_computation.1 | async-start | bytes 8388608
  13.1 26.6 %slice-start.2 = ((s8[16777216]{0:T(1024)(128)(4,1)}), s8[4194304]{0:T(1024)(128)(4,1)S(1)}, s32[]{:S(2)}) async-start(s8[16777216]{0:T(1024)(128)(4,1)} %bitcast.3), calls=%async_computation.2 | async-start | bytes 8388608
  13.1 26.6 %slice-start.3 = ((s8[16777216]{0:T(1024)(128)(4,1)}), s8[4194304]{0:T(1024)(128)(4,1)S(1)}, s32[]{:S(2)}) async-start(s8[16777216]{0:T(1024)(128)(4,1)} %bitcast.3), calls=%async_computation.3 | async-start | bytes 8388608
  13.1 26.6 %copy-start = (bf16[8192,1024]{1,0:T(8,128)(2,1)S(1)}, bf16[8192,1024]{1,0:T(8,128)(2,1)}, u32[]{:S(2)}) copy-start(bf16[8192,1024]{1,0:T(8,128)(2,1)} %refs_5_.5) | copy-start | bytes 50331652
  33.1 4.0 %collective-permute-start.4 = (bf16[32,8192]{1,0:T(8,128)(2,1)S(1)}, bf16[32,8192]{1,0:T(8,128)(2,1)S(1)}, u32[]{:S(2)}, u32[]{:S(2)}) collective-permute-start(bf16[32,8192]{1,0:T(8,128)(2,1)S(1)} %collective-permute-done.1.refs_2_), channel_id=1, source_target_pairs={{0,1},{1,0},{2,3},{3,2},{4,5},{5,4},{6,7},{7,6},{8,9},{9,8},{10,11... | collective-permute-start | bytes 1572872 | tf_op jit(solution)/shard_map/ppermute | solution.py:404
  33.1 6.5 %collective-permute-start.3 = (bf16[32,8192]{1,0:T(8,128)(2,1)S(1)}, bf16[32,8192]{1,0:T(8,128)(2,1)S(1)}, u32[]{:S(2)}, u32[]{:S(2)}) collective-permute-start(bf16[32,8192]{1,0:T(8,128)(2,1)S(1)} %collective-permute-done.refs_0_), channel_id=1, source_target_pairs={{0,1},{1,0},{2,3},{3,2},{4,5},{5,4},{6,7},{7,6},{8,9},{9,8},{10,11... | collective-permute-start | bytes 1572872 | tf_op jit(solution)/shard_map/ppermute | solution.py:404
  33.6 13.8 %collective-permute-start.6 = (bf16[128,2048]{1,0:T(8,128)(2,1)S(1)}, bf16[128,2048]{1,0:T(8,128)(2,1)S(1)}, u32[]{:S(2)}, u32[]{:S(2)}) collective-permute-start(bf16[128,2048]{1,0:T(8,128)(2,1)S(1)} %wave0.1.refs_0_), channel_id=1, source_target_pairs={{0,16},{8,24},{16,0},{24,8},{1,17},{9,25},{17,1},{25,9},{2,18},{10... | collective-permute-start | bytes 1572872 | tf_op jit(solution)/shard_map/ppermute | solution.py:407
  35.1 13.6 %collective-permute-start.5 = (bf16[128,2048]{1,0:T(8,128)(2,1)S(1)}, bf16[128,2048]{1,0:T(8,128)(2,1)S(1)}, u32[]{:S(2)}, u32[]{:S(2)}) collective-permute-start(bf16[128,2048]{1,0:T(8,128)(2,1)S(1)} %wave0.1.refs_0_), channel_id=1, source_target_pairs={{0,8},{8,0},{16,24},{24,16},{1,9},{9,1},{17,25},{25,17},{2,10},{10... | collective-permute-start | bytes 1572872 | tf_op jit(solution)/shard_map/ppermute | solution.py:407
  36.6 24.2 %collective-permute-start.10 = (bf16[32,8192]{1,0:T(8,128)(2,1)S(1)}, bf16[32,8192]{1,0:T(8,128)(2,1)S(1)}, u32[]{:S(2)}, u32[]{:S(2)}) collective-permute-start(bf16[32,8192]{1,0:T(8,128)(2,1)S(1)} %copy-done.5), channel_id=1, source_target_pairs={{0,2},{1,3},{2,0},{3,1},{4,6},{5,7},{6,4},{7,5},{8,10},{9,11},{10,... | collective-permute-start | bytes 1572872 | tf_op jit(solution)/shard_map/ppermute | solution.py:401
  37.1 25.2 %collective-permute-start.9 = (bf16[32,8192]{1,0:T(8,128)(2,1)S(1)}, bf16[32,8192]{1,0:T(8,128)(2,1)S(1)}, u32[]{:S(2)}, u32[]{:S(2)}) collective-permute-start(bf16[32,8192]{1,0:T(8,128)(2,1)S(1)} %copy-done.5), channel_id=1, source_target_pairs={{0,4},{1,5},{2,6},{3,7},{4,0},{5,1},{6,2},{7,3},{8,12},{9,13},{10,... | collective-permute-start | bytes 1572872 | tf_op jit(solution)/shard_map/ppermute | solution.py:401
  48.7 13.6 %collective-permute-start.8 = (bf16[128,2048]{1,0:T(8,128)(2,1)S(1)}, bf16[128,2048]{1,0:T(8,128)(2,1)S(1)}, u32[]{:S(2)}, u32[]{:S(2)}) collective-permute-start(bf16[128,2048]{1,0:T(8,128)(2,1)S(1)} %wave1.1.refs_4_), channel_id=1, source_target_pairs={{0,16},{8,24},{16,0},{24,8},{1,17},{9,25},{17,1},{25,9},{2,18},{10... | collective-permute-start | bytes 1572872 | tf_op jit(solution)/shard_map/ppermute | solution.py:407
  49.2 13.1 %collective-permute-start.7 = (bf16[128,2048]{1,0:T(8,128)(2,1)S(1)}, bf16[128,2048]{1,0:T(8,128)(2,1)S(1)}, u32[]{:S(2)}, u32[]{:S(2)}) collective-permute-start(bf16[128,2048]{1,0:T(8,128)(2,1)S(1)} %wave1.1.refs_4_), channel_id=1, source_target_pairs={{0,8},{8,0},{16,24},{24,16},{1,9},{9,1},{17,25},{25,17},{2,10},{10... | collective-permute-start | bytes 1572872 | tf_op jit(solution)/shard_map/ppermute | solution.py:407
  62.2 11.4 %collective-permute-start.11 = (bf16[128,2048]{1,0:T(8,128)(2,1)S(1)}, bf16[128,2048]{1,0:T(8,128)(2,1)S(1)}, u32[]{:S(2)}, u32[]{:S(2)}) collective-permute-start(bf16[128,2048]{1,0:T(8,128)(2,1)S(1)} %collective-permute-done.5.refs_1_), channel_id=1, source_target_pairs={{0,16},{8,24},{16,0},{24,8},{1,17},{9,25},{17,1},{25,9},{2,18},{10... | collective-permute-start | bytes 1572872 | tf_op jit(solution)/shard_map/ppermute | solution.py:407
  63.1 12.1 %collective-permute-start.12 = (bf16[128,2048]{1,0:T(8,128)(2,1)S(1)}, bf16[128,2048]{1,0:T(8,128)(2,1)S(1)}, u32[]{:S(2)}, u32[]{:S(2)}) collective-permute-start(bf16[128,2048]{1,0:T(8,128)(2,1)S(1)} %collective-permute-done.8.refs_6_), channel_id=1, source_target_pairs={{0,8},{8,0},{16,24},{24,16},{1,9},{9,1},{17,25},{25,17},{2,10},{10... | collective-permute-start | bytes 1572872 | tf_op jit(solution)/shard_map/ppermute | solution.py:407
  64.6 1.9 %collective-permute-start.14 = (bf16[32,8192]{1,0:T(8,128)(2,1)S(1)}, bf16[32,8192]{1,0:T(8,128)(2,1)S(1)}, u32[]{:S(2)}, u32[]{:S(2)}) collective-permute-start(bf16[32,8192]{1,0:T(8,128)(2,1)S(1)} %collective-permute-done.10.refs_2_), channel_id=1, source_target_pairs={{0,1},{1,0},{2,3},{3,2},{4,5},{5,4},{6,7},{7,6},{8,9},{9,8},{10,11... | collective-permute-start | bytes 1572872 | tf_op jit(solution)/shard_map/ppermute | solution.py:404
  64.6 2.7 %collective-permute-start.13 = (bf16[32,8192]{1,0:T(8,128)(2,1)S(1)}, bf16[32,8192]{1,0:T(8,128)(2,1)S(1)}, u32[]{:S(2)}, u32[]{:S(2)}) collective-permute-start(bf16[32,8192]{1,0:T(8,128)(2,1)S(1)} %collective-permute-done.9.refs_0_), channel_id=1, source_target_pairs={{0,1},{1,0},{2,3},{3,2},{4,5},{5,4},{6,7},{7,6},{8,9},{9,8},{10,11... | collective-permute-start | bytes 1572872 | tf_op jit(solution)/shard_map/ppermute | solution.py:404
  65.2 25.1 %collective-permute-start.20 = (bf16[64,8192]{1,0:T(8,128)(2,1)S(1)}, bf16[64,8192]{1,0:T(8,128)(2,1)S(1)}, u32[]{:S(2)}, u32[]{:S(2)}) collective-permute-start(bf16[64,8192]{1,0:T(8,128)(2,1)S(1)} %pad_maximum_fusion), channel_id=1, source_target_pairs={{0,2},{1,3},{2,0},{3,1},{4,6},{5,7},{6,4},{7,5},{8,10},{9,11},{10,... | collective-permute-start | bytes 3145736 | tf_op jit(solution)/shard_map/ppermute | solution.py:401
  66.5 23.8 %collective-permute-start.19 = (bf16[64,8192]{1,0:T(8,128)(2,1)S(1)}, bf16[64,8192]{1,0:T(8,128)(2,1)S(1)}, u32[]{:S(2)}, u32[]{:S(2)}) collective-permute-start(bf16[64,8192]{1,0:T(8,128)(2,1)S(1)} %get-tuple-element.62.refs_0_), channel_id=1, source_target_pairs={{2,4},{3,5},{4,2},{5,3},{10,12},{11,13},{12,10},{13,11},{18,20},{1... | collective-permute-start | bytes 3145736 | tf_op jit(solution)/shard_map/ppermute | solution.py:401
  75.2 45.6 %copy-start.1 = (s32[16]{0:T(128)S(1)}, s32[16]{0:T(128)}, u32[]{:S(2)}) copy-start(s32[16]{0:T(128)} %lengths.1) | copy-start | bytes 196
  75.2 45.6 %copy-start.2 = (s32[16]{0:T(128)S(1)}, s32[16]{0:T(128)}, u32[]{:S(2)}) copy-start(s32[16]{0:T(128)} %owner.1) | copy-start | bytes 196
  75.2 8.4 %collective-permute-start.17 = (bf16[64,2048]{1,0:T(8,128)(2,1)S(1)}, bf16[64,2048]{1,0:T(8,128)(2,1)S(1)}, u32[]{:S(2)}, u32[]{:S(2)}) collective-permute-start(bf16[64,2048]{1,0:T(8,128)(2,1)S(1)} %get-tuple-element.60.refs_8_), channel_id=1, source_target_pairs={{0,16},{8,24},{16,0},{24,8},{1,17},{9,25},{17,1},{25,9},{2,18},{10... | collective-permute-start | bytes 786440 | tf_op jit(solution)/shard_map/ppermute | solution.py:407
  75.6 10.0 %collective-permute-start.15 = (bf16[64,2048]{1,0:T(8,128)(2,1)S(1)}, bf16[64,2048]{1,0:T(8,128)(2,1)S(1)}, u32[]{:S(2)}, u32[]{:S(2)}) collective-permute-start(bf16[64,2048]{1,0:T(8,128)(2,1)S(1)} %get-tuple-element.60.refs_8_), channel_id=1, source_target_pairs={{0,8},{8,0},{16,24},{24,16},{1,9},{9,1},{17,25},{25,17},{2,10},{10... | collective-permute-start | bytes 786440 | tf_op jit(solution)/shard_map/ppermute | solution.py:407
  77.3 9.1 %collective-permute-start.18 = (bf16[64,2048]{1,0:T(8,128)(2,1)S(1)}, bf16[64,2048]{1,0:T(8,128)(2,1)S(1)}, u32[]{:S(2)}, u32[]{:S(2)}) collective-permute-start(bf16[64,2048]{1,0:T(8,128)(2,1)S(1)} %get-tuple-element.61.refs_9_), channel_id=1, source_target_pairs={{0,16},{8,24},{16,0},{24,8},{1,17},{9,25},{17,1},{25,9},{2,18},{10... | collective-permute-start | bytes 786440 | tf_op jit(solution)/shard_map/ppermute | solution.py:407
  83.6 6.4 %collective-permute-start.16 = (bf16[64,2048]{1,0:T(8,128)(2,1)S(1)}, bf16[64,2048]{1,0:T(8,128)(2,1)S(1)}, u32[]{:S(2)}, u32[]{:S(2)}) collective-permute-start(bf16[64,2048]{1,0:T(8,128)(2,1)S(1)} %get-tuple-element.61.refs_9_), channel_id=1, source_target_pairs={{0,8},{8,0},{16,24},{24,16},{1,9},{9,1},{17,25},{25,17},{2,10},{10... | collective-permute-start | bytes 786440 | tf_op jit(solution)/shard_map/ppermute | solution.py:407
  86.4 13.3 %copy-start.3 = (bf16[64,2048]{1,0:T(8,128)(2,1)}, bf16[64,2048]{1,0:T(8,128)(2,1)S(1)}, u32[]{:S(2)}) copy-start(bf16[64,2048]{1,0:T(8,128)(2,1)S(1)} %collective-permute-done.18.refs_13_) | copy-start | bytes 786436
  90.0 9.7 %copy-start.4 = (bf16[64,2048]{1,0:T(8,128)(2,1)}, bf16[64,2048]{1,0:T(8,128)(2,1)S(1)}, u32[]{:S(2)}) copy-start(bf16[64,2048]{1,0:T(8,128)(2,1)S(1)} %collective-permute-done.16.refs_11_) | copy-start | bytes 786436
  90.3 2.9 %collective-permute-start.21 = (bf16[64,8192]{1,0:T(8,128)(2,1)S(1)}, bf16[64,8192]{1,0:T(8,128)(2,1)S(1)}, u32[]{:S(2)}, u32[]{:S(2)}) collective-permute-start(bf16[64,8192]{1,0:T(8,128)(2,1)S(1)} %collective-permute-done.19.refs_0_), channel_id=1, source_target_pairs={{0,1},{1,0},{2,3},{3,2},{4,5},{5,4},{6,7},{7,6},{8,9},{9,8},{10,11... | collective-permute-start | bytes 3145736 | tf_op jit(solution)/shard_map/ppermute | solution.py:404
  90.3 4.2 %collective-permute-start.22 = (bf16[64,8192]{1,0:T(8,128)(2,1)S(1)}, bf16[64,8192]{1,0:T(8,128)(2,1)S(1)}, u32[]{:S(2)}, u32[]{:S(2)}) collective-permute-start(bf16[64,8192]{1,0:T(8,128)(2,1)S(1)} %collective-permute-done.20.refs_2_), channel_id=1, source_target_pairs={{0,1},{1,0},{2,3},{3,2},{4,5},{5,4},{6,7},{7,6},{8,9},{9,8},{10,11... | collective-permute-start | bytes 3145736 | tf_op jit(solution)/shard_map/ppermute | solution.py:404
  90.8 8.9 %collective-permute-start.23 = (bf16[64,2048]{1,0:T(8,128)(2,1)S(1)}, bf16[64,2048]{1,0:T(8,128)(2,1)S(1)}, u32[]{:S(2)}, u32[]{:S(2)}) collective-permute-start(bf16[64,2048]{1,0:T(8,128)(2,1)S(1)} %collective-permute-done.15.refs_10_), channel_id=1, source_target_pairs={{0,16},{8,24},{16,0},{24,8},{1,17},{9,25},{17,1},{25,9},{2,18},{10... | collective-permute-start | bytes 786440 | tf_op jit(solution)/shard_map/ppermute | solution.py:407
  91.4 8.3 %collective-permute-start.24 = (bf16[64,2048]{1,0:T(8,128)(2,1)S(1)}, bf16[64,2048]{1,0:T(8,128)(2,1)S(1)}, u32[]{:S(2)}, u32[]{:S(2)}) collective-permute-start(bf16[64,2048]{1,0:T(8,128)(2,1)S(1)} %collective-permute-done.18.refs_13_), channel_id=1, source_target_pairs={{0,8},{8,0},{16,24},{24,16},{1,9},{9,1},{17,25},{25,17},{2,10},{10... | collective-permute-start | bytes 786440 | tf_op jit(solution)/shard_map/ppermute | solution.py:407
  99.7 9.2 %collective-permute-start.25 = (bf16[64,2048]{1,0:T(8,128)(2,1)S(1)}, bf16[64,2048]{1,0:T(8,128)(2,1)S(1)}, u32[]{:S(2)}, u32[]{:S(2)}) collective-permute-start(bf16[64,2048]{1,0:T(8,128)(2,1)S(1)} %get-tuple-element.74.refs_16_), channel_id=1, source_target_pairs={{0,8},{8,0},{16,24},{24,16},{1,9},{9,1},{17,25},{25,17},{2,10},{10... | collective-permute-start | bytes 786440 | tf_op jit(solution)/shard_map/ppermute | solution.py:407
  101.5 9.2 %collective-permute-start.28 = (bf16[64,2048]{1,0:T(8,128)(2,1)S(1)}, bf16[64,2048]{1,0:T(8,128)(2,1)S(1)}, u32[]{:S(2)}, u32[]{:S(2)}) collective-permute-start(bf16[64,2048]{1,0:T(8,128)(2,1)S(1)} %get-tuple-element.75.refs_17_), channel_id=1, source_target_pairs={{0,16},{8,24},{16,0},{24,8},{1,17},{9,25},{17,1},{25,9},{2,18},{10... | collective-permute-start | bytes 786440 | tf_op jit(solution)/shard_map/ppermute | solution.py:407
  102.6 13.7 %collective-permute-start.27 = (bf16[64,2048]{1,0:T(8,128)(2,1)S(1)}, bf16[64,2048]{1,0:T(8,128)(2,1)S(1)}, u32[]{:S(2)}, u32[]{:S(2)}) collective-permute-start(bf16[64,2048]{1,0:T(8,128)(2,1)S(1)} %get-tuple-element.74.refs_16_), channel_id=1, source_target_pairs={{0,16},{8,24},{16,0},{24,8},{1,17},{9,25},{17,1},{25,9},{2,18},{10... | collective-permute-start | bytes 786440 | tf_op jit(solution)/shard_map/ppermute | solution.py:407
  103.5 12.8 %collective-permute-start.26 = (bf16[64,2048]{1,0:T(8,128)(2,1)S(1)}, bf16[64,2048]{1,0:T(8,128)(2,1)S(1)}, u32[]{:S(2)}, u32[]{:S(2)}) collective-permute-start(bf16[64,2048]{1,0:T(8,128)(2,1)S(1)} %get-tuple-element.75.refs_17_), channel_id=1, source_target_pairs={{0,8},{8,0},{16,24},{24,16},{1,9},{9,1},{17,25},{25,17},{2,10},{10... | collective-permute-start | bytes 786440 | tf_op jit(solution)/shard_map/ppermute | solution.py:407
  108.9 11.9 %collective-permute-start.29 = (bf16[64,2048]{1,0:T(8,128)(2,1)S(1)}, bf16[64,2048]{1,0:T(8,128)(2,1)S(1)}, u32[]{:S(2)}, u32[]{:S(2)}) collective-permute-start(bf16[64,2048]{1,0:T(8,128)(2,1)S(1)} %collective-permute-done.25.refs_18_), channel_id=1, source_target_pairs={{0,16},{8,24},{16,0},{24,8},{1,17},{9,25},{17,1},{25,9},{2,18},{10... | collective-permute-start | bytes 786440 | tf_op jit(solution)/shard_map/ppermute | solution.py:407
  110.7 10.1 %collective-permute-start.30 = (bf16[64,2048]{1,0:T(8,128)(2,1)S(1)}, bf16[64,2048]{1,0:T(8,128)(2,1)S(1)}, u32[]{:S(2)}, u32[]{:S(2)}) collective-permute-start(bf16[64,2048]{1,0:T(8,128)(2,1)S(1)} %collective-permute-done.28.refs_21_), channel_id=1, source_target_pairs={{0,8},{8,0},{16,24},{24,16},{1,9},{9,1},{17,25},{25,17},{2,10},{10... | collective-permute-start | bytes 786440 | tf_op jit(solution)/shard_map/ppermute | solution.py:407

commit v5 on v4

--- a/solution.py
+++ b/solution.py
@@ -164,15 +164,11 @@
 def wave_kernel(pieces, kind, mode, count, *refs):
     sources = refs[:count]
     wk, wv, kb, vb, cos, sin = refs[count : count + 6]
-    outs, x, sem, scratch = list(refs[count + 6 :]), None, None, []
+    outs = refs[count + 6 :]
     if mode == "use":
         x, sem = outs[-2:]
         outs = outs[:-2]
         kept = (wk, wv)
-    elif mode == "keep":
-        x, sem, wsem = outs[-3:]
-        kept = outs[-5:-3]
-        outs = outs[:-5]
     else:
         x, sem, wsem, blocks = outs[-4:]
         outs = outs[:-4]
@@ -188,7 +184,7 @@
         return kept[i // each].at[:, pl.ds(i % each * tile, tile)]
 
     copies = []
-    if mode != "use":
+    if mode == "stream":
         for i in range(total):
             cols = pl.ds(i % each * tile, tile)
             copies.append(
@@ -217,9 +213,9 @@
     else:
         rows = both(*sources) if kind == "whole" else [(sources[i], sources[i + 1], 0) for i in range(0, count, 2)]
         load(rows, sem, wait=False)
-    ahead = {"use": 0, "keep": total, "stream": DEPTH}[mode]
-    for i in range(ahead):
-        fetch(i)
+    if mode == "stream":
+        for i in range(DEPTH):
+            fetch(i)
     c, s = rotation(pieces, cos, sin)
     load(rows, sem, start=False)
     part = x.shape[0] // len(outs)
@@ -258,12 +254,9 @@
     hbm = pl.BlockSpec(memory_space=ANY)
     scratch = [VMEM((m, deep), BF), pltpu.SemaphoreType.DMA((2 * len(pieces),))]
     outs = [VMEM((m // split, 2 * width), BF)] * split
-    if mode != "use":
+    if mode == "stream":
         scratch.append(pltpu.SemaphoreType.DMA((4 * width // tile,)))
-    if mode == "stream":
         scratch.append(VMEM((DEPTH, deep, tile), BF))
-    if mode == "keep":
-        outs += [VMEM((deep, width), BF)] * 2
     return pl.pallas_call(
         functools.partial(wave_kernel, pieces, kind, mode, len(sources)),
         out_shape=outs,
@@ -465,8 +458,6 @@
         each = total // split
         for d, parts in enumerate(got):
             row = 0
-            if d == 0:
-                mine.update(range(len(arrays), len(arrays) + split))
             if early and d in (1, 2):
                 mine.add(len(arrays) + split - 1)
                 parts = [*parts[:-1], in_hbm(parts[-1])]

time: 127 us -> 128 us (level)
  Pallas kernels: 37.6 us -> 39 us
    pallas_call x1, Pallas kernels: 5.5 us -> 6.88 us  [place(): pl.pallas_call(functools.partial(place_kernel, units, own), out_shape=(ou...]
where the time goes in v5:
time: 128 us
  waiting for transfers between devices  50.7 us (40%)
  Pallas kernels  39 us (30%)
  starting transfers between devices  33.3 us (26%)
  other arithmetic  2.11 us (2%)
  local copies, waits for them, and re-layouts  1.75 us (1%)
    ppermute x18, waiting for transfers between devices, across(): return lax.ppermute(x, 'group', [(i, i ^ bit) for i in range(4)])  30.5 us
    pallas_call x4, Pallas kernels, wave(): pl.pallas_call(functools.partial(wave_kernel, pieces, kind, mode, len(sou...  29.2 us
    ppermute x18, starting transfers between devices, across(): return lax.ppermute(x, 'group', [(i, i ^ bit) for i in range(4)])  21.8 us
    ppermute x6, waiting for transfers between devices, line(): lax.ppermute(x, 'head', [(2 * a + c, 2 * b + c) for a, b in pairs for c i...  18 us
    ppermute x6, starting transfers between devices, line(): lax.ppermute(x, 'head', [(2 * a + c, 2 * b + c) for a, b in pairs for c i...  9.47 us
    pallas_call x1, Pallas kernels, place(): pl.pallas_call(functools.partial(place_kernel, units, own), out_shape=(ou...  6.88 us
    pallas_call x1, Pallas kernels, normalise(): pl.pallas_call(norm_kernel, out_shape=(VMEM((rows, wide), BF), VMEM((PART...  2.89 us
  transfers between devices with their start and end apart: 31, of which 18 were waited for; matrix products, arithmetic and copies ran while one was open for 3% of the time, Pallas kernels for 23%

profile of v5, /device:TPU:0, one launch (start us, length us, event | category | flops | bytes accessed | tf_op | source)
XLA Modules:
  0.0 127.9 jit_solution(3998659394607252248)
XLA Ops:
  0.6 2.9 %norm.1 = (bf16[64,8192]{1,0:T(8,128)(2,1)S(1)}, bf16[32,8192]{1,0:T(8,128)(2,1)}, bf16[32,8192]{1,0:T(8,128)(2,1)}) custom-call(bf16[64,8192]{1,0:T(8,128)(2,1)} %x_hbm.1, bf16[64,128]{1,0:T(8,128)(2,1)} %bitcast.5), custom_call_target="tpu_custom_call" | custom-call | flops 524288 | bytes 64 | tf_op jit(solution)/shard_map/norm/pallas_call | solution.py:103
  3.5 0.5 collective-permute-start.2
  4.0 2.6 %collective-permute-start.1 = (bf16[32,8192]{1,0:T(8,128)(2,1)}, bf16[32,8192]{1,0:T(8,128)(2,1)S(1)}, u32[]{:S(2)}, u32[]{:S(2)}) collective-permute-start(bf16[32,8192]{1,0:T(8,128)(2,1)} %get-tuple-element.39), channel_id=1, source_target_pairs={{0,2},{1,3},{2,0},{3,1},{4,6},{5,7},{6,4},{7,5},{8,10},{9,11},{10,... | collective-permute-start | bytes 1572872 | tf_op jit(solution)/shard_map/ppermute | solution.py:394
  6.7 2.6 %collective-permute-start = (bf16[32,8192]{1,0:T(8,128)(2,1)}, bf16[32,8192]{1,0:T(8,128)(2,1)S(1)}, u32[]{:S(2)}, u32[]{:S(2)}) collective-permute-start(bf16[32,8192]{1,0:T(8,128)(2,1)} %get-tuple-element.39), channel_id=1, source_target_pairs={{0,4},{1,5},{2,6},{3,7},{4,0},{5,1},{6,2},{7,3},{8,12},{9,13},{10,... | collective-permute-start | bytes 1572872 | tf_op jit(solution)/shard_map/ppermute | solution.py:394
  9.3 0.8 dynamic-slice_convert_fusion
  10.0 0.1 reshape.31
  10.1 0.1 fusion.1
  10.2 0.7 reshape.29.refs_4_.refs_6_
  10.9 0.7 reshape.30.refs_5_.refs_7_
  11.6 0.1 reshape.32
  11.7 0.1 reshape.33
  11.8 0.1 maximum_bitcast_fusion
  11.8 1.0 fusion
  12.8 0.2 pad_maximum_fusion.1
  13.1 13.9 %wave0.1.refs_0_ = bf16[128,2048]{1,0:T(8,128)(2,1)S(1)} custom-call(bf16[64,8192]{1,0:T(8,128)(2,1)S(1)} %get-tuple-element.62.refs_0_, bf16[64,8192]{1,0:T(8,128)(2,1)S(1)} %collective-permute-done.2.refs_1_, bf16[8192,1024]{1,0:T(8,128)(2,1)} %refs_4_.5, bf16[8192,1024]{1,0:T(8,128)(2,1)} %refs_5_.5, bf16[1,1024]{1,0:T(2,128)(2,1)S(1)} %reshape.29.refs_4_.refs_6_, ...), custom_call_target="tpu_custom_call" | custom-call | flops 131072 | bytes 262144 | tf_op jit(solution)/shard_map/wave0/pallas_call | solution.py:260
  27.0 3.5 %collective-permute-done.1.refs_2_ = bf16[32,8192]{1,0:T(8,128)(2,1)S(1)} collective-permute-done((bf16[32,8192]{1,0:T(8,128)(2,1)}, bf16[32,8192]{1,0:T(8,128)(2,1)S(1)}, u32[]{:S(2)}, u32[]{:S(2)}) %collective-permute-start.1) | collective-permute-done | bytes 524320 | tf_op jit(solution)/shard_map/ppermute | solution.py:394
  30.5 2.6 %collective-permute-done.refs_0_ = bf16[32,8192]{1,0:T(8,128)(2,1)S(1)} collective-permute-done((bf16[32,8192]{1,0:T(8,128)(2,1)}, bf16[32,8192]{1,0:T(8,128)(2,1)S(1)}, u32[]{:S(2)}, u32[]{:S(2)}) %collective-permute-start) | collective-permute-done | bytes 524320 | tf_op jit(solution)/shard_map/ppermute | solution.py:394
  33.1 0.5 collective-permute-start.3
  33.6 1.5 %collective-permute-start.6 = (bf16[128,2048]{1,0:T(8,128)(2,1)S(1)}, bf16[128,2048]{1,0:T(8,128)(2,1)S(1)}, u32[]{:S(2)}, u32[]{:S(2)}) collective-permute-start(bf16[128,2048]{1,0:T(8,128)(2,1)S(1)} %wave0.1.refs_0_), channel_id=1, source_target_pairs={{0,16},{8,24},{16,0},{24,8},{1,17},{9,25},{17,1},{25,9},{2,18},{10... | collective-permute-start | bytes 1572872 | tf_op jit(solution)/shard_map/ppermute | solution.py:400
  35.1 1.5 %collective-permute-start.5 = (bf16[128,2048]{1,0:T(8,128)(2,1)S(1)}, bf16[128,2048]{1,0:T(8,128)(2,1)S(1)}, u32[]{:S(2)}, u32[]{:S(2)}) collective-permute-start(bf16[128,2048]{1,0:T(8,128)(2,1)S(1)} %wave0.1.refs_0_), channel_id=1, source_target_pairs={{0,8},{8,0},{16,24},{24,16},{1,9},{9,1},{17,25},{25,17},{2,10},{10... | collective-permute-start | bytes 1572872 | tf_op jit(solution)/shard_map/ppermute | solution.py:400
  36.6 0.4 collective-permute-start.10
  37.1 2.6 %collective-permute-start.9 = (bf16[32,8192]{1,0:T(8,128)(2,1)S(1)}, bf16[32,8192]{1,0:T(8,128)(2,1)S(1)}, u32[]{:S(2)}, u32[]{:S(2)}) collective-permute-start(bf16[32,8192]{1,0:T(8,128)(2,1)S(1)} %copy-done.5), channel_id=1, source_target_pairs={{0,4},{1,5},{2,6},{3,7},{4,0},{5,1},{6,2},{7,3},{8,12},{9,13},{10,... | collective-permute-start | bytes 1572872 | tf_op jit(solution)/shard_map/ppermute | solution.py:394
  39.7 5.2 %wave1.1.refs_4_ = bf16[128,2048]{1,0:T(8,128)(2,1)S(1)} custom-call(bf16[32,8192]{1,0:T(8,128)(2,1)S(1)} %collective-permute-done.refs_0_, bf16[32,8192]{1,0:T(8,128)(2,1)S(1)} %collective-permute-done.3.refs_1_, bf16[32,8192]{1,0:T(8,128)(2,1)S(1)} %collective-permute-done.1.refs_2_, bf16[32,8192]{1,0:T(8,128)(2,1)S(1)} %collective-permute-done.4.refs_3_, ...), custom_call_target="tpu_custom_call" | custom-call | flops 131072 | bytes 262144 | tf_op jit(solution)/shard_map/wave1/pallas_call | solution.py:260
  44.9 2.6 %collective-permute-done.6.refs_2_ = bf16[128,2048]{1,0:T(8,128)(2,1)S(1)} collective-permute-done((bf16[128,2048]{1,0:T(8,128)(2,1)S(1)}, bf16[128,2048]{1,0:T(8,128)(2,1)S(1)}, u32[]{:S(2)}, u32[]{:S(2)}) %collective-permute-start.6) | collective-permute-done | bytes 524320 | tf_op jit(solution)/shard_map/ppermute | solution.py:400
  47.4 1.2 collective-permute-done.5.refs_1_
  48.7 0.5 collective-permute-start.8
  49.2 1.5 %collective-permute-start.7 = (bf16[128,2048]{1,0:T(8,128)(2,1)S(1)}, bf16[128,2048]{1,0:T(8,128)(2,1)S(1)}, u32[]{:S(2)}, u32[]{:S(2)}) collective-permute-start(bf16[128,2048]{1,0:T(8,128)(2,1)S(1)} %wave1.1.refs_4_), channel_id=1, source_target_pairs={{0,8},{8,0},{16,24},{24,16},{1,9},{9,1},{17,25},{25,17},{2,10},{10... | collective-permute-start | bytes 1572872 | tf_op jit(solution)/shard_map/ppermute | solution.py:400
  50.7 10.2 %collective-permute-done.10.refs_2_ = bf16[32,8192]{1,0:T(8,128)(2,1)S(1)} collective-permute-done((bf16[32,8192]{1,0:T(8,128)(2,1)S(1)}, bf16[32,8192]{1,0:T(8,128)(2,1)S(1)}, u32[]{:S(2)}, u32[]{:S(2)}) %collective-permute-start.10) | collective-permute-done | bytes 524320 | tf_op jit(solution)/shard_map/ppermute | solution.py:394
  60.8 1.4 %collective-permute-done.9.refs_0_ = bf16[32,8192]{1,0:T(8,128)(2,1)S(1)} collective-permute-done((bf16[32,8192]{1,0:T(8,128)(2,1)S(1)}, bf16[32,8192]{1,0:T(8,128)(2,1)S(1)}, u32[]{:S(2)}, u32[]{:S(2)}) %collective-permute-start.9) | collective-permute-done | bytes 524320 | tf_op jit(solution)/shard_map/ppermute | solution.py:394
  62.2 0.8 collective-permute-start.11
  63.1 1.5 %collective-permute-start.12 = (bf16[128,2048]{1,0:T(8,128)(2,1)S(1)}, bf16[128,2048]{1,0:T(8,128)(2,1)S(1)}, u32[]{:S(2)}, u32[]{:S(2)}) collective-permute-start(bf16[128,2048]{1,0:T(8,128)(2,1)S(1)} %collective-permute-done.8.refs_6_), channel_id=1, source_target_pairs={{0,8},{8,0},{16,24},{24,16},{1,9},{9,1},{17,25},{25,17},{2,10},{10... | collective-permute-start | bytes 1572872 | tf_op jit(solution)/shard_map/ppermute | solution.py:400
  64.6 0.5 collective-permute-start.13
  65.1 0.1 pad_maximum_fusion
  65.2 0.5 collective-permute-start.20
  65.7 0.8 collective-permute-done.14.refs_3_
  66.5 0.7 collective-permute-start.19
  67.2 0.0 collective-permute-done.13.refs_1_
  67.2 5.0 %wave2.1 = (bf16[64,2048]{1,0:T(8,128)(2,1)S(1)}, bf16[64,2048]{1,0:T(8,128)(2,1)S(1)}) custom-call(bf16[32,8192]{1,0:T(8,128)(2,1)S(1)} %collective-permute-done.9.refs_0_, bf16[32,8192]{1,0:T(8,128)(2,1)S(1)} %collective-permute-done.13.refs_1_, bf16[32,8192]{1,0:T(8,128)(2,1)S(1)} %collective-permute-done.10.refs_2_, ...), custom_call_target="tpu_custom_call" | custom-call | flops 131072 | bytes 262144 | tf_op jit(solution)/shard_map/wave2/pallas_call | solution.py:260
  72.2 1.4 %collective-permute-done.11.refs_3_ = bf16[128,2048]{1,0:T(8,128)(2,1)S(1)} collective-permute-done((bf16[128,2048]{1,0:T(8,128)(2,1)S(1)}, bf16[128,2048]{1,0:T(8,128)(2,1)S(1)}, u32[]{:S(2)}, u32[]{:S(2)}) %collective-permute-start.11) | collective-permute-done | bytes 524320 | tf_op jit(solution)/shard_map/ppermute | solution.py:400
  73.6 1.6 %collective-permute-done.12.refs_7_ = bf16[128,2048]{1,0:T(8,128)(2,1)S(1)} collective-permute-done((bf16[128,2048]{1,0:T(8,128)(2,1)S(1)}, bf16[128,2048]{1,0:T(8,128)(2,1)S(1)}, u32[]{:S(2)}, u32[]{:S(2)}) %collective-permute-start.12) | collective-permute-done | bytes 524320 | tf_op jit(solution)/shard_map/ppermute | solution.py:400
  75.2 0.4 collective-permute-start.17
  75.6 1.7 %collective-permute-start.15 = (bf16[64,2048]{1,0:T(8,128)(2,1)S(1)}, bf16[64,2048]{1,0:T(8,128)(2,1)S(1)}, u32[]{:S(2)}, u32[]{:S(2)}) collective-permute-start(bf16[64,2048]{1,0:T(8,128)(2,1)S(1)} %get-tuple-element.60.refs_8_), channel_id=1, source_target_pairs={{0,8},{8,0},{16,24},{24,16},{1,9},{9,1},{17,25},{25,17},{2,10},{10... | collective-permute-start | bytes 786440 | tf_op jit(solution)/shard_map/ppermute | solution.py:400
  77.3 1.7 %collective-permute-start.18 = (bf16[64,2048]{1,0:T(8,128)(2,1)S(1)}, bf16[64,2048]{1,0:T(8,128)(2,1)S(1)}, u32[]{:S(2)}, u32[]{:S(2)}) collective-permute-start(bf16[64,2048]{1,0:T(8,128)(2,1)S(1)} %get-tuple-element.61.refs_9_), channel_id=1, source_target_pairs={{0,16},{8,24},{16,0},{24,8},{1,17},{9,25},{17,1},{25,9},{2,18},{10... | collective-permute-start | bytes 786440 | tf_op jit(solution)/shard_map/ppermute | solution.py:400
  79.0 4.6 %collective-permute-done.17.refs_12_ = bf16[64,2048]{1,0:T(8,128)(2,1)S(1)} collective-permute-done((bf16[64,2048]{1,0:T(8,128)(2,1)S(1)}, bf16[64,2048]{1,0:T(8,128)(2,1)S(1)}, u32[]{:S(2)}, u32[]{:S(2)}) %collective-permute-start.17) | collective-permute-done | bytes 262176 | tf_op jit(solution)/shard_map/ppermute | solution.py:400
  83.6 2.0 %collective-permute-start.16 = (bf16[64,2048]{1,0:T(8,128)(2,1)S(1)}, bf16[64,2048]{1,0:T(8,128)(2,1)S(1)}, u32[]{:S(2)}, u32[]{:S(2)}) collective-permute-start(bf16[64,2048]{1,0:T(8,128)(2,1)S(1)} %get-tuple-element.61.refs_9_), channel_id=1, source_target_pairs={{0,8},{8,0},{16,24},{24,16},{1,9},{9,1},{17,25},{25,17},{2,10},{10... | collective-permute-start | bytes 786440 | tf_op jit(solution)/shard_map/ppermute | solution.py:400
  85.6 0.8 collective-permute-done.18.refs_13_
  86.4 3.6 %collective-permute-done.16.refs_11_ = bf16[64,2048]{1,0:T(8,128)(2,1)S(1)} collective-permute-done((bf16[64,2048]{1,0:T(8,128)(2,1)S(1)}, bf16[64,2048]{1,0:T(8,128)(2,1)S(1)}, u32[]{:S(2)}, u32[]{:S(2)}) %collective-permute-start.16) | collective-permute-done | bytes 262176 | tf_op jit(solution)/shard_map/ppermute | solution.py:400
  90.0 0.3 collective-permute-done.20.refs_2_
  90.3 0.5 collective-permute-start.22
  90.8 0.6 collective-permute-start.23
  91.4 1.7 %collective-permute-start.24 = (bf16[64,2048]{1,0:T(8,128)(2,1)S(1)}, bf16[64,2048]{1,0:T(8,128)(2,1)S(1)}, u32[]{:S(2)}, u32[]{:S(2)}) collective-permute-start(bf16[64,2048]{1,0:T(8,128)(2,1)S(1)} %collective-permute-done.18.refs_13_), channel_id=1, source_target_pairs={{0,8},{8,0},{16,24},{24,16},{1,9},{9,1},{17,25},{25,17},{2,10},{10... | collective-permute-start | bytes 786440 | tf_op jit(solution)/shard_map/ppermute | solution.py:400
  93.2 1.3 %collective-permute-done.22.refs_3_ = bf16[64,8192]{1,0:T(8,128)(2,1)S(1)} collective-permute-done((bf16[64,8192]{1,0:T(8,128)(2,1)S(1)}, bf16[64,8192]{1,0:T(8,128)(2,1)S(1)}, u32[]{:S(2)}, u32[]{:S(2)}) %collective-permute-start.22) | collective-permute-done | bytes 1048608 | tf_op jit(solution)/shard_map/ppermute | solution.py:397
  94.5 5.2 %wave3.1 = (bf16[64,2048]{1,0:T(8,128)(2,1)S(1)}, bf16[64,2048]{1,0:T(8,128)(2,1)S(1)}) custom-call(bf16[64,8192]{1,0:T(8,128)(2,1)S(1)} %collective-permute-done.19.refs_0_, bf16[64,8192]{1,0:T(8,128)(2,1)S(1)} %collective-permute-done.21.refs_1_, bf16[64,8192]{1,0:T(8,128)(2,1)S(1)} %collective-permute-done.20.refs_2_, ...), custom_call_target="tpu_custom_call" | custom-call | flops 131072 | bytes 262144 | tf_op jit(solution)/shard_map/wave3/pallas_call | solution.py:260
  99.7 1.8 %collective-permute-start.25 = (bf16[64,2048]{1,0:T(8,128)(2,1)S(1)}, bf16[64,2048]{1,0:T(8,128)(2,1)S(1)}, u32[]{:S(2)}, u32[]{:S(2)}) collective-permute-start(bf16[64,2048]{1,0:T(8,128)(2,1)S(1)} %get-tuple-element.74.refs_16_), channel_id=1, source_target_pairs={{0,8},{8,0},{16,24},{24,16},{1,9},{9,1},{17,25},{25,17},{2,10},{10... | collective-permute-start | bytes 786440 | tf_op jit(solution)/shard_map/ppermute | solution.py:400
  101.5 1.1 collective-permute-start.28
  102.6 1.0 collective-permute-start.27
  103.5 0.3 collective-permute-start.26
  103.8 5.1 %collective-permute-done.25.refs_18_ = bf16[64,2048]{1,0:T(8,128)(2,1)S(1)} collective-permute-done((bf16[64,2048]{1,0:T(8,128)(2,1)S(1)}, bf16[64,2048]{1,0:T(8,128)(2,1)S(1)}, u32[]{:S(2)}, u32[]{:S(2)}) %collective-permute-start.25) | collective-permute-done | bytes 262176 | tf_op jit(solution)/shard_map/ppermute | solution.py:400
  108.9 1.1 collective-permute-start.29
  110.0 0.6 collective-permute-done.28.refs_21_
  110.7 1.1 collective-permute-start.30
  111.8 4.5 %collective-permute-done.27.refs_20_ = bf16[64,2048]{1,0:T(8,128)(2,1)S(1)} collective-permute-done((bf16[64,2048]{1,0:T(8,128)(2,1)S(1)}, bf16[64,2048]{1,0:T(8,128)(2,1)S(1)}, u32[]{:S(2)}, u32[]{:S(2)}) %collective-permute-start.27) | collective-permute-done | bytes 262176 | tf_op jit(solution)/shard_map/ppermute | solution.py:400
  116.3 4.5 %collective-permute-done.29.refs_22_ = bf16[64,2048]{1,0:T(8,128)(2,1)S(1)} collective-permute-done((bf16[64,2048]{1,0:T(8,128)(2,1)S(1)}, bf16[64,2048]{1,0:T(8,128)(2,1)S(1)}, u32[]{:S(2)}, u32[]{:S(2)}) %collective-permute-start.29) | collective-permute-done | bytes 262176 | tf_op jit(solution)/shard_map/ppermute | solution.py:400
  120.8 6.9 %place.1 = (bf16[1024,1024]{1,0:T(8,128)(2,1)}, bf16[1024,1024]{1,0:T(8,128)(2,1)}) custom-call(s32[16]{0:T(128)S(1)} %copy-done.1, s32[16]{0:T(128)S(1)} %copy-done.2, bf16[128,2048]{1,0:T(8,128)(2,1)S(1)} %wave0.1.refs_0_, bf16[128,2048]{1,0:T(8,128)(2,1)S(1)} %collective-permute-done.5.refs_1_, bf16[128,2048]{1,0:T(8,128)(2,1)S(1)} %collective-permute-done.6.refs_2_, ...), custom_call_target="tpu_custom_call" | custom-call | bytes 20971520 | tf_op jit(solution)/shard_map/place/pallas_call | solution.py:371
  (37 shorter events, 0.1 us)
Async XLA Ops:
  3.5 9.5 %collective-permute-start.2 = (bf16[64,8192]{1,0:T(8,128)(2,1)S(1)}, bf16[64,8192]{1,0:T(8,128)(2,1)S(1)}, u32[]{:S(2)}, u32[]{:S(2)}) collective-permute-start(bf16[64,8192]{1,0:T(8,128)(2,1)S(1)} %get-tuple-element.62.refs_0_), channel_id=1, source_target_pairs={{0,1},{1,0},{2,3},{3,2},{4,5},{5,4},{6,7},{7,6},{8,9},{9,8},{10,11... | collective-permute-start | bytes 3145736 | tf_op jit(solution)/shard_map/ppermute | solution.py:397
  4.0 26.5 %collective-permute-start.1 = (bf16[32,8192]{1,0:T(8,128)(2,1)}, bf16[32,8192]{1,0:T(8,128)(2,1)S(1)}, u32[]{:S(2)}, u32[]{:S(2)}) collective-permute-start(bf16[32,8192]{1,0:T(8,128)(2,1)} %get-tuple-element.39), channel_id=1, source_target_pairs={{0,2},{1,3},{2,0},{3,1},{4,6},{5,7},{6,4},{7,5},{8,10},{9,11},{10,... | collective-permute-start | bytes 1572872 | tf_op jit(solution)/shard_map/ppermute | solution.py:394
  6.7 26.4 %collective-permute-start = (bf16[32,8192]{1,0:T(8,128)(2,1)}, bf16[32,8192]{1,0:T(8,128)(2,1)S(1)}, u32[]{:S(2)}, u32[]{:S(2)}) collective-permute-start(bf16[32,8192]{1,0:T(8,128)(2,1)} %get-tuple-element.39), channel_id=1, source_target_pairs={{0,4},{1,5},{2,6},{3,7},{4,0},{5,1},{6,2},{7,3},{8,12},{9,13},{10,... | collective-permute-start | bytes 1572872 | tf_op jit(solution)/shard_map/ppermute | solution.py:394
  13.1 26.6 %slice-start = ((s8[16777216]{0:T(1024)(128)(4,1)}), s8[4194304]{0:T(1024)(128)(4,1)S(1)}, s32[]{:S(2)}) async-start(s8[16777216]{0:T(1024)(128)(4,1)} %bitcast.3), calls=%async_computation | async-start | bytes 8388608
  13.1 23.6 %copy-start.5 = (bf16[32,8192]{1,0:T(8,128)(2,1)S(1)}, bf16[32,8192]{1,0:T(8,128)(2,1)}, u32[]{:S(2)}) copy-start(bf16[32,8192]{1,0:T(8,128)(2,1)} %get-tuple-element.47) | copy-start | bytes 1572868
  13.1 26.6 %slice-start.1 = ((s8[16777216]{0:T(1024)(128)(4,1)}), s8[4194304]{0:T(1024)(128)(4,1)S(1)}, s32[]{:S(2)}) async-start(s8[16777216]{0:T(1024)(128)(4,1)} %bitcast.3), calls=%async_computation.1 | async-start | bytes 8388608
  13.1 26.6 %slice-start.2 = ((s8[16777216]{0:T(1024)(128)(4,1)}), s8[4194304]{0:T(1024)(128)(4,1)S(1)}, s32[]{:S(2)}) async-start(s8[16777216]{0:T(1024)(128)(4,1)} %bitcast.3), calls=%async_computation.2 | async-start | bytes 8388608
  13.1 26.6 %slice-start.3 = ((s8[16777216]{0:T(1024)(128)(4,1)}), s8[4194304]{0:T(1024)(128)(4,1)S(1)}, s32[]{:S(2)}) async-start(s8[16777216]{0:T(1024)(128)(4,1)} %bitcast.3), calls=%async_computation.3 | async-start | bytes 8388608
  13.1 26.6 %copy-start = (bf16[8192,1024]{1,0:T(8,128)(2,1)S(1)}, bf16[8192,1024]{1,0:T(8,128)(2,1)}, u32[]{:S(2)}) copy-start(bf16[8192,1024]{1,0:T(8,128)(2,1)} %refs_5_.5) | copy-start | bytes 50331652
  33.1 4.0 %collective-permute-start.4 = (bf16[32,8192]{1,0:T(8,128)(2,1)S(1)}, bf16[32,8192]{1,0:T(8,128)(2,1)S(1)}, u32[]{:S(2)}, u32[]{:S(2)}) collective-permute-start(bf16[32,8192]{1,0:T(8,128)(2,1)S(1)} %collective-permute-done.1.refs_2_), channel_id=1, source_target_pairs={{0,1},{1,0},{2,3},{3,2},{4,5},{5,4},{6,7},{7,6},{8,9},{9,8},{10,11... | collective-permute-start | bytes 1572872 | tf_op jit(solution)/shard_map/ppermute | solution.py:397
  33.1 6.5 %collective-permute-start.3 = (bf16[32,8192]{1,0:T(8,128)(2,1)S(1)}, bf16[32,8192]{1,0:T(8,128)(2,1)S(1)}, u32[]{:S(2)}, u32[]{:S(2)}) collective-permute-start(bf16[32,8192]{1,0:T(8,128)(2,1)S(1)} %collective-permute-done.refs_0_), channel_id=1, source_target_pairs={{0,1},{1,0},{2,3},{3,2},{4,5},{5,4},{6,7},{7,6},{8,9},{9,8},{10,11... | collective-permute-start | bytes 1572872 | tf_op jit(solution)/shard_map/ppermute | solution.py:397
  33.6 13.8 %collective-permute-start.6 = (bf16[128,2048]{1,0:T(8,128)(2,1)S(1)}, bf16[128,2048]{1,0:T(8,128)(2,1)S(1)}, u32[]{:S(2)}, u32[]{:S(2)}) collective-permute-start(bf16[128,2048]{1,0:T(8,128)(2,1)S(1)} %wave0.1.refs_0_), channel_id=1, source_target_pairs={{0,16},{8,24},{16,0},{24,8},{1,17},{9,25},{17,1},{25,9},{2,18},{10... | collective-permute-start | bytes 1572872 | tf_op jit(solution)/shard_map/ppermute | solution.py:400
  35.1 13.6 %collective-permute-start.5 = (bf16[128,2048]{1,0:T(8,128)(2,1)S(1)}, bf16[128,2048]{1,0:T(8,128)(2,1)S(1)}, u32[]{:S(2)}, u32[]{:S(2)}) collective-permute-start(bf16[128,2048]{1,0:T(8,128)(2,1)S(1)} %wave0.1.refs_0_), channel_id=1, source_target_pairs={{0,8},{8,0},{16,24},{24,16},{1,9},{9,1},{17,25},{25,17},{2,10},{10... | collective-permute-start | bytes 1572872 | tf_op jit(solution)/shard_map/ppermute | solution.py:400
  36.6 24.2 %collective-permute-start.10 = (bf16[32,8192]{1,0:T(8,128)(2,1)S(1)}, bf16[32,8192]{1,0:T(8,128)(2,1)S(1)}, u32[]{:S(2)}, u32[]{:S(2)}) collective-permute-start(bf16[32,8192]{1,0:T(8,128)(2,1)S(1)} %copy-done.5), channel_id=1, source_target_pairs={{0,2},{1,3},{2,0},{3,1},{4,6},{5,7},{6,4},{7,5},{8,10},{9,11},{10,... | collective-permute-start | bytes 1572872 | tf_op jit(solution)/shard_map/ppermute | solution.py:394
  37.1 25.2 %collective-permute-start.9 = (bf16[32,8192]{1,0:T(8,128)(2,1)S(1)}, bf16[32,8192]{1,0:T(8,128)(2,1)S(1)}, u32[]{:S(2)}, u32[]{:S(2)}) collective-permute-start(bf16[32,8192]{1,0:T(8,128)(2,1)S(1)} %copy-done.5), channel_id=1, source_target_pairs={{0,4},{1,5},{2,6},{3,7},{4,0},{5,1},{6,2},{7,3},{8,12},{9,13},{10,... | collective-permute-start | bytes 1572872 | tf_op jit(solution)/shard_map/ppermute | solution.py:394
  48.7 13.6 %collective-permute-start.8 = (bf16[128,2048]{1,0:T(8,128)(2,1)S(1)}, bf16[128,2048]{1,0:T(8,128)(2,1)S(1)}, u32[]{:S(2)}, u32[]{:S(2)}) collective-permute-start(bf16[128,2048]{1,0:T(8,128)(2,1)S(1)} %wave1.1.refs_4_), channel_id=1, source_target_pairs={{0,16},{8,24},{16,0},{24,8},{1,17},{9,25},{17,1},{25,9},{2,18},{10... | collective-permute-start | bytes 1572872 | tf_op jit(solution)/shard_map/ppermute | solution.py:400
  49.2 13.1 %collective-permute-start.7 = (bf16[128,2048]{1,0:T(8,128)(2,1)S(1)}, bf16[128,2048]{1,0:T(8,128)(2,1)S(1)}, u32[]{:S(2)}, u32[]{:S(2)}) collective-permute-start(bf16[128,2048]{1,0:T(8,128)(2,1)S(1)} %wave1.1.refs_4_), channel_id=1, source_target_pairs={{0,8},{8,0},{16,24},{24,16},{1,9},{9,1},{17,25},{25,17},{2,10},{10... | collective-permute-start | bytes 1572872 | tf_op jit(solution)/shard_map/ppermute | solution.py:400
  62.2 11.4 %collective-permute-start.11 = (bf16[128,2048]{1,0:T(8,128)(2,1)S(1)}, bf16[128,2048]{1,0:T(8,128)(2,1)S(1)}, u32[]{:S(2)}, u32[]{:S(2)}) collective-permute-start(bf16[128,2048]{1,0:T(8,128)(2,1)S(1)} %collective-permute-done.5.refs_1_), channel_id=1, source_target_pairs={{0,16},{8,24},{16,0},{24,8},{1,17},{9,25},{17,1},{25,9},{2,18},{10... | collective-permute-start | bytes 1572872 | tf_op jit(solution)/shard_map/ppermute | solution.py:400
  63.1 12.1 %collective-permute-start.12 = (bf16[128,2048]{1,0:T(8,128)(2,1)S(1)}, bf16[128,2048]{1,0:T(8,128)(2,1)S(1)}, u32[]{:S(2)}, u32[]{:S(2)}) collective-permute-start(bf16[128,2048]{1,0:T(8,128)(2,1)S(1)} %collective-permute-done.8.refs_6_), channel_id=1, source_target_pairs={{0,8},{8,0},{16,24},{24,16},{1,9},{9,1},{17,25},{25,17},{2,10},{10... | collective-permute-start | bytes 1572872 | tf_op jit(solution)/shard_map/ppermute | solution.py:400
  64.6 1.9 %collective-permute-start.14 = (bf16[32,8192]{1,0:T(8,128)(2,1)S(1)}, bf16[32,8192]{1,0:T(8,128)(2,1)S(1)}, u32[]{:S(2)}, u32[]{:S(2)}) collective-permute-start(bf16[32,8192]{1,0:T(8,128)(2,1)S(1)} %collective-permute-done.10.refs_2_), channel_id=1, source_target_pairs={{0,1},{1,0},{2,3},{3,2},{4,5},{5,4},{6,7},{7,6},{8,9},{9,8},{10,11... | collective-permute-start | bytes 1572872 | tf_op jit(solution)/shard_map/ppermute | solution.py:397
  64.6 2.7 %collective-permute-start.13 = (bf16[32,8192]{1,0:T(8,128)(2,1)S(1)}, bf16[32,8192]{1,0:T(8,128)(2,1)S(1)}, u32[]{:S(2)}, u32[]{:S(2)}) collective-permute-start(bf16[32,8192]{1,0:T(8,128)(2,1)S(1)} %collective-permute-done.9.refs_0_), channel_id=1, source_target_pairs={{0,1},{1,0},{2,3},{3,2},{4,5},{5,4},{6,7},{7,6},{8,9},{9,8},{10,11... | collective-permute-start | bytes 1572872 | tf_op jit(solution)/shard_map/ppermute | solution.py:397
  65.2 25.1 %collective-permute-start.20 = (bf16[64,8192]{1,0:T(8,128)(2,1)S(1)}, bf16[64,8192]{1,0:T(8,128)(2,1)S(1)}, u32[]{:S(2)}, u32[]{:S(2)}) collective-permute-start(bf16[64,8192]{1,0:T(8,128)(2,1)S(1)} %pad_maximum_fusion), channel_id=1, source_target_pairs={{0,2},{1,3},{2,0},{3,1},{4,6},{5,7},{6,4},{7,5},{8,10},{9,11},{10,... | collective-permute-start | bytes 3145736 | tf_op jit(solution)/shard_map/ppermute | solution.py:394
  66.5 23.8 %collective-permute-start.19 = (bf16[64,8192]{1,0:T(8,128)(2,1)S(1)}, bf16[64,8192]{1,0:T(8,128)(2,1)S(1)}, u32[]{:S(2)}, u32[]{:S(2)}) collective-permute-start(bf16[64,8192]{1,0:T(8,128)(2,1)S(1)} %get-tuple-element.62.refs_0_), channel_id=1, source_target_pairs={{2,4},{3,5},{4,2},{5,3},{10,12},{11,13},{12,10},{13,11},{18,20},{1... | collective-permute-start | bytes 3145736 | tf_op jit(solution)/shard_map/ppermute | solution.py:394
  75.2 45.6 %copy-start.1 = (s32[16]{0:T(128)S(1)}, s32[16]{0:T(128)}, u32[]{:S(2)}) copy-start(s32[16]{0:T(128)} %lengths.1) | copy-start | bytes 196
  75.2 45.6 %copy-start.2 = (s32[16]{0:T(128)S(1)}, s32[16]{0:T(128)}, u32[]{:S(2)}) copy-start(s32[16]{0:T(128)} %owner.1) | copy-start | bytes 196
  75.2 8.4 %collective-permute-start.17 = (bf16[64,2048]{1,0:T(8,128)(2,1)S(1)}, bf16[64,2048]{1,0:T(8,128)(2,1)S(1)}, u32[]{:S(2)}, u32[]{:S(2)}) collective-permute-start(bf16[64,2048]{1,0:T(8,128)(2,1)S(1)} %get-tuple-element.60.refs_8_), channel_id=1, source_target_pairs={{0,16},{8,24},{16,0},{24,8},{1,17},{9,25},{17,1},{25,9},{2,18},{10... | collective-permute-start | bytes 786440 | tf_op jit(solution)/shard_map/ppermute | solution.py:400
  75.6 10.0 %collective-permute-start.15 = (bf16[64,2048]{1,0:T(8,128)(2,1)S(1)}, bf16[64,2048]{1,0:T(8,128)(2,1)S(1)}, u32[]{:S(2)}, u32[]{:S(2)}) collective-permute-start(bf16[64,2048]{1,0:T(8,128)(2,1)S(1)} %get-tuple-element.60.refs_8_), channel_id=1, source_target_pairs={{0,8},{8,0},{16,24},{24,16},{1,9},{9,1},{17,25},{25,17},{2,10},{10... | collective-permute-start | bytes 786440 | tf_op jit(solution)/shard_map/ppermute | solution.py:400
  77.3 9.1 %collective-permute-start.18 = (bf16[64,2048]{1,0:T(8,128)(2,1)S(1)}, bf16[64,2048]{1,0:T(8,128)(2,1)S(1)}, u32[]{:S(2)}, u32[]{:S(2)}) collective-permute-start(bf16[64,2048]{1,0:T(8,128)(2,1)S(1)} %get-tuple-element.61.refs_9_), channel_id=1, source_target_pairs={{0,16},{8,24},{16,0},{24,8},{1,17},{9,25},{17,1},{25,9},{2,18},{10... | collective-permute-start | bytes 786440 | tf_op jit(solution)/shard_map/ppermute | solution.py:400
  83.6 6.4 %collective-permute-start.16 = (bf16[64,2048]{1,0:T(8,128)(2,1)S(1)}, bf16[64,2048]{1,0:T(8,128)(2,1)S(1)}, u32[]{:S(2)}, u32[]{:S(2)}) collective-permute-start(bf16[64,2048]{1,0:T(8,128)(2,1)S(1)} %get-tuple-element.61.refs_9_), channel_id=1, source_target_pairs={{0,8},{8,0},{16,24},{24,16},{1,9},{9,1},{17,25},{25,17},{2,10},{10... | collective-permute-start | bytes 786440 | tf_op jit(solution)/shard_map/ppermute | solution.py:400
  86.4 13.3 %copy-start.3 = (bf16[64,2048]{1,0:T(8,128)(2,1)}, bf16[64,2048]{1,0:T(8,128)(2,1)S(1)}, u32[]{:S(2)}) copy-start(bf16[64,2048]{1,0:T(8,128)(2,1)S(1)} %collective-permute-done.18.refs_13_) | copy-start | bytes 786436
  90.0 9.7 %copy-start.4 = (bf16[64,2048]{1,0:T(8,128)(2,1)}, bf16[64,2048]{1,0:T(8,128)(2,1)S(1)}, u32[]{:S(2)}) copy-start(bf16[64,2048]{1,0:T(8,128)(2,1)S(1)} %collective-permute-done.16.refs_11_) | copy-start | bytes 786436
  90.3 2.9 %collective-permute-start.21 = (bf16[64,8192]{1,0:T(8,128)(2,1)S(1)}, bf16[64,8192]{1,0:T(8,128)(2,1)S(1)}, u32[]{:S(2)}, u32[]{:S(2)}) collective-permute-start(bf16[64,8192]{1,0:T(8,128)(2,1)S(1)} %collective-permute-done.19.refs_0_), channel_id=1, source_target_pairs={{0,1},{1,0},{2,3},{3,2},{4,5},{5,4},{6,7},{7,6},{8,9},{9,8},{10,11... | collective-permute-start | bytes 3145736 | tf_op jit(solution)/shard_map/ppermute | solution.py:397
  90.3 4.2 %collective-permute-start.22 = (bf16[64,8192]{1,0:T(8,128)(2,1)S(1)}, bf16[64,8192]{1,0:T(8,128)(2,1)S(1)}, u32[]{:S(2)}, u32[]{:S(2)}) collective-permute-start(bf16[64,8192]{1,0:T(8,128)(2,1)S(1)} %collective-permute-done.20.refs_2_), channel_id=1, source_target_pairs={{0,1},{1,0},{2,3},{3,2},{4,5},{5,4},{6,7},{7,6},{8,9},{9,8},{10,11... | collective-permute-start | bytes 3145736 | tf_op jit(solution)/shard_map/ppermute | solution.py:397
  90.8 8.9 %collective-permute-start.23 = (bf16[64,2048]{1,0:T(8,128)(2,1)S(1)}, bf16[64,2048]{1,0:T(8,128)(2,1)S(1)}, u32[]{:S(2)}, u32[]{:S(2)}) collective-permute-start(bf16[64,2048]{1,0:T(8,128)(2,1)S(1)} %collective-permute-done.15.refs_10_), channel_id=1, source_target_pairs={{0,16},{8,24},{16,0},{24,8},{1,17},{9,25},{17,1},{25,9},{2,18},{10... | collective-permute-start | bytes 786440 | tf_op jit(solution)/shard_map/ppermute | solution.py:400
  91.4 8.3 %collective-permute-start.24 = (bf16[64,2048]{1,0:T(8,128)(2,1)S(1)}, bf16[64,2048]{1,0:T(8,128)(2,1)S(1)}, u32[]{:S(2)}, u32[]{:S(2)}) collective-permute-start(bf16[64,2048]{1,0:T(8,128)(2,1)S(1)} %collective-permute-done.18.refs_13_), channel_id=1, source_target_pairs={{0,8},{8,0},{16,24},{24,16},{1,9},{9,1},{17,25},{25,17},{2,10},{10... | collective-permute-start | bytes 786440 | tf_op jit(solution)/shard_map/ppermute | solution.py:400
  99.7 9.2 %collective-permute-start.25 = (bf16[64,2048]{1,0:T(8,128)(2,1)S(1)}, bf16[64,2048]{1,0:T(8,128)(2,1)S(1)}, u32[]{:S(2)}, u32[]{:S(2)}) collective-permute-start(bf16[64,2048]{1,0:T(8,128)(2,1)S(1)} %get-tuple-element.74.refs_16_), channel_id=1, source_target_pairs={{0,8},{8,0},{16,24},{24,16},{1,9},{9,1},{17,25},{25,17},{2,10},{10... | collective-permute-start | bytes 786440 | tf_op jit(solution)/shard_map/ppermute | solution.py:400
  101.5 9.2 %collective-permute-start.28 = (bf16[64,2048]{1,0:T(8,128)(2,1)S(1)}, bf16[64,2048]{1,0:T(8,128)(2,1)S(1)}, u32[]{:S(2)}, u32[]{:S(2)}) collective-permute-start(bf16[64,2048]{1,0:T(8,128)(2,1)S(1)} %get-tuple-element.75.refs_17_), channel_id=1, source_target_pairs={{0,16},{8,24},{16,0},{24,8},{1,17},{9,25},{17,1},{25,9},{2,18},{10... | collective-permute-start | bytes 786440 | tf_op jit(solution)/shard_map/ppermute | solution.py:400
  102.6 13.7 %collective-permute-start.27 = (bf16[64,2048]{1,0:T(8,128)(2,1)S(1)}, bf16[64,2048]{1,0:T(8,128)(2,1)S(1)}, u32[]{:S(2)}, u32[]{:S(2)}) collective-permute-start(bf16[64,2048]{1,0:T(8,128)(2,1)S(1)} %get-tuple-element.74.refs_16_), channel_id=1, source_target_pairs={{0,16},{8,24},{16,0},{24,8},{1,17},{9,25},{17,1},{25,9},{2,18},{10... | collective-permute-start | bytes 786440 | tf_op jit(solution)/shard_map/ppermute | solution.py:400
  103.5 12.8 %collective-permute-start.26 = (bf16[64,2048]{1,0:T(8,128)(2,1)S(1)}, bf16[64,2048]{1,0:T(8,128)(2,1)S(1)}, u32[]{:S(2)}, u32[]{:S(2)}) collective-permute-start(bf16[64,2048]{1,0:T(8,128)(2,1)S(1)} %get-tuple-element.75.refs_17_), channel_id=1, source_target_pairs={{0,8},{8,0},{16,24},{24,16},{1,9},{9,1},{17,25},{25,17},{2,10},{10... | collective-permute-start | bytes 786440 | tf_op jit(solution)/shard_map/ppermute | solution.py:400
  108.9 11.9 %collective-permute-start.29 = (bf16[64,2048]{1,0:T(8,128)(2,1)S(1)}, bf16[64,2048]{1,0:T(8,128)(2,1)S(1)}, u32[]{:S(2)}, u32[]{:S(2)}) collective-permute-start(bf16[64,2048]{1,0:T(8,128)(2,1)S(1)} %collective-permute-done.25.refs_18_), channel_id=1, source_target_pairs={{0,16},{8,24},{16,0},{24,8},{1,17},{9,25},{17,1},{25,9},{2,18},{10... | collective-permute-start | bytes 786440 | tf_op jit(solution)/shard_map/ppermute | solution.py:400
  110.7 10.1 %collective-permute-start.30 = (bf16[64,2048]{1,0:T(8,128)(2,1)S(1)}, bf16[64,2048]{1,0:T(8,128)(2,1)S(1)}, u32[]{:S(2)}, u32[]{:S(2)}) collective-permute-start(bf16[64,2048]{1,0:T(8,128)(2,1)S(1)} %collective-permute-done.28.refs_21_), channel_id=1, source_target_pairs={{0,8},{8,0},{16,24},{24,16},{1,9},{9,1},{17,25},{25,17},{2,10},{10... | collective-permute-start | bytes 786440 | tf_op jit(solution)/shard_map/ppermute | solution.py:400
